TPU v7x, 512 devices: a whole 4x4x16 slice. The times are simulated.
512 devices in a mesh: wide: 32 (over x, z_lo), narrow: 16 (over z_hi, y, core).
Axes of the slice: x: 4, y: 4, z: 16 (z_hi: 2, z_lo: 8; z = z_hi * 8 + z_lo), core: 2. Of those that a mesh axis runs over, the one named last changes fastest.
Arguments:
- grad: bfloat16 [4096, 4096], P('narrow', 'wide'), may hold values from -6 to 6
- moment: float32 [4096, 4096], P('narrow', 'wide'), may hold values from -4 to 4
- second: float32 [4096, 4096], P('narrow', 'wide'), may hold values from 0.05 to 2
- left_basis: bfloat16 [4096, 4096], P('wide', 'narrow'), may hold values from -0.09375 to 0.09375
- right_basis: bfloat16 [4096, 4096], P('narrow', 'wide'), may hold values from -0.09375 to 0.09375
Outputs:
- moment_new: float32 [4096, 4096], P('narrow', 'wide')
- second_new: float32 [4096, 4096], P('narrow', 'wide')
- update: bfloat16 [4096, 4096], P('narrow', 'wide')
All inputs are finite; a program needn't handle non-finite values.
Results may differ from a plain program's by a relative error of at most 0.027.
Values may be sent and summed in bfloat16 or wider, within the bound.
No kernel may reach another device: no remote copies, remote signals or barrier semaphores. Data moves between devices by JAX's collectives and lax.ppermute only.
A program may use at most 64 MiB of HBM per device.

v0:
```python
import jax
import jax.numpy as jnp
from jax import lax
from jax.sharding import PartitionSpec as P

STEP = 10


beta_first = 0.95
beta_second = 0.95
epsilon = 1e-08


def shards(grad, moment, second, left_basis, right_basis):
    moment_new = beta_first * moment + (1.0 - beta_first) * grad.astype(jnp.float32)
    moment_low = moment_new.astype(jnp.bfloat16)
    right_cols = lax.all_gather(right_basis, "narrow", axis=0, tiled=True)
    pieces = (
        lax.all_gather(grad, "wide", axis=1, tiled=True),
        lax.all_gather(moment_low, "wide", axis=1, tiled=True),
    )
    basis_rows = right_cols
    first = jnp.dot(pieces[0], basis_rows, preferred_element_type=jnp.float32)
    other = jnp.dot(pieces[1], basis_rows, preferred_element_type=jnp.float32)
    right_grad = first
    right_moment = other
    right_grad = right_grad.astype(jnp.bfloat16)
    right_moment = right_moment.astype(jnp.bfloat16)
    left_cols = lax.all_gather(left_basis, "wide", axis=0, tiled=True)
    contract_rows = (((0,), (0,)), ((), ()))
    pieces = (
        lax.all_gather(right_grad, "narrow", axis=0, tiled=True),
        lax.all_gather(right_moment, "narrow", axis=0, tiled=True),
    )
    basis_rows = left_cols
    first = lax.dot_general(
        basis_rows, pieces[0], contract_rows, preferred_element_type=jnp.float32
    )
    other = lax.dot_general(
        basis_rows, pieces[1], contract_rows, preferred_element_type=jnp.float32
    )
    second_new = beta_second * second + (1.0 - beta_second) * first * first
    bias_first = 1.0 - beta_first**STEP
    bias_second = 1.0 - beta_second**STEP
    normed = (other / bias_first / (jnp.sqrt(second_new / bias_second) + epsilon)).astype(
        jnp.bfloat16
    )
    contract_cols = (((1,), (1,)), ((), ()))
    basis_rows = right_cols
    spectral_cols = lax.psum_scatter(
        lax.dot_general(
            basis_rows, normed, contract_cols, preferred_element_type=jnp.float32
        ).astype(jnp.bfloat16),
        "wide",
        scatter_dimension=0,
        tiled=True,
    )
    basis_rows = left_cols
    update = lax.psum_scatter(
        lax.dot_general(
            basis_rows, spectral_cols, contract_cols, preferred_element_type=jnp.float32
        ).astype(jnp.bfloat16),
        "narrow",
        scatter_dimension=0,
        tiled=True,
    )
    return (moment_new, second_new, update)


def solution(mesh):
    in_specs = (
        P("narrow", "wide"),
        P("narrow", "wide"),
        P("narrow", "wide"),
        P("wide", "narrow"),
        P("narrow", "wide"),
    )
    out_specs = (P("narrow", "wide"), P("narrow", "wide"), P("narrow", "wide"))
    return jax.shard_map(shards, mesh=mesh, in_specs=in_specs, out_specs=out_specs, check_vma=False)
```

profile of v0, /device:TPU:6, one launch (start us, length us, event | category | flops | bytes accessed | tf_op | source)
XLA Modules:
  0.0 1237.5 jit_solution(17264907382996547116)
XLA Ops:
  7.2 0.7 all-gather.9.cloned.1.call-update
  7.9 0.7 all-gather.7.cloned.1.call-update
  8.7 0.9 copy.15
  9.6 1.0 copy.14
  10.6 0.7 fusion.14
  11.4 0.5 all-gather.13.cloned.1.call-update
  12.0 81.6 %all-gather.9.cloned.1.call-done = bf16[4096,128]{1,0:T(8,128)(2,1)} async-done(((bf16[256,128]{1,0:T(8,128)(2,1)}), bf16[4096,128]{1,0:T(8,128)(2,1)}) %all-gather.9.cloned.1.call-update) | async-done | bytes 1048592 | tf_op jit(solution)/shard_map/all_gather | solution.py:17
  93.6 170.2 %all-gather.7.cloned.1.call-done = bf16[256,4096]{1,0:T(8,128)(2,1)} async-done(((bf16[256,128]{1,0:T(8,128)(2,1)}), bf16[256,4096]{1,0:T(8,128)(2,1)}) %all-gather.7.cloned.1.call-update) | async-done | bytes 2097168 | tf_op jit(solution)/shard_map/all_gather | solution.py:19
  263.8 3.2 convolution_convert_fusion.3
  267.0 214.7 %all-gather.15.cloned.1.call-done = bf16[256,4096]{0,1:T(8,128)(2,1)} async-done(((bf16[256,128]{0,1:T(8,128)(2,1)}), bf16[256,4096]{0,1:T(8,128)(2,1)}) %all-gather.15.cloned.1.call-update) | async-done | bytes 2097168 | tf_op jit(solution)/shard_map/all_gather | solution.py:20
  481.8 3.0 convolution_convert_fusion.2
  484.8 0.1 copy.16
  484.9 224.2 %all-gather.13.cloned.1.call-done = bf16[4096,256]{1,0:T(8,128)(2,1)} async-done(((bf16[128,256]{1,0:T(8,128)(2,1)}), bf16[4096,256]{1,0:T(8,128)(2,1)}) %all-gather.13.cloned.1.call-update) | async-done | bytes 2097168 | tf_op jit(solution)/shard_map/all_gather | solution.py:29
  709.1 98.0 %all-gather.11.cloned.1.call-done = bf16[4096,128]{1,0:T(8,128)(2,1)} async-done(((bf16[256,128]{1,0:T(8,128)(2,1)}), bf16[4096,128]{1,0:T(8,128)(2,1)}) %all-gather.11.cloned.1.call-update) | async-done | bytes 1048592 | tf_op jit(solution)/shard_map/all_gather | solution.py:32
  807.1 2.4 fusion.5
  809.5 69.9 %all-gather.17.cloned.1.call-done = bf16[4096,128]{1,0:T(8,128)(2,1)} async-done(((bf16[256,128]{1,0:T(8,128)(2,1)}), bf16[4096,128]{1,0:T(8,128)(2,1)}) %all-gather.17.cloned.1.call-update) | async-done | bytes 1048592 | tf_op jit(solution)/shard_map/all_gather | solution.py:33
  879.4 4.2 fusion
  883.7 4.1 copy.20
  887.8 216.8 %reduce-scatter.7.cloned.1.call-done = bf16[128,256]{1,0:T(8,128)(2,1)} async-done(((bf16[4096,256]{1,0:T(8,128)(2,1)}), bf16[128,256]{1,0:T(8,128)(2,1)}) %reduce-scatter.7.cloned.1.call-update) | async-done | bytes 65552
  1104.7 2.7 fusion.1
  1107.3 0.8 copy.17
  1108.1 0.8 copy.18
  1108.8 120.2 %reduce-scatter.5.cloned.1.call-done = bf16[256,128]{0,1:T(8,128)(2,1)} async-done(((bf16[4096,128]{0,1:T(8,128)(2,1)}), bf16[256,128]{0,1:T(8,128)(2,1)}) %reduce-scatter.5.cloned.1.call-update) | async-done | bytes 65552 | tf_op jit(solution)/shard_map/reduce_scatter | solution.py:59
  1229.0 1.6 copy.19
  (19 shorter events, 0.4 us)
Async XLA Ops:
  7.2 86.4 %all-gather.9.cloned.1.call-start = ((), (), s32[]{:S(2)}) async-start(), calls=%async_computation.3 | async-start | bytes 1114112 | tf_op jit(solution)/shard_map/all_gather | solution.py:17
  7.9 255.9 %all-gather.7.cloned.1.call-start = ((), (), s32[]{:S(2)}) async-start(), calls=%async_computation.2 | async-start | bytes 2162688 | tf_op jit(solution)/shard_map/all_gather | solution.py:19
  8.6 473.1 %all-gather.15.cloned.1.call-start = ((), (), s32[]{:S(2)}) async-start(), calls=%async_computation.6 | async-start | bytes 2162688 | tf_op jit(solution)/shard_map/all_gather | solution.py:20
  11.3 697.8 %all-gather.13.cloned.1.call-start = ((), (), s32[]{:S(2)}) async-start(), calls=%async_computation.5 | async-start | bytes 2162688 | tf_op jit(solution)/shard_map/all_gather | solution.py:29
  11.9 795.2 %all-gather.11.cloned.1.call-start = ((), (), s32[]{:S(2)}) async-start(), calls=%async_computation.4 | async-start | bytes 1114112 | tf_op jit(solution)/shard_map/all_gather | solution.py:32
  93.5 388.2 %copy-start.1 = (bf16[4096,128]{1,0:T(8,128)(2,1)S(1)}, bf16[4096,128]{1,0:T(8,128)(2,1)}, u32[]{:S(2)}) copy-start(bf16[4096,128]{1,0:T(8,128)(2,1)} %all-gather.9.cloned.1.call-done) | copy-start | bytes 3145732
  267.0 217.9 %copy-start.2 = (f32[256,128]{1,0:T(8,128)S(1)}, f32[256,128]{1,0:T(8,128)}, u32[]{:S(2)}) copy-start(f32[256,128]{1,0:T(8,128)} %param.7) | copy-start | bytes 393220
  267.0 612.4 %all-gather.17.cloned.1.call-start = ((), (), s32[]{:S(2)}) async-start(), calls=%async_computation.7 | async-start | bytes 1114112 | tf_op jit(solution)/shard_map/all_gather | solution.py:33
  484.8 619.9 %reduce-scatter.7.cloned.1.call-start = ((), (), s32[]{:S(2)}) async-start(), calls=%async_computation.9 | async-start | bytes 2162688
  709.1 170.3 %copy-start = (bf16[4096,256]{1,0:T(8,128)(2,1)S(1)}, bf16[4096,256]{1,0:T(8,128)(2,1)}, u32[]{:S(2)}) copy-start(bf16[4096,256]{1,0:T(8,128)(2,1)} %all-gather.13.cloned.1.call-done) | copy-start | bytes 6291460
  887.8 341.3 %reduce-scatter.5.cloned.1.call-start = ((), (), s32[]{:S(2)}) async-start(), calls=%async_computation.8 | async-start | bytes 1114112 | tf_op jit(solution)/shard_map/reduce_scatter | solution.py:59
Sparse Core Ops, SparseCore 0:
  11.3 82.1 all-gather.8
  95.6 168.1 all-gather.6
  266.4 215.2 all-gather.14
  483.7 225.3 all-gather.12
  712.8 94.1 all-gather.10
  810.8 68.5 all-gather.16
  887.9 216.7 reduce-scatter.6
  1110.1 118.9 reduce-scatter.4
where the time goes:
time: 1240 us
  waiting for transfers between devices  1200 us (97%)
  matrix products  15.5 us (1%)
  between operations  14.2 us (1%)
    all_gather x1, waiting for transfers between devices, shards(): left_cols = lax.all_gather(left_basis, 'wide', axis=0, tiled=True)  224 us
    unnamed x9, waiting for transfers between devices  219 us
    all_gather x1, waiting for transfers between devices, shards(): lax.all_gather(moment_low, 'wide', axis=1, tiled=True)  215 us
    all_gather x1, waiting for transfers between devices, shards(): lax.all_gather(grad, 'wide', axis=1, tiled=True)  170 us
    reduce_scatter x1, waiting for transfers between devices, shards(): lax.psum_scatter(lax.dot_general(basis_rows, spectral_cols, contract_cols...  120 us
    all_gather x1, waiting for transfers between devices, shards(): lax.all_gather(right_grad, 'narrow', axis=0, tiled=True)  98 us
    all_gather x1, waiting for transfers between devices, shards(): right_cols = lax.all_gather(right_basis, 'narrow', axis=0, tiled=True)  81.6 us
    all_gather x1, waiting for transfers between devices, shards(): lax.all_gather(right_moment, 'narrow', axis=0, tiled=True)  69.9 us
  transfers between devices with their start and end apart: 8, of which 8 were waited for; matrix products, arithmetic and copies ran while one was open for 1% of the time, Pallas kernels for 0%

commit v1 on v0

v1 whole, which is shorter than its diff:
```python
import functools
import jax
import jax.numpy as jnp
from jax import lax
from jax.experimental import pallas as pl
from jax.experimental.pallas import tpu as pltpu
from jax.sharding import Mesh, PartitionSpec as P

STEP = 10

beta_first = 0.95
beta_second = 0.95
epsilon = 1e-08

AXES = ("x", "zl", "zh", "y", "core")
SIZES = (4, 8, 2, 4, 2)
BF16 = jnp.bfloat16
F32 = jnp.float32


def swap(value, axis, offset):
    size = dict(zip(AXES, SIZES))[axis]
    return lax.ppermute(value, axis, [(i, i ^ offset) for i in range(size)])


def pick_tiles(index, source, rows, cols, grid):
    down, across = grid

    def kernel(index_ref, source_ref, out_ref):
        for t in range(down * across):
            r, c = divmod(t, across)
            out_ref[r * rows : (r + 1) * rows, c * cols : (c + 1) * cols] = source_ref[index_ref[t]]

    return pl.pallas_call(
        kernel,
        out_shape=jax.ShapeDtypeStruct((down * rows, across * cols), source.dtype),
        in_specs=[
            pl.BlockSpec(memory_space=pltpu.SMEM),
            pl.BlockSpec(memory_space=pltpu.VMEM),
        ],
        out_specs=pl.BlockSpec(memory_space=pltpu.VMEM),
        compiler_params=pltpu.CompilerParams(vmem_limit_bytes=16 * 2**20),
        cost_estimate=pl.CostEstimate(
            flops=0, bytes_accessed=4 * down * rows * across * cols, transcendentals=0
        ),
    )(index, source)


def gather_line(value, axis):
    for offset in (4, 2, 1):
        value = jnp.concatenate([value, swap(value, "zl", offset)], axis=axis)
    return value


def shards(grad, moment, second, left_basis, right_basis):
    rows, cols = grad.shape
    x = lax.axis_index("x")
    zl = lax.axis_index("zl")
    zh = lax.axis_index("zh")
    y = lax.axis_index("y")
    core = lax.axis_index("core")
    y1, y0 = y // 2, y % 2
    x1, x0 = x // 2, x % 2

    moment_new = beta_first * moment + (1.0 - beta_first) * grad.astype(F32)
    both = jnp.concatenate([grad, moment_new.astype(BF16)], axis=0)

    tiles = jnp.stack([right_basis, swap(right_basis, "zh", 1)], axis=0)
    tiles = jnp.stack([tiles] + [swap(tiles, "y", k) for k in (1, 2, 3)], axis=0)
    tiles = tiles.reshape(2, 2, 2, rows, cols)
    parts = []
    for ox in range(4):
        want_zh = (x1 ^ (ox // 2)) ^ zh
        want_y1 = (x0 ^ (ox % 2)) ^ y1
        part = lax.dynamic_slice(
            tiles, (want_y1, 0, want_zh, 0, 0), (1, 2, 1, rows, cols)
        ).reshape(2, rows, cols)
        parts.append(part if ox == 0 else swap(part, "x", ox))
    parts = jnp.stack(parts, axis=0)
    parts = jnp.stack([parts, swap(parts, "core", 1)], axis=0)
    source = parts.reshape(32, rows // 2, cols)
    index = []
    for p in range(8):
        o = ((p & 1) << 2) | (p & 2) | (p >> 2)
        want = zl ^ o
        for ox in range(4):
            oc = ((want >> 1) & 1) ^ core
            oy0 = (want >> 2) ^ y0
            index.append(((oc * 4 + ox) * 2 + oy0) * 2 + (want & 1))
    right = pick_tiles(jnp.stack(index).astype(jnp.int32), source, rows // 2, cols, (8, 4))

    left = gather_line(left_basis, 0)
    left = jnp.concatenate([left] + [swap(left, "x", k) for k in (1, 2, 3)], axis=0)
    index = []
    for oc in range(2):
        for oy in range(4):
            for ozh in range(2):
                for half in range(2):
                    block = ((zh ^ ozh) * 8 + (y ^ oy) * 2 + (core ^ oc)) * 2 + half
                    o = (block % 8) ^ zl
                    p = ((o & 1) << 2) | (o & 2) | (o >> 2)
                    index.append(((block // 8) ^ x) * 8 + p)
    left_rows, left_width = left_basis.shape
    left = pick_tiles(
        jnp.stack(index).astype(jnp.int32),
        left.reshape(32, left_rows, left_width),
        left_rows,
        left_width,
        (32, 1),
    )

    both = gather_line(both, 1)
    partial = jnp.dot(both, right, preferred_element_type=F32)
    total = partial[:, :cols]
    for k in (1, 2, 3):
        piece = partial[:, k * cols : (k + 1) * cols].astype(BF16)
        total = total + swap(piece, "x", k).astype(F32)
    total = total.astype(BF16)
    rotated = jnp.concatenate([total[:rows], total[rows:]], axis=1)

    rotated = jnp.concatenate([rotated, swap(rotated, "zh", 1)], axis=0)
    rotated = jnp.concatenate([rotated] + [swap(rotated, "y", k) for k in (1, 2, 3)], axis=0)
    rotated = jnp.concatenate([rotated, swap(rotated, "core", 1)], axis=0)
    rot = lax.dot_general(
        left, rotated, (((0,), (0,)), ((), ())), preferred_element_type=F32
    )
    first, other = rot[:, :cols], rot[:, cols:]
    second_new = beta_second * second + (1.0 - beta_second) * first * first
    bias_first = 1.0 - beta_first**STEP
    bias_second = 1.0 - beta_second**STEP
    normed = (other / bias_first / (jnp.sqrt(second_new / bias_second) + epsilon)).astype(BF16)

    normed = jnp.concatenate([normed] + [swap(normed, "x", k) for k in (1, 2, 3)], axis=1)
    spectral = lax.dot_general(
        normed, right, (((1,), (1,)), ((), ())), preferred_element_type=F32
    )
    for offset in (1, 2, 4):
        half = spectral.shape[1] // 2
        sent = swap(spectral[:, half:].astype(BF16), "zl", offset)
        spectral = spectral[:, :half] + sent.astype(F32)
    spectral = spectral.astype(BF16)

    update = jnp.dot(left, spectral, preferred_element_type=F32)
    half = update.shape[0] // 2
    update = update[:half] + swap(update[half:].astype(BF16), "core", 1).astype(F32)
    quarter = half // 4
    total = update[:quarter]
    for k in (1, 2, 3):
        piece = update[k * quarter : (k + 1) * quarter].astype(BF16)
        total = total + swap(piece, "y", k).astype(F32)
    update = total[:rows] + swap(total[rows:].astype(BF16), "zh", 1).astype(F32)
    return (moment_new, second_new, update.astype(BF16))


def solution(mesh):
    fine = Mesh(mesh.devices.reshape(SIZES), AXES)
    spec = P(("zh", "y", "core"), ("x", "zl"))
    left_spec = P(("x", "zl"), ("zh", "y", "core"))
    return jax.shard_map(
        shards,
        mesh=fine,
        in_specs=(spec, spec, spec, left_spec, spec),
        out_specs=(spec, spec, spec),
        check_vma=False,
    )
```

time: 1240 us -> 264 us (0.21)
  waiting for transfers between devices: 1200 us -> 80 us
  starting transfers between devices: 0.32 us -> 152 us
    all_gather x6 -> x0, waiting for transfers between devices: 859 us -> none  [the longest x1 224 us: shards(): left_cols = lax.all_gather(left_basis, 'wide', axis=0, tiled=True)]
    unnamed x9 -> x0, waiting for transfers between devices: 219 us -> none
    ppermute x0 -> x36, starting transfers between devices: none -> 152 us  [swap(): return lax.ppermute(value, axis, [(i, i ^ offset) for i in range(size)])]
    reduce_scatter x1 -> x0, waiting for transfers between devices: 120 us -> none  [shards(): lax.psum_scatter(lax.dot_general(basis_rows, spectral_cols, contract_cols...]
    ppermute x0 -> x36, waiting for transfers between devices: none -> 80 us  [swap(): return lax.ppermute(value, axis, [(i, i ^ offset) for i in range(size)])]
  transfers between devices with their start and end apart: 8 -> 36, of which waited for: 8 -> 17; matrix products, arithmetic and copies ran while one was open for 1% -> 5% of each run, Pallas kernels for 0% -> 1%
where the time goes in v1:
time: 264 us; the launch traced here: 259 us
  starting transfers between devices  152 us (58%)
  waiting for transfers between devices  80 us (30%)
  local copies, waits for them, and re-layouts  15.2 us (6%)
  matrix products  3.73 us (1%)
  between operations  3.19 us (1%)
  other arithmetic  3.07 us (1%)
    ppermute x36, starting transfers between devices, swap(): return lax.ppermute(value, axis, [(i, i ^ offset) for i in range(size)])  152 us
    ppermute x36, waiting for transfers between devices, swap(): return lax.ppermute(value, axis, [(i, i ^ offset) for i in range(size)])  80 us
    unnamed x21, local copies, waits for them, and re-layouts  10.8 us
  transfers between devices with their start and end apart: 36, of which 17 were waited for; matrix products, arithmetic and copies ran while one was open for 5% of the time, Pallas kernels for 1%

profile of v1, /device:TPU:6, one launch (start us, length us, event | category | flops | bytes accessed | tf_op | source)
XLA Modules:
  0.0 259.0 jit_solution(12420634924452104229)
XLA Ops:
  0.6 15.7 %collective-permute-start.9 = (bf16[256,128]{1,0:T(8,128)(2,1)}, bf16[256,128]{1,0:T(8,128)(2,1)S(1)}, u32[]{:S(2)}, u32[]{:S(2)}) collective-permute-start(bf16[256,128]{1,0:T(8,128)(2,1)} %param.9), channel_id=1, source_target_pairs={{0,8},{8,0},{1,9},{9,1},{2,10},{10,2},{3,11},{11,3},{4,12},{12,4},... | collective-permute-start | bytes 196616 | tf_op jit(solution)/shard_map/ppermute | solution.py:23
  21.7 4.9 %collective-permute-start.12 = (bf16[2,256,128]{2,1,0:T(8,128)(2,1)S(1)}, bf16[2,256,128]{2,1,0:T(8,128)(2,1)S(1)}, u32[]{:S(2)}, u32[]{:S(2)}) collective-permute-start(bf16[2,256,128]{2,1,0:T(8,128)(2,1)S(1)} %get-tuple-element.42), channel_id=1, source_target_pairs={{0,6},{2,4},{4,2},{6,0},{1,7},{3,5},{5,3},{7,1},{8,14},{10,12},{12... | collective-permute-start | bytes 393224 | tf_op jit(solution)/shard_map/ppermute | solution.py:23
  31.6 6.5 %collective-permute-start.6 = (bf16[512,128]{0,1:T(8,128)(2,1)S(1)}, bf16[512,128]{0,1:T(8,128)(2,1)S(1)}, u32[]{:S(2)}, u32[]{:S(2)}) collective-permute-start(bf16[512,128]{0,1:T(8,128)(2,1)S(1)} %pad_maximum_fusion.7), channel_id=1, source_target_pairs={{0,64},{16,80},{32,96},{48,112},{64,0},{80,16},{96,32},{112,48},{1... | collective-permute-start | bytes 393224 | tf_op jit(solution)/shard_map/ppermute | solution.py:23
  40.6 4.5 %collective-permute-start.14 = (bf16[2,256,128]{2,1,0:T(8,128)(2,1)S(1)}, bf16[2,256,128]{2,1,0:T(8,128)(2,1)S(1)}, u32[]{:S(2)}, u32[]{:S(2)}) collective-permute-start(bf16[2,256,128]{2,1,0:T(8,128)(2,1)S(1)} %get-tuple-element.22), channel_id=1, source_target_pairs={{0,256},{128,384},{256,0},{384,128},{1,257},{129,385},{257,1},{385... | collective-permute-start | bytes 393224 | tf_op jit(solution)/shard_map/ppermute | solution.py:23
  48.3 5.6 %collective-permute-start.7 = (bf16[512,256]{0,1:T(8,128)(2,1)S(1)}, bf16[512,256]{0,1:T(8,128)(2,1)S(1)}, u32[]{:S(2)}, u32[]{:S(2)}) collective-permute-start(bf16[512,256]{0,1:T(8,128)(2,1)S(1)} %pad_maximum_fusion.4), channel_id=1, source_target_pairs={{0,32},{16,48},{32,0},{48,16},{64,96},{80,112},{96,64},{112,80},{1... | collective-permute-start | bytes 786440 | tf_op jit(solution)/shard_map/ppermute | solution.py:23
  55.9 5.4 %collective-permute-done.7 = bf16[512,256]{0,1:T(8,128)(2,1)S(1)} collective-permute-done((bf16[512,256]{0,1:T(8,128)(2,1)S(1)}, bf16[512,256]{0,1:T(8,128)(2,1)S(1)}, u32[]{:S(2)}, u32[]{:S(2)}) %collective-permute-start.7) | collective-permute-done | bytes 262176 | tf_op jit(solution)/shard_map/ppermute | solution.py:23
  64.9 11.4 %collective-permute-done.8 = bf16[512,512]{0,1:T(8,128)(2,1)} collective-permute-done((bf16[512,512]{0,1:T(8,128)(2,1)S(1)}, bf16[512,512]{0,1:T(8,128)(2,1)}, u32[]{:S(2)}, u32[]{:S(2)}) %collective-permute-start.8) | collective-permute-done | bytes 524320 | tf_op jit(solution)/shard_map/ppermute | solution.py:23
  80.5 4.3 %collective-permute-start.18 = (bf16[512,128]{0,1:T(8,128)(2,1)S(1)}, bf16[512,128]{0,1:T(8,128)(2,1)S(1)}, u32[]{:S(2)}, u32[]{:S(2)}) collective-permute-start(bf16[512,128]{0,1:T(8,128)(2,1)S(1)} %get-tuple-element.17), channel_id=1, source_target_pairs={{0,256},{128,384},{256,0},{384,128},{1,257},{129,385},{257,1},{385... | collective-permute-start | bytes 393224 | tf_op jit(solution)/shard_map/ppermute | solution.py:23
  88.0 6.5 %collective-permute-start = (bf16[128,256]{1,0:T(8,128)(2,1)S(1)}, bf16[128,256]{1,0:T(8,128)(2,1)S(1)}, u32[]{:S(2)}, u32[]{:S(2)}) collective-permute-start(bf16[128,256]{1,0:T(8,128)(2,1)S(1)} %copy-done.2), channel_id=1, source_target_pairs={{0,64},{16,80},{32,96},{48,112},{64,0},{80,16},{96,32},{112,48},{1... | collective-permute-start | bytes 196616 | tf_op jit(solution)/shard_map/ppermute | solution.py:23
  95.3 10.2 %collective-permute-start.20 = (bf16[256,256]{0,1:T(8,128)(2,1)S(1)}, bf16[256,256]{0,1:T(8,128)(2,1)S(1)}, u32[]{:S(2)}, u32[]{:S(2)}) collective-permute-start(bf16[256,256]{0,1:T(8,128)(2,1)S(1)} %get-tuple-element.38), channel_id=1, source_target_pairs={{0,8},{8,0},{1,9},{9,1},{2,10},{10,2},{3,11},{11,3},{4,12},{12,4},... | collective-permute-start | bytes 393224 | tf_op jit(solution)/shard_map/ppermute | solution.py:23
  108.2 8.0 %collective-permute-done.20 = bf16[256,256]{0,1:T(8,128)(2,1)S(1)} collective-permute-done((bf16[256,256]{0,1:T(8,128)(2,1)S(1)}, bf16[256,256]{0,1:T(8,128)(2,1)S(1)}, u32[]{:S(2)}, u32[]{:S(2)}) %collective-permute-start.20) | collective-permute-done | bytes 131104 | tf_op jit(solution)/shard_map/ppermute | solution.py:23
  116.2 3.9 %collective-permute-start.21 = (bf16[512,256]{0,1:T(8,128)(2,1)S(1)}, bf16[512,256]{0,1:T(8,128)(2,1)S(1)}, u32[]{:S(2)}, u32[]{:S(2)}) collective-permute-start(bf16[512,256]{0,1:T(8,128)(2,1)S(1)} %pad_maximum_fusion.5), channel_id=1, source_target_pairs={{0,2},{2,0},{4,6},{6,4},{1,3},{3,1},{5,7},{7,5},{8,10},{10,8},{12,... | collective-permute-start | bytes 786440 | tf_op jit(solution)/shard_map/ppermute | solution.py:23
  132.3 4.8 %collective-permute-done.23 = bf16[512,256]{0,1:T(8,128)(2,1)S(1)} collective-permute-done((bf16[512,256]{0,1:T(8,128)(2,1)S(1)}, bf16[512,256]{0,1:T(8,128)(2,1)S(1)}, u32[]{:S(2)}, u32[]{:S(2)}) %collective-permute-start.23) | collective-permute-done | bytes 262176 | tf_op jit(solution)/shard_map/ppermute | solution.py:23
  144.1 4.4 %collective-permute-start.4 = (bf16[1024,256]{1,0:T(8,128)(2,1)}, bf16[1024,256]{1,0:T(8,128)(2,1)}, u32[]{:S(2)}, u32[]{:S(2)}) collective-permute-start(bf16[1024,256]{1,0:T(8,128)(2,1)} %get-tuple-element.24), channel_id=1, source_target_pairs={{0,256},{128,384},{256,0},{384,128},{1,257},{129,385},{257,1},{385... | collective-permute-start | bytes 1572872 | tf_op jit(solution)/shard_map/ppermute | solution.py:23
  153.6 4.6 %collective-permute-done.3 = bf16[1024,256]{1,0:T(8,128)(2,1)} collective-permute-done((bf16[1024,256]{1,0:T(8,128)(2,1)}, bf16[1024,256]{1,0:T(8,128)(2,1)}, u32[]{:S(2)}, u32[]{:S(2)}) %collective-permute-start.3) | collective-permute-done | bytes 524320 | tf_op jit(solution)/shard_map/ppermute | solution.py:23
  159.2 11.5 %collective-permute-done.4 = bf16[1024,256]{1,0:T(8,128)(2,1)} collective-permute-done((bf16[1024,256]{1,0:T(8,128)(2,1)}, bf16[1024,256]{1,0:T(8,128)(2,1)}, u32[]{:S(2)}, u32[]{:S(2)}) %collective-permute-start.4) | collective-permute-done | bytes 524320 | tf_op jit(solution)/shard_map/ppermute | solution.py:23
  171.8 5.3 %collective-permute-done.5 = bf16[1024,256]{1,0:T(8,128)(2,1)} collective-permute-done((bf16[1024,256]{1,0:T(8,128)(2,1)}, bf16[1024,256]{1,0:T(8,128)(2,1)}, u32[]{:S(2)}, u32[]{:S(2)}) %collective-permute-start.5) | collective-permute-done | bytes 524320 | tf_op jit(solution)/shard_map/ppermute | solution.py:23
  187.8 4.0 %collective-permute-start.25 = (bf16[256,128]{0,1:T(8,128)(2,1)S(1)}, bf16[256,128]{0,1:T(8,128)(2,1)S(1)}, u32[]{:S(2)}, u32[]{:S(2)}) collective-permute-start(bf16[256,128]{0,1:T(8,128)(2,1)S(1)} %get-tuple-element.8), channel_id=1, source_target_pairs={{0,128},{128,0},{256,384},{384,256},{1,129},{129,1},{257,385},{385... | collective-permute-start | bytes 196616 | tf_op jit(solution)/shard_map/ppermute | solution.py:23
  197.2 6.1 %collective-permute-done.28 = bf16[256,512]{1,0:T(8,128)(2,1)S(1)} collective-permute-done((bf16[256,512]{1,0:T(8,128)(2,1)S(1)}, bf16[256,512]{1,0:T(8,128)(2,1)S(1)}, u32[]{:S(2)}, u32[]{:S(2)}) %collective-permute-start.28) | collective-permute-done | bytes 262176 | tf_op jit(solution)/shard_map/ppermute | solution.py:23
  203.5 6.5 %collective-permute-start.29 = (bf16[256,256]{1,0:T(8,128)(2,1)S(1)}, bf16[256,256]{1,0:T(8,128)(2,1)S(1)}, u32[]{:S(2)}, u32[]{:S(2)}) collective-permute-start(bf16[256,256]{1,0:T(8,128)(2,1)S(1)} %slice.156), channel_id=1, source_target_pairs={{0,32},{16,48},{32,0},{48,16},{64,96},{80,112},{96,64},{112,80},{1... | collective-permute-start | bytes 393224 | tf_op jit(solution)/shard_map/ppermute | solution.py:23
  213.9 5.2 %collective-permute-start.30 = (bf16[256,128]{1,0:T(8,128)(2,1)S(1)}, bf16[256,128]{1,0:T(8,128)(2,1)S(1)}, u32[]{:S(2)}, u32[]{:S(2)}) collective-permute-start(bf16[256,128]{1,0:T(8,128)(2,1)S(1)} %slice.158), channel_id=1, source_target_pairs={{0,64},{16,80},{32,96},{48,112},{64,0},{80,16},{96,32},{112,48},{1... | collective-permute-start | bytes 196616 | tf_op jit(solution)/shard_map/ppermute | solution.py:23
  219.1 4.9 %collective-permute-done.30 = bf16[256,128]{1,0:T(8,128)(2,1)S(1)} collective-permute-done((bf16[256,128]{1,0:T(8,128)(2,1)S(1)}, bf16[256,128]{1,0:T(8,128)(2,1)S(1)}, u32[]{:S(2)}, u32[]{:S(2)}) %collective-permute-start.30) | collective-permute-done | bytes 65568 | tf_op jit(solution)/shard_map/ppermute | solution.py:23
  228.7 4.0 %collective-permute-start.34 = (bf16[512,128]{1,0:T(8,128)(2,1)S(1)}, bf16[512,128]{1,0:T(8,128)(2,1)S(1)}, u32[]{:S(2)}, u32[]{:S(2)}) collective-permute-start(bf16[512,128]{1,0:T(8,128)(2,1)S(1)} %get-tuple-element.13), channel_id=1, source_target_pairs={{0,6},{2,4},{4,2},{6,0},{1,7},{3,5},{5,3},{7,1},{8,14},{10,12},{12... | collective-permute-start | bytes 393224 | tf_op jit(solution)/shard_map/ppermute | solution.py:23
  242.7 10.8 %collective-permute-start.35 = (bf16[256,128]{1,0:T(8,128)(2,1)S(1)}, bf16[256,128]{1,0:T(8,128)(2,1)S(1)}, u32[]{:S(2)}, u32[]{:S(2)}) collective-permute-start(bf16[256,128]{1,0:T(8,128)(2,1)S(1)} %slice.157), channel_id=1, source_target_pairs={{0,8},{8,0},{1,9},{9,1},{2,10},{10,2},{3,11},{11,3},{4,12},{12,4},... | collective-permute-start | bytes 196616 | tf_op jit(solution)/shard_map/ppermute | solution.py:23
  (109 shorter events, 96.6 us)
Async XLA Ops:
  0.6 20.3 %collective-permute-start.9 = (bf16[256,128]{1,0:T(8,128)(2,1)}, bf16[256,128]{1,0:T(8,128)(2,1)S(1)}, u32[]{:S(2)}, u32[]{:S(2)}) collective-permute-start(bf16[256,128]{1,0:T(8,128)(2,1)} %param.9), channel_id=1, source_target_pairs={{0,8},{8,0},{1,9},{9,1},{2,10},{10,2},{3,11},{11,3},{4,12},{12,4},... | collective-permute-start | bytes 196616 | tf_op jit(solution)/shard_map/ppermute | solution.py:23
  21.7 16.5 %collective-permute-start.12 = (bf16[2,256,128]{2,1,0:T(8,128)(2,1)S(1)}, bf16[2,256,128]{2,1,0:T(8,128)(2,1)S(1)}, u32[]{:S(2)}, u32[]{:S(2)}) collective-permute-start(bf16[2,256,128]{2,1,0:T(8,128)(2,1)S(1)} %get-tuple-element.42), channel_id=1, source_target_pairs={{0,6},{2,4},{4,2},{6,0},{1,7},{3,5},{5,3},{7,1},{8,14},{10,12},{12... | collective-permute-start | bytes 393224 | tf_op jit(solution)/shard_map/ppermute | solution.py:23
  26.7 11.6 %collective-permute-start.11 = (bf16[2,256,128]{2,1,0:T(8,128)(2,1)S(1)}, bf16[2,256,128]{2,1,0:T(8,128)(2,1)S(1)}, u32[]{:S(2)}, u32[]{:S(2)}) collective-permute-start(bf16[2,256,128]{2,1,0:T(8,128)(2,1)S(1)} %get-tuple-element.42), channel_id=1, source_target_pairs={{0,4},{2,6},{4,0},{6,2},{1,5},{3,7},{5,1},{7,3},{8,12},{10,14},{12... | collective-permute-start | bytes 393224 | tf_op jit(solution)/shard_map/ppermute | solution.py:23
  31.6 16.6 %collective-permute-start.6 = (bf16[512,128]{0,1:T(8,128)(2,1)S(1)}, bf16[512,128]{0,1:T(8,128)(2,1)S(1)}, u32[]{:S(2)}, u32[]{:S(2)}) collective-permute-start(bf16[512,128]{0,1:T(8,128)(2,1)S(1)} %pad_maximum_fusion.7), channel_id=1, source_target_pairs={{0,64},{16,80},{32,96},{48,112},{64,0},{80,16},{96,32},{112,48},{1... | collective-permute-start | bytes 393224 | tf_op jit(solution)/shard_map/ppermute | solution.py:23
  38.4 15.5 %collective-permute-start.15 = (bf16[2,256,128]{2,1,0:T(8,128)(2,1)S(1)}, bf16[2,256,128]{2,1,0:T(8,128)(2,1)S(1)}, u32[]{:S(2)}, u32[]{:S(2)}) collective-permute-start(bf16[2,256,128]{2,1,0:T(8,128)(2,1)S(1)} %get-tuple-element.21), channel_id=1, source_target_pairs={{0,384},{128,256},{256,128},{384,0},{1,385},{129,257},{257,129},{3... | collective-permute-start | bytes 393224 | tf_op jit(solution)/shard_map/ppermute | solution.py:23
  40.6 13.3 %collective-permute-start.14 = (bf16[2,256,128]{2,1,0:T(8,128)(2,1)S(1)}, bf16[2,256,128]{2,1,0:T(8,128)(2,1)S(1)}, u32[]{:S(2)}, u32[]{:S(2)}) collective-permute-start(bf16[2,256,128]{2,1,0:T(8,128)(2,1)S(1)} %get-tuple-element.22), channel_id=1, source_target_pairs={{0,256},{128,384},{256,0},{384,128},{1,257},{129,385},{257,1},{385... | collective-permute-start | bytes 393224 | tf_op jit(solution)/shard_map/ppermute | solution.py:23
  48.3 13.1 %collective-permute-start.7 = (bf16[512,256]{0,1:T(8,128)(2,1)S(1)}, bf16[512,256]{0,1:T(8,128)(2,1)S(1)}, u32[]{:S(2)}, u32[]{:S(2)}) collective-permute-start(bf16[512,256]{0,1:T(8,128)(2,1)S(1)} %pad_maximum_fusion.4), channel_id=1, source_target_pairs={{0,32},{16,48},{32,0},{48,16},{64,96},{80,112},{96,64},{112,80},{1... | collective-permute-start | bytes 786440 | tf_op jit(solution)/shard_map/ppermute | solution.py:23
  54.0 10.1 %collective-permute-start.16 = (bf16[4,2,256,128]{3,2,1,0:T(8,128)(2,1)S(1)}, bf16[4,2,256,128]{3,2,1,0:T(8,128)(2,1)S(1)}, u32[]{:S(2)}, u32[]{:S(2)}) collective-permute-start(bf16[4,2,256,128]{3,2,1,0:T(8,128)(2,1)S(1)} %get-tuple-element.19), channel_id=1, source_target_pairs={{0,1},{1,0},{2,3},{3,2},{4,5},{5,4},{6,7},{7,6},{8,9},{9,8},{10,11... | collective-permute-start | bytes 1572872 | tf_op jit(solution)/shard_map/ppermute | solution.py:23
  61.4 14.9 %collective-permute-start.8 = (bf16[512,512]{0,1:T(8,128)(2,1)S(1)}, bf16[512,512]{0,1:T(8,128)(2,1)}, u32[]{:S(2)}, u32[]{:S(2)}) collective-permute-start(bf16[512,512]{0,1:T(8,128)(2,1)S(1)} %pad_maximum_fusion.1), channel_id=1, source_target_pairs={{0,16},{16,0},{32,48},{48,32},{64,80},{80,64},{96,112},{112,96},{1... | collective-permute-start | bytes 1572872 | tf_op jit(solution)/shard_map/ppermute | solution.py:23
  78.1 16.4 %collective-permute-start.19 = (bf16[512,128]{0,1:T(8,128)(2,1)S(1)}, bf16[512,128]{0,1:T(8,128)(2,1)S(1)}, u32[]{:S(2)}, u32[]{:S(2)}) collective-permute-start(bf16[512,128]{0,1:T(8,128)(2,1)S(1)} %get-tuple-element.16), channel_id=1, source_target_pairs={{0,384},{128,256},{256,128},{384,0},{1,385},{129,257},{257,129},{3... | collective-permute-start | bytes 393224 | tf_op jit(solution)/shard_map/ppermute | solution.py:23
  80.5 14.0 %collective-permute-start.18 = (bf16[512,128]{0,1:T(8,128)(2,1)S(1)}, bf16[512,128]{0,1:T(8,128)(2,1)S(1)}, u32[]{:S(2)}, u32[]{:S(2)}) collective-permute-start(bf16[512,128]{0,1:T(8,128)(2,1)S(1)} %get-tuple-element.17), channel_id=1, source_target_pairs={{0,256},{128,384},{256,0},{384,128},{1,257},{129,385},{257,1},{385... | collective-permute-start | bytes 393224 | tf_op jit(solution)/shard_map/ppermute | solution.py:23
  88.0 18.2 %collective-permute-start = (bf16[128,256]{1,0:T(8,128)(2,1)S(1)}, bf16[128,256]{1,0:T(8,128)(2,1)S(1)}, u32[]{:S(2)}, u32[]{:S(2)}) collective-permute-start(bf16[128,256]{1,0:T(8,128)(2,1)S(1)} %copy-done.2), channel_id=1, source_target_pairs={{0,64},{16,80},{32,96},{48,112},{64,0},{80,16},{96,32},{112,48},{1... | collective-permute-start | bytes 196616 | tf_op jit(solution)/shard_map/ppermute | solution.py:23
  95.3 20.8 %collective-permute-start.20 = (bf16[256,256]{0,1:T(8,128)(2,1)S(1)}, bf16[256,256]{0,1:T(8,128)(2,1)S(1)}, u32[]{:S(2)}, u32[]{:S(2)}) collective-permute-start(bf16[256,256]{0,1:T(8,128)(2,1)S(1)} %get-tuple-element.38), channel_id=1, source_target_pairs={{0,8},{8,0},{1,9},{9,1},{2,10},{10,2},{3,11},{11,3},{4,12},{12,4},... | collective-permute-start | bytes 393224 | tf_op jit(solution)/shard_map/ppermute | solution.py:23
  106.2 18.2 %collective-permute-start.1 = (bf16[256,256]{1,0:T(8,128)(2,1)S(1)}, bf16[256,256]{1,0:T(8,128)(2,1)S(1)}, u32[]{:S(2)}, u32[]{:S(2)}) collective-permute-start(bf16[256,256]{1,0:T(8,128)(2,1)S(1)} %pad_maximum_fusion.10), channel_id=1, source_target_pairs={{0,32},{16,48},{32,0},{48,16},{64,96},{80,112},{96,64},{112,80},{1... | collective-permute-start | bytes 393224 | tf_op jit(solution)/shard_map/ppermute | solution.py:23
  116.2 14.6 %collective-permute-start.21 = (bf16[512,256]{0,1:T(8,128)(2,1)S(1)}, bf16[512,256]{0,1:T(8,128)(2,1)S(1)}, u32[]{:S(2)}, u32[]{:S(2)}) collective-permute-start(bf16[512,256]{0,1:T(8,128)(2,1)S(1)} %pad_maximum_fusion.5), channel_id=1, source_target_pairs={{0,2},{2,0},{4,6},{6,4},{1,3},{3,1},{5,7},{7,5},{8,10},{10,8},{12,... | collective-permute-start | bytes 786440 | tf_op jit(solution)/shard_map/ppermute | solution.py:23
  120.7 10.8 %collective-permute-start.22 = (bf16[512,256]{0,1:T(8,128)(2,1)S(1)}, bf16[512,256]{0,1:T(8,128)(2,1)S(1)}, u32[]{:S(2)}, u32[]{:S(2)}) collective-permute-start(bf16[512,256]{0,1:T(8,128)(2,1)S(1)} %pad_maximum_fusion.5), channel_id=1, source_target_pairs={{0,4},{2,6},{4,0},{6,2},{1,5},{3,7},{5,1},{7,3},{8,12},{10,14},{12... | collective-permute-start | bytes 786440 | tf_op jit(solution)/shard_map/ppermute | solution.py:23
  124.5 16.0 %collective-permute-start.2 = (bf16[512,256]{1,0:T(8,128)(2,1)S(1)}, bf16[512,256]{1,0:T(8,128)(2,1)S(1)}, u32[]{:S(2)}, u32[]{:S(2)}) collective-permute-start(bf16[512,256]{1,0:T(8,128)(2,1)S(1)} %pad_maximum_fusion.6), channel_id=1, source_target_pairs={{0,16},{16,0},{32,48},{48,32},{64,80},{80,64},{96,112},{112,96},{1... | collective-permute-start | bytes 786440 | tf_op jit(solution)/shard_map/ppermute | solution.py:23
  137.9 41.0 %collective-permute-start.24 = (bf16[2048,256]{0,1:T(8,128)(2,1)}, bf16[2048,256]{0,1:T(8,128)(2,1)}, u32[]{:S(2)}, u32[]{:S(2)}) collective-permute-start(bf16[2048,256]{0,1:T(8,128)(2,1)} %get-tuple-element.26), channel_id=1, source_target_pairs={{0,1},{1,0},{2,3},{3,2},{4,5},{5,4},{6,7},{7,6},{8,9},{9,8},{10,11... | collective-permute-start | bytes 3145736 | tf_op jit(solution)/shard_map/ppermute | solution.py:23
  141.2 16.9 %collective-permute-start.3 = (bf16[1024,256]{1,0:T(8,128)(2,1)}, bf16[1024,256]{1,0:T(8,128)(2,1)}, u32[]{:S(2)}, u32[]{:S(2)}) collective-permute-start(bf16[1024,256]{1,0:T(8,128)(2,1)} %get-tuple-element.24), channel_id=1, source_target_pairs={{0,128},{128,0},{256,384},{384,256},{1,129},{129,1},{257,385},{385... | collective-permute-start | bytes 1572872 | tf_op jit(solution)/shard_map/ppermute | solution.py:23
  144.1 26.6 %collective-permute-start.4 = (bf16[1024,256]{1,0:T(8,128)(2,1)}, bf16[1024,256]{1,0:T(8,128)(2,1)}, u32[]{:S(2)}, u32[]{:S(2)}) collective-permute-start(bf16[1024,256]{1,0:T(8,128)(2,1)} %get-tuple-element.24), channel_id=1, source_target_pairs={{0,256},{128,384},{256,0},{384,128},{1,257},{129,385},{257,1},{385... | collective-permute-start | bytes 1572872 | tf_op jit(solution)/shard_map/ppermute | solution.py:23
  148.6 28.5 %collective-permute-start.5 = (bf16[1024,256]{1,0:T(8,128)(2,1)}, bf16[1024,256]{1,0:T(8,128)(2,1)}, u32[]{:S(2)}, u32[]{:S(2)}) collective-permute-start(bf16[1024,256]{1,0:T(8,128)(2,1)} %get-tuple-element.24), channel_id=1, source_target_pairs={{0,384},{128,256},{256,128},{384,0},{1,385},{129,257},{257,129},{3... | collective-permute-start | bytes 1572872 | tf_op jit(solution)/shard_map/ppermute | solution.py:23
  203.5 10.3 %collective-permute-start.29 = (bf16[256,256]{1,0:T(8,128)(2,1)S(1)}, bf16[256,256]{1,0:T(8,128)(2,1)S(1)}, u32[]{:S(2)}, u32[]{:S(2)}) collective-permute-start(bf16[256,256]{1,0:T(8,128)(2,1)S(1)} %slice.156), channel_id=1, source_target_pairs={{0,32},{16,48},{32,0},{48,16},{64,96},{80,112},{96,64},{112,80},{1... | collective-permute-start | bytes 393224 | tf_op jit(solution)/shard_map/ppermute | solution.py:23
  213.9 10.1 %collective-permute-start.30 = (bf16[256,128]{1,0:T(8,128)(2,1)S(1)}, bf16[256,128]{1,0:T(8,128)(2,1)S(1)}, u32[]{:S(2)}, u32[]{:S(2)}) collective-permute-start(bf16[256,128]{1,0:T(8,128)(2,1)S(1)} %slice.158), channel_id=1, source_target_pairs={{0,64},{16,80},{32,96},{48,112},{64,0},{80,16},{96,32},{112,48},{1... | collective-permute-start | bytes 196616 | tf_op jit(solution)/shard_map/ppermute | solution.py:23
  242.7 15.7 %collective-permute-start.35 = (bf16[256,128]{1,0:T(8,128)(2,1)S(1)}, bf16[256,128]{1,0:T(8,128)(2,1)S(1)}, u32[]{:S(2)}, u32[]{:S(2)}) collective-permute-start(bf16[256,128]{1,0:T(8,128)(2,1)S(1)} %slice.157), channel_id=1, source_target_pairs={{0,8},{8,0},{1,9},{9,1},{2,10},{10,2},{3,11},{11,3},{4,12},{12,4},... | collective-permute-start | bytes 196616 | tf_op jit(solution)/shard_map/ppermute | solution.py:23
  (16 other events, 150.9 us)

commit v2 on v1

v2 whole, which is shorter than its diff:
```python
import jax
import jax.numpy as jnp
from jax import lax
from jax.experimental import pallas as pl
from jax.experimental.pallas import tpu as pltpu
from jax.sharding import Mesh, PartitionSpec as P

STEP = 10

beta_first = 0.95
beta_second = 0.95
epsilon = 1e-08

AXES = ("x", "zl", "zh", "y", "core")
SIZES = (4, 8, 2, 4, 2)
BF16 = jnp.bfloat16
F32 = jnp.float32


def swap(value, axis, offset):
    size = dict(zip(AXES, SIZES))[axis]
    return lax.ppermute(value, axis, [(i, i ^ offset) for i in range(size)])


def exchange(blocks, axis):
    return lax.all_to_all(blocks, axis, 0, 0, tiled=True)


def spread(value, axis):
    return exchange(jnp.broadcast_to(value[None], (4,) + value.shape), axis)


def place(index, sources, shape, size, moves, vmem):
    def kernel(index_ref, *refs):
        out_ref = refs[-1]
        for n, (source, lead, row, col, out_col) in enumerate(moves):
            tile = refs[source][lead + (pl.ds(row * size, size), pl.ds(col * size, size))]
            to = pl.multiple_of(index_ref[n] * size, size)
            out_ref[pl.ds(to, size), out_col * size : (out_col + 1) * size] = tile

    in_vmem = pl.BlockSpec(memory_space=pltpu.VMEM)
    nbytes = 4 * shape[0] * shape[1]
    return pl.pallas_call(
        kernel,
        out_shape=jax.ShapeDtypeStruct(shape, BF16),
        in_specs=[pl.BlockSpec(memory_space=pltpu.SMEM)] + [in_vmem] * len(sources),
        out_specs=in_vmem,
        compiler_params=pltpu.CompilerParams(vmem_limit_bytes=vmem),
        cost_estimate=pl.CostEstimate(flops=0, bytes_accessed=nbytes, transcendentals=0),
    )(index, *sources)


def reversed_bits(o):
    return ((o & 1) << 2) | (o & 2) | (o >> 2)


def shards(grad, moment, second, left_basis, right_basis):
    rows, cols = grad.shape
    x = lax.axis_index("x")
    zl = lax.axis_index("zl")
    zh = lax.axis_index("zh")
    y = lax.axis_index("y")
    core = lax.axis_index("core")
    barrier = lax.optimization_barrier

    moment_new = beta_first * moment + (1.0 - beta_first) * grad.astype(F32)
    line = jnp.concatenate(
        [grad, moment_new.astype(BF16), left_basis[:, :cols], left_basis[:, cols:]], axis=0
    )
    line, basis = barrier((line, right_basis))

    line = jnp.concatenate([line, swap(line, "zl", 4)], axis=1)
    basis = lax.all_gather(basis, "zh")
    line, basis = barrier((line, basis))

    line = jnp.concatenate([line, swap(line, "zl", 2)], axis=1)
    basis = spread(basis, "y")
    basis = basis.reshape(2, 2, 2, rows, cols).transpose(2, 0, 1, 3, 4)
    basis = basis.reshape(4, 2, rows, cols)
    line, basis = barrier((line, basis))

    line = jnp.concatenate([line, swap(line, "zl", 1)], axis=1)
    basis = exchange(basis, "x")
    basis = [basis, swap(basis, "core", 1)]
    index, moves = [], []
    for oc in range(2):
        for ox in range(4):
            for y0 in range(2):
                for half in range(2):
                    owner = y0 * 4 + (core ^ oc) * 2 + half
                    index.append(reversed_bits(owner ^ zl))
                    moves.append((oc, (ox, y0), half, 0, ox))
    right = place(
        jnp.stack(index).astype(jnp.int32), basis, (8 * cols, 4 * cols), cols, moves, 4 * 2**20
    )

    partial = jnp.dot(line[: 2 * rows], right, preferred_element_type=F32).astype(BF16)
    left, partial = barrier((line[2 * rows :], partial))
    partial = partial.reshape(2 * rows, 4, cols).transpose(1, 0, 2)
    total = jnp.sum(exchange(partial, "x").astype(F32), axis=0).astype(BF16)
    rotated = jnp.concatenate([total[:rows], total[rows:]], axis=1)

    left = [left] + [swap(left, "x", k) for k in (1, 3, 2)]
    rotated = jnp.concatenate([rotated, swap(rotated, "zh", 1)], axis=0)
    rotated, *left = barrier((rotated, *left))
    index, moves = [], []
    for number, ox in enumerate((0, 1, 3, 2)):
        for p in range(8):
            block = (x ^ ox) * 8 + (zl ^ reversed_bits(p))
            n = block // 2
            place_of = ((((n & 1) ^ core) * 4 + ((n >> 1) & 3)) * 2 + ((n >> 3) ^ zh)) * 2
            for half in range(2):
                index.append(place_of + (block & 1))
                moves.append((number, (), half, p, half))
    rotated = spread(rotated, "y").reshape(8 * rows, 2 * cols)
    left = place(
        jnp.stack(index).astype(jnp.int32), left, (32 * cols, 2 * cols), cols, moves, 8 * 2**20
    )
    other = swap(rotated, "core", 1)
    contract_rows = (((0,), (0,)), ((), ()))
    rot = lax.dot_general(
        left[: 8 * rows], rotated, contract_rows, preferred_element_type=F32
    ) + lax.dot_general(left[8 * rows :], other, contract_rows, preferred_element_type=F32)
    first, other = rot[:, :cols], rot[:, cols:]
    second_new = beta_second * second + (1.0 - beta_second) * first * first
    bias_first = 1.0 - beta_first**STEP
    bias_second = 1.0 - beta_second**STEP
    normed = (other / bias_first / (jnp.sqrt(second_new / bias_second) + epsilon)).astype(BF16)

    normed = spread(normed, "x").transpose(1, 0, 2).reshape(rows, 4 * cols)
    spectral = lax.dot_general(
        normed, right, (((1,), (1,)), ((), ())), preferred_element_type=F32
    )
    for offset in (1, 2, 4):
        half = spectral.shape[1] // 2
        sent = swap(spectral[:, half:].astype(BF16), "zl", offset)
        spectral = spectral[:, :half] + sent.astype(F32)
    spectral = spectral.astype(BF16)

    kept = barrier(jnp.dot(left[: 8 * rows], spectral, preferred_element_type=F32))
    sent = jnp.dot(left[8 * rows :], spectral, preferred_element_type=F32).astype(BF16)
    update = (kept + swap(sent, "core", 1).astype(F32)).astype(BF16)
    update = exchange(update.reshape(4, 2 * rows, cols), "y")
    update = jnp.sum(update.astype(F32), axis=0)
    update = update[:rows] + swap(update[rows:].astype(BF16), "zh", 1).astype(F32)
    return (moment_new, second_new, update.astype(BF16))


def solution(mesh):
    fine = Mesh(mesh.devices.reshape(SIZES), AXES)
    spec = P(("zh", "y", "core"), ("x", "zl"))
    left_spec = P(("x", "zl"), ("zh", "y", "core"))
    return jax.shard_map(
        shards,
        mesh=fine,
        in_specs=(spec, spec, spec, left_spec, spec),
        out_specs=(spec, spec, spec),
        check_vma=False,
    )
```

time: 264 us -> 235 us (0.89); the launches traced: 259 us -> 233 us
  starting transfers between devices: 152 us -> 67.4 us
  blocking collectives: 0 us -> 67.4 us
  local copies, waits for them, and re-layouts: 15.2 us -> 7.5 us
  waiting for transfers between devices: 80 us -> 76.1 us
    ppermute x36 -> x14, starting transfers between devices: 152 us -> 58.1 us  [swap(): return lax.ppermute(value, axis, [(i, i ^ offset) for i in range(size)])]
    all_to_all x0 -> x4, blocking collectives: none -> 52.1 us  [exchange(): return lax.all_to_all(blocks, axis, 0, 0, tiled=True)]
    all_gather x0 -> x1, blocking collectives: none -> 15.3 us  [shards(): basis = lax.all_gather(basis, 'zh')]
    all_to_all x0 -> x2, starting transfers between devices: none -> 9.23 us  [exchange(): return lax.all_to_all(blocks, axis, 0, 0, tiled=True)]
    unnamed x21 -> x19, local copies, waits for them, and re-layouts: 10.8 us -> 4.27 us
    ppermute x36 -> x14, waiting for transfers between devices: 80 us -> 75.1 us  [swap(): return lax.ppermute(value, axis, [(i, i ^ offset) for i in range(size)])]
    concatenate x4 -> x1, local copies, waits for them, and re-layouts: 3.9 us -> 0.08 us  [shards(): line = jnp.concatenate([line, swap(line, 'zl', 1)], axis=1)]
  transfers between devices with their start and end apart: 36 -> 16, of which waited for: 17 -> 10; matrix products, arithmetic and copies ran while one was open for 5% -> 2% of each run, Pallas kernels for 1% -> 0%
where the time goes in v2:
time: 235 us; the launch traced here: 233 us
  waiting for transfers between devices  76.1 us (32%)
  starting transfers between devices  67.4 us (29%)
  blocking collectives  67.4 us (29%)
  local copies, waits for them, and re-layouts  7.5 us (3%)
  matrix products  5.47 us (2%)
  other arithmetic  5.39 us (2%)
    ppermute x14, waiting for transfers between devices, swap(): return lax.ppermute(value, axis, [(i, i ^ offset) for i in range(size)])  75.1 us
    ppermute x14, starting transfers between devices, swap(): return lax.ppermute(value, axis, [(i, i ^ offset) for i in range(size)])  58.1 us
    all_to_all x4, blocking collectives, exchange(): return lax.all_to_all(blocks, axis, 0, 0, tiled=True)  52.1 us
    all_gather x1, blocking collectives, shards(): basis = lax.all_gather(basis, 'zh')  15.3 us
    all_to_all x2, starting transfers between devices, exchange(): return lax.all_to_all(blocks, axis, 0, 0, tiled=True)  9.23 us
  transfers between devices with their start and end apart: 16, of which 10 were waited for; matrix products, arithmetic and copies ran while one was open for 2% of the time, Pallas kernels for 0%

profile of v2, /device:TPU:6, one launch (start us, length us, event | category | flops | bytes accessed | tf_op | source)
XLA Modules:
  0.0 233.1 jit_solution(1197366755241942269)
XLA Ops:
  3.9 9.1 %collective-permute-start = (bf16[768,128]{1,0:T(8,128)(2,1)S(1)}, bf16[768,128]{1,0:T(8,128)(2,1)S(1)}, u32[]{:S(2)}, u32[]{:S(2)}) collective-permute-start(bf16[768,128]{1,0:T(8,128)(2,1)S(1)} %pad_maximum_fusion.3), channel_id=1, source_target_pairs={{0,64},{16,80},{32,96},{48,112},{64,0},{80,16},{96,32},{112,48},{1... | collective-permute-start | bytes 589832 | tf_op jit(solution)/shard_map/ppermute | solution.py:22
  13.0 15.3 %all-gather = bf16[512,128]{1,0:T(8,128)(2,1)S(1)} all-gather(bf16[256,128]{1,0:T(8,128)(2,1)} %param.9), channel_id=2, replica_groups=mesh['x'=4,'zl'=8,'zh'=2,'y'=4,'core'=2] {'zh'}, dimensions={0}, use_global_device_ids=true | all-gather | bytes 196608 | tf_op jit(solution)/shard_map/all_gather | solution.py:73
  28.3 7.8 %collective-permute-done = bf16[768,128]{1,0:T(8,128)(2,1)S(1)} collective-permute-done((bf16[768,128]{1,0:T(8,128)(2,1)S(1)}, bf16[768,128]{1,0:T(8,128)(2,1)S(1)}, u32[]{:S(2)}, u32[]{:S(2)}) %collective-permute-start) | collective-permute-done | bytes 196640 | tf_op jit(solution)/shard_map/ppermute | solution.py:22
  37.1 4.5 %all-to-all-start = ((bf16[4,2,256,128]{3,2,1,0:T(8,128)(2,1)}), bf16[4,2,256,128]{3,2,1,0:T(8,128)(2,1)S(1)}, u32[]{:S(2)}, u32[]{:S(2)}) async-start(bf16[4,2,256,128]{3,2,1,0:T(8,128)(2,1)} %broadcast_in_dim.6), calls=%async_computation | async-start | bytes 1048576 | tf_op jit(solution)/shard_map/all_to_all | solution.py:26
  41.5 8.0 %collective-permute-start.1 = (bf16[768,256]{1,0:T(8,128)(2,1)S(1)}, bf16[768,256]{1,0:T(8,128)(2,1)S(1)}, u32[]{:S(2)}, u32[]{:S(2)}) collective-permute-start(bf16[768,256]{1,0:T(8,128)(2,1)S(1)} %pad_maximum_fusion.1), channel_id=1, source_target_pairs={{0,32},{16,48},{32,0},{48,16},{64,96},{80,112},{96,64},{112,80},{1... | collective-permute-start | bytes 1179656 | tf_op jit(solution)/shard_map/ppermute | solution.py:22
  50.5 12.9 %collective-permute-done.1 = bf16[768,256]{1,0:T(8,128)(2,1)S(1)} collective-permute-done((bf16[768,256]{1,0:T(8,128)(2,1)S(1)}, bf16[768,256]{1,0:T(8,128)(2,1)S(1)}, u32[]{:S(2)}, u32[]{:S(2)}) %collective-permute-start.1) | collective-permute-done | bytes 393248 | tf_op jit(solution)/shard_map/ppermute | solution.py:22
  65.4 12.2 %all_to_all.30.refs_0_ = bf16[4,2,256,128]{3,2,1,0:T(8,128)(2,1)S(1)} all-to-all(bf16[4,2,256,128]{3,2,1,0:T(8,128)(2,1)S(1)} %bitcast.63), channel_id=1, replica_groups=mesh['x'=4,'zl'=8,'zh'=2,'y'=4,'core'=2] {'x'}, dimensions={0} | all-to-all | bytes 1048576 | tf_op jit(solution)/shard_map/all_to_all | solution.py:26
  79.7 5.1 %collective-permute-done.2 = bf16[768,512]{1,0:T(8,128)(2,1)S(1)} collective-permute-done((bf16[768,512]{1,0:T(8,128)(2,1)S(1)}, bf16[768,512]{1,0:T(8,128)(2,1)S(1)}, u32[]{:S(2)}, u32[]{:S(2)}) %collective-permute-start.2) | collective-permute-done | bytes 786464 | tf_op jit(solution)/shard_map/ppermute | solution.py:22
  87.3 4.8 %all-to-all-start.2 = ((bf16[4,512,128]{2,1,0:T(8,128)(2,1)}), bf16[4,512,128]{2,1,0:T(8,128)(2,1)}, u32[]{:S(2)}, u32[]{:S(2)}) async-start(bf16[4,512,128]{2,1,0:T(8,128)(2,1)} %bitcast_bitcast_fusion), calls=%async_computation.2 | async-start | bytes 1048576 | tf_op jit(solution)/shard_map/all_to_all | solution.py:26
  92.1 3.4 %collective-permute-start.7 = (bf16[256,1024]{1,0:T(8,128)(2,1)S(1)}, bf16[256,1024]{1,0:T(8,128)(2,1)S(1)}, u32[]{:S(2)}, u32[]{:S(2)}) collective-permute-start(bf16[256,1024]{1,0:T(8,128)(2,1)S(1)} %slice.78.refs_0_), channel_id=1, source_target_pairs={{0,256},{128,384},{256,0},{384,128},{1,257},{129,385},{257,1},{385... | collective-permute-start | bytes 1572872 | tf_op jit(solution)/shard_map/ppermute | solution.py:22
  95.4 4.0 %collective-permute-start.6 = (bf16[256,1024]{1,0:T(8,128)(2,1)S(1)}, bf16[256,1024]{1,0:T(8,128)(2,1)S(1)}, u32[]{:S(2)}, u32[]{:S(2)}) collective-permute-start(bf16[256,1024]{1,0:T(8,128)(2,1)S(1)} %slice.78.refs_0_), channel_id=1, source_target_pairs={{0,384},{128,256},{256,128},{384,0},{1,385},{129,257},{257,129},{3... | collective-permute-start | bytes 1572872 | tf_op jit(solution)/shard_map/ppermute | solution.py:22
  99.4 1.9 collective-permute-start.5
  102.5 9.1 %collective-permute-start.4 = (bf16[256,256]{1,0:T(8,128)(2,1)S(1)}, bf16[256,256]{1,0:T(8,128)(2,1)S(1)}, u32[]{:S(2)}, u32[]{:S(2)}) collective-permute-start(bf16[256,256]{1,0:T(8,128)(2,1)S(1)} %pad_maximum_fusion.4), channel_id=1, source_target_pairs={{0,8},{8,0},{1,9},{9,1},{2,10},{10,2},{3,11},{11,3},{4,12},{12,4},... | collective-permute-start | bytes 393224 | tf_op jit(solution)/shard_map/ppermute | solution.py:22
  111.7 13.2 %collective-permute-done.4 = bf16[256,256]{1,0:T(8,128)(2,1)S(1)} collective-permute-done((bf16[256,256]{1,0:T(8,128)(2,1)S(1)}, bf16[256,256]{1,0:T(8,128)(2,1)S(1)}, u32[]{:S(2)}, u32[]{:S(2)}) %collective-permute-start.4) | collective-permute-done | bytes 131104 | tf_op jit(solution)/shard_map/ppermute | solution.py:22
  125.1 16.1 %all_to_all.31 = bf16[4,512,256]{2,1,0:T(8,128)(2,1)} all-to-all(bf16[4,512,256]{2,1,0:T(8,128)(2,1)S(1)} %broadcast_in_dim.7), channel_id=1, replica_groups=mesh['x'=4,'zl'=8,'zh'=2,'y'=4,'core'=2] {'y'}, dimensions={0} | all-to-all | bytes 2097152 | tf_op jit(solution)/shard_map/all_to_all | solution.py:26
  141.2 1.9 collective-permute-start.8
  153.8 11.4 %all_to_all.32 = bf16[4,256,128]{1,2,0:T(8,128)(2,1)S(1)} all-to-all(bf16[4,256,128]{1,2,0:T(8,128)(2,1)S(1)} %broadcast_in_dim.8), channel_id=1, replica_groups=mesh['x'=4,'zl'=8,'zh'=2,'y'=4,'core'=2] {'x'}, dimensions={0} | all-to-all | bytes 524288 | tf_op jit(solution)/shard_map/all_to_all | solution.py:26
  165.7 4.6 %collective-permute-start.9 = (bf16[256,512]{1,0:T(8,128)(2,1)S(1)}, bf16[256,512]{1,0:T(8,128)(2,1)S(1)}, u32[]{:S(2)}, u32[]{:S(2)}) collective-permute-start(bf16[256,512]{1,0:T(8,128)(2,1)S(1)} %slice.124), channel_id=1, source_target_pairs={{0,16},{16,0},{32,48},{48,32},{64,80},{80,64},{96,112},{112,96},{1... | collective-permute-start | bytes 786440 | tf_op jit(solution)/shard_map/ppermute | solution.py:22
  170.3 5.9 %collective-permute-done.9 = bf16[256,512]{1,0:T(8,128)(2,1)S(1)} collective-permute-done((bf16[256,512]{1,0:T(8,128)(2,1)S(1)}, bf16[256,512]{1,0:T(8,128)(2,1)S(1)}, u32[]{:S(2)}, u32[]{:S(2)}) %collective-permute-start.9) | collective-permute-done | bytes 262176 | tf_op jit(solution)/shard_map/ppermute | solution.py:22
  178.2 7.9 %collective-permute-done.10 = bf16[256,256]{1,0:T(8,128)(2,1)S(1)} collective-permute-done((bf16[256,256]{1,0:T(8,128)(2,1)S(1)}, bf16[256,256]{1,0:T(8,128)(2,1)S(1)}, u32[]{:S(2)}, u32[]{:S(2)}) %collective-permute-start.10) | collective-permute-done | bytes 131104 | tf_op jit(solution)/shard_map/ppermute | solution.py:22
  188.0 9.9 %collective-permute-done.11 = bf16[256,128]{1,0:T(8,128)(2,1)S(1)} collective-permute-done((bf16[256,128]{1,0:T(8,128)(2,1)S(1)}, bf16[256,128]{1,0:T(8,128)(2,1)S(1)}, u32[]{:S(2)}, u32[]{:S(2)}) %collective-permute-start.11) | collective-permute-done | bytes 65568 | tf_op jit(solution)/shard_map/ppermute | solution.py:22
  202.3 12.5 %all_to_all.33 = bf16[4,512,128]{2,1,0:T(8,128)(2,1)S(1)} all-to-all(bf16[4,512,128]{2,1,0:T(8,128)(2,1)S(1)} %bitcast.64), channel_id=1, replica_groups=mesh['x'=4,'zl'=8,'zh'=2,'y'=4,'core'=2] {'y'}, dimensions={0} | all-to-all | bytes 1048576 | tf_op jit(solution)/shard_map/all_to_all | solution.py:26
  214.9 6.6 %collective-permute-start.13 = (bf16[256,128]{1,0:T(8,128)(2,1)S(1)}, bf16[256,128]{1,0:T(8,128)(2,1)S(1)}, u32[]{:S(2)}, u32[]{:S(2)}) collective-permute-start(bf16[256,128]{1,0:T(8,128)(2,1)S(1)} %slice.126), channel_id=1, source_target_pairs={{0,8},{8,0},{1,9},{9,1},{2,10},{10,2},{3,11},{11,3},{4,12},{12,4},... | collective-permute-start | bytes 196616 | tf_op jit(solution)/shard_map/ppermute | solution.py:22
  221.4 11.0 %collective-permute-done.13 = bf16[256,128]{1,0:T(8,128)(2,1)S(1)} collective-permute-done((bf16[256,128]{1,0:T(8,128)(2,1)S(1)}, bf16[256,128]{1,0:T(8,128)(2,1)S(1)}, u32[]{:S(2)}, u32[]{:S(2)}) %collective-permute-start.13) | collective-permute-done | bytes 65568 | tf_op jit(solution)/shard_map/ppermute | solution.py:22
  (69 shorter events, 32.0 us)
Async XLA Ops:
  3.9 32.2 %collective-permute-start = (bf16[768,128]{1,0:T(8,128)(2,1)S(1)}, bf16[768,128]{1,0:T(8,128)(2,1)S(1)}, u32[]{:S(2)}, u32[]{:S(2)}) collective-permute-start(bf16[768,128]{1,0:T(8,128)(2,1)S(1)} %pad_maximum_fusion.3), channel_id=1, source_target_pairs={{0,64},{16,80},{32,96},{48,112},{64,0},{80,16},{96,32},{112,48},{1... | collective-permute-start | bytes 589832 | tf_op jit(solution)/shard_map/ppermute | solution.py:22
  37.1 13.4 %all-to-all-start = ((bf16[4,2,256,128]{3,2,1,0:T(8,128)(2,1)}), bf16[4,2,256,128]{3,2,1,0:T(8,128)(2,1)S(1)}, u32[]{:S(2)}, u32[]{:S(2)}) async-start(bf16[4,2,256,128]{3,2,1,0:T(8,128)(2,1)} %broadcast_in_dim.6), calls=%async_computation | async-start | bytes 1048576 | tf_op jit(solution)/shard_map/all_to_all | solution.py:26
  41.5 21.8 %collective-permute-start.1 = (bf16[768,256]{1,0:T(8,128)(2,1)S(1)}, bf16[768,256]{1,0:T(8,128)(2,1)S(1)}, u32[]{:S(2)}, u32[]{:S(2)}) collective-permute-start(bf16[768,256]{1,0:T(8,128)(2,1)S(1)} %pad_maximum_fusion.1), channel_id=1, source_target_pairs={{0,32},{16,48},{32,0},{48,16},{64,96},{80,112},{96,64},{112,80},{1... | collective-permute-start | bytes 1179656 | tf_op jit(solution)/shard_map/ppermute | solution.py:22
  63.4 21.4 %collective-permute-start.2 = (bf16[768,512]{1,0:T(8,128)(2,1)S(1)}, bf16[768,512]{1,0:T(8,128)(2,1)S(1)}, u32[]{:S(2)}, u32[]{:S(2)}) collective-permute-start(bf16[768,512]{1,0:T(8,128)(2,1)S(1)} %pad_maximum_fusion), channel_id=1, source_target_pairs={{0,16},{16,0},{32,48},{48,32},{64,80},{80,64},{96,112},{112,96},{1... | collective-permute-start | bytes 2359304 | tf_op jit(solution)/shard_map/ppermute | solution.py:22
  77.5 7.4 %collective-permute-start.3 = (bf16[4,2,256,128]{3,2,1,0:T(8,128)(2,1)S(1)}, bf16[4,2,256,128]{3,2,1,0:T(8,128)(2,1)S(1)}, u32[]{:S(2)}, u32[]{:S(2)}) collective-permute-start(bf16[4,2,256,128]{3,2,1,0:T(8,128)(2,1)S(1)} %all_to_all.30.refs_0_), channel_id=1, source_target_pairs={{0,1},{1,0},{2,3},{3,2},{4,5},{5,4},{6,7},{7,6},{8,9},{9,8},{10,11... | collective-permute-start | bytes 1572872 | tf_op jit(solution)/shard_map/ppermute | solution.py:22
  84.9 14.5 %copy-start = (bf16[256,1024]{1,0:T(8,128)(2,1)}, bf16[256,1024]{1,0:T(8,128)(2,1)S(1)}, u32[]{:S(2)}) copy-start(bf16[256,1024]{1,0:T(8,128)(2,1)S(1)} %slice.78.refs_0_) | copy-start | bytes 1572868
  87.3 14.1 %all-to-all-start.2 = ((bf16[4,512,128]{2,1,0:T(8,128)(2,1)}), bf16[4,512,128]{2,1,0:T(8,128)(2,1)}, u32[]{:S(2)}, u32[]{:S(2)}) async-start(bf16[4,512,128]{2,1,0:T(8,128)(2,1)} %bitcast_bitcast_fusion), calls=%async_computation.2 | async-start | bytes 1048576 | tf_op jit(solution)/shard_map/all_to_all | solution.py:26
  92.1 32.9 %collective-permute-start.7 = (bf16[256,1024]{1,0:T(8,128)(2,1)S(1)}, bf16[256,1024]{1,0:T(8,128)(2,1)S(1)}, u32[]{:S(2)}, u32[]{:S(2)}) collective-permute-start(bf16[256,1024]{1,0:T(8,128)(2,1)S(1)} %slice.78.refs_0_), channel_id=1, source_target_pairs={{0,256},{128,384},{256,0},{384,128},{1,257},{129,385},{257,1},{385... | collective-permute-start | bytes 1572872 | tf_op jit(solution)/shard_map/ppermute | solution.py:22
  95.4 29.5 %collective-permute-start.6 = (bf16[256,1024]{1,0:T(8,128)(2,1)S(1)}, bf16[256,1024]{1,0:T(8,128)(2,1)S(1)}, u32[]{:S(2)}, u32[]{:S(2)}) collective-permute-start(bf16[256,1024]{1,0:T(8,128)(2,1)S(1)} %slice.78.refs_0_), channel_id=1, source_target_pairs={{0,384},{128,256},{256,128},{384,0},{1,385},{129,257},{257,129},{3... | collective-permute-start | bytes 1572872 | tf_op jit(solution)/shard_map/ppermute | solution.py:22
  99.4 25.5 %collective-permute-start.5 = (bf16[256,1024]{1,0:T(8,128)(2,1)S(1)}, bf16[256,1024]{1,0:T(8,128)(2,1)S(1)}, u32[]{:S(2)}, u32[]{:S(2)}) collective-permute-start(bf16[256,1024]{1,0:T(8,128)(2,1)S(1)} %slice.78.refs_0_), channel_id=1, source_target_pairs={{0,128},{128,0},{256,384},{384,256},{1,129},{129,1},{257,385},{385... | collective-permute-start | bytes 1572872 | tf_op jit(solution)/shard_map/ppermute | solution.py:22
  102.5 22.4 %collective-permute-start.4 = (bf16[256,256]{1,0:T(8,128)(2,1)S(1)}, bf16[256,256]{1,0:T(8,128)(2,1)S(1)}, u32[]{:S(2)}, u32[]{:S(2)}) collective-permute-start(bf16[256,256]{1,0:T(8,128)(2,1)S(1)} %pad_maximum_fusion.4), channel_id=1, source_target_pairs={{0,8},{8,0},{1,9},{9,1},{2,10},{10,2},{3,11},{11,3},{4,12},{12,4},... | collective-permute-start | bytes 393224 | tf_op jit(solution)/shard_map/ppermute | solution.py:22
  124.9 16.2 %copy-start.2 = (bf16[256,1024]{1,0:T(8,128)(2,1)}, bf16[256,1024]{1,0:T(8,128)(2,1)S(1)}, u32[]{:S(2)}) copy-start(bf16[256,1024]{1,0:T(8,128)(2,1)S(1)} %collective-permute-done.7.refs_3_) | copy-start | bytes 1572868
  125.0 16.2 %copy-start.4 = (bf16[256,1024]{1,0:T(8,128)(2,1)}, bf16[256,1024]{1,0:T(8,128)(2,1)S(1)}, u32[]{:S(2)}) copy-start(bf16[256,1024]{1,0:T(8,128)(2,1)S(1)} %collective-permute-done.6.refs_2_) | copy-start | bytes 1572868
  125.0 16.2 %copy-start.6 = (bf16[256,1024]{1,0:T(8,128)(2,1)}, bf16[256,1024]{1,0:T(8,128)(2,1)S(1)}, u32[]{:S(2)}) copy-start(bf16[256,1024]{1,0:T(8,128)(2,1)S(1)} %collective-permute-done.5.refs_1_) | copy-start | bytes 1572868
  141.2 10.0 %collective-permute-start.8 = (bf16[2048,256]{1,0:T(8,128)(2,1)}, bf16[2048,256]{1,0:T(8,128)(2,1)}, u32[]{:S(2)}, u32[]{:S(2)}) collective-permute-start(bf16[2048,256]{1,0:T(8,128)(2,1)} %bitcast.45), channel_id=1, source_target_pairs={{0,1},{1,0},{2,3},{3,2},{4,5},{5,4},{6,7},{7,6},{8,9},{9,8},{10,11... | collective-permute-start | bytes 3145736 | tf_op jit(solution)/shard_map/ppermute | solution.py:22
  144.3 1.0 copy-start.1
  145.4 1.0 copy-start.3
  147.5 1.0 copy-start.7
  151.1 1.8 copy-start.8
  165.7 10.5 %collective-permute-start.9 = (bf16[256,512]{1,0:T(8,128)(2,1)S(1)}, bf16[256,512]{1,0:T(8,128)(2,1)S(1)}, u32[]{:S(2)}, u32[]{:S(2)}) collective-permute-start(bf16[256,512]{1,0:T(8,128)(2,1)S(1)} %slice.124), channel_id=1, source_target_pairs={{0,16},{16,0},{32,48},{48,32},{64,80},{80,64},{96,112},{112,96},{1... | collective-permute-start | bytes 786440 | tf_op jit(solution)/shard_map/ppermute | solution.py:22
  176.3 9.8 %collective-permute-start.10 = (bf16[256,256]{1,0:T(8,128)(2,1)S(1)}, bf16[256,256]{1,0:T(8,128)(2,1)S(1)}, u32[]{:S(2)}, u32[]{:S(2)}) collective-permute-start(bf16[256,256]{1,0:T(8,128)(2,1)S(1)} %slice.125), channel_id=1, source_target_pairs={{0,32},{16,48},{32,0},{48,16},{64,96},{80,112},{96,64},{112,80},{1... | collective-permute-start | bytes 393224 | tf_op jit(solution)/shard_map/ppermute | solution.py:22
  186.1 11.9 %collective-permute-start.11 = (bf16[256,128]{1,0:T(8,128)(2,1)S(1)}, bf16[256,128]{1,0:T(8,128)(2,1)S(1)}, u32[]{:S(2)}, u32[]{:S(2)}) collective-permute-start(bf16[256,128]{1,0:T(8,128)(2,1)S(1)} %slice.127), channel_id=1, source_target_pairs={{0,64},{16,80},{32,96},{48,112},{64,0},{80,16},{96,32},{112,48},{1... | collective-permute-start | bytes 196616 | tf_op jit(solution)/shard_map/ppermute | solution.py:22
  198.4 3.8 %collective-permute-start.12 = (bf16[2048,128]{1,0:T(8,128)(2,1)S(1)}, bf16[2048,128]{1,0:T(8,128)(2,1)S(1)}, u32[]{:S(2)}, u32[]{:S(2)}) collective-permute-start(bf16[2048,128]{1,0:T(8,128)(2,1)S(1)} %convolution_convert_fusion), channel_id=1, source_target_pairs={{0,1},{1,0},{2,3},{3,2},{4,5},{5,4},{6,7},{7,6},{8,9},{9,8},{10,11... | collective-permute-start | bytes 1572872 | tf_op jit(solution)/shard_map/ppermute | solution.py:22
  214.9 17.6 %collective-permute-start.13 = (bf16[256,128]{1,0:T(8,128)(2,1)S(1)}, bf16[256,128]{1,0:T(8,128)(2,1)S(1)}, u32[]{:S(2)}, u32[]{:S(2)}) collective-permute-start(bf16[256,128]{1,0:T(8,128)(2,1)S(1)} %slice.126), channel_id=1, source_target_pairs={{0,8},{8,0},{1,9},{9,1},{2,10},{10,2},{3,11},{11,3},{4,12},{12,4},... | collective-permute-start | bytes 196616 | tf_op jit(solution)/shard_map/ppermute | solution.py:22
  (1 other events, 1.0 us)

commit v3 on v2

--- a/solution.py
+++ b/solution.py
@@ -64,45 +64,49 @@
     barrier = lax.optimization_barrier
 
     moment_new = beta_first * moment + (1.0 - beta_first) * grad.astype(F32)
-    line = jnp.concatenate(
-        [grad, moment_new.astype(BF16), left_basis[:, :cols], left_basis[:, cols:]], axis=0
-    )
-    line, basis = barrier((line, right_basis))
+    line = jnp.concatenate([grad, moment_new.astype(BF16)], axis=0)
+    line, basis, left = barrier((line, right_basis, left_basis))
 
     line = jnp.concatenate([line, swap(line, "zl", 4)], axis=1)
-    basis = lax.all_gather(basis, "zh")
-    line, basis = barrier((line, basis))
+    basis = lax.all_gather(lax.all_gather(basis, "zh"), "core", axis=1)
+    line, basis, left = barrier((line, basis, left))
 
     line = jnp.concatenate([line, swap(line, "zl", 2)], axis=1)
+    left = jnp.concatenate([left, swap(left, "zl", 4)], axis=0)
     basis = spread(basis, "y")
-    basis = basis.reshape(2, 2, 2, rows, cols).transpose(2, 0, 1, 3, 4)
-    basis = basis.reshape(4, 2, rows, cols)
-    line, basis = barrier((line, basis))
+    basis = basis.reshape(2, 2, 2, 2, rows, cols).transpose(2, 0, 1, 3, 4, 5)
+    basis = basis.reshape(4, 4, rows, cols)
+    line, basis, left = barrier((line, basis, left))
 
     line = jnp.concatenate([line, swap(line, "zl", 1)], axis=1)
+    left = jnp.concatenate([left, swap(left, "zl", 2)], axis=0)
     basis = exchange(basis, "x")
-    basis = [basis, swap(basis, "core", 1)]
-    index, moves = [], []
-    for oc in range(2):
-        for ox in range(4):
-            for y0 in range(2):
-                for half in range(2):
-                    owner = y0 * 4 + (core ^ oc) * 2 + half
-                    index.append(reversed_bits(owner ^ zl))
-                    moves.append((oc, (ox, y0), half, 0, ox))
-    right = place(
-        jnp.stack(index).astype(jnp.int32), basis, (8 * cols, 4 * cols), cols, moves, 4 * 2**20
+    index, other_index, moves = [], [], []
+    for block in range(4):
+        for half in range(2):
+            owner = block * 2 + half
+            for ox in range(4):
+                index.append(reversed_bits(owner ^ zl))
+                other_index.append((owner & 3) * 2 + ((owner ^ zl) >> 2))
+                moves.append((0, (ox, block), half, 0, ox))
+    shape = (8 * cols, 4 * cols)
+    right = place(jnp.stack(index).astype(jnp.int32), [basis], shape, cols, moves, 4 * 2**20)
+    right_back = place(
+        jnp.stack(other_index).astype(jnp.int32), [basis], shape, cols, moves, 4 * 2**20
     )
 
-    partial = jnp.dot(line[: 2 * rows], right, preferred_element_type=F32).astype(BF16)
-    left, partial = barrier((line[2 * rows :], partial))
+    partial = jnp.dot(line, right, preferred_element_type=F32).astype(BF16)
+    left, partial = barrier((left, partial))
+    left = jnp.concatenate([left, swap(left, "zl", 1)], axis=0)
     partial = partial.reshape(2 * rows, 4, cols).transpose(1, 0, 2)
     total = jnp.sum(exchange(partial, "x").astype(F32), axis=0).astype(BF16)
     rotated = jnp.concatenate([total[:rows], total[rows:]], axis=1)
+    left, rotated = barrier((left, rotated))
 
-    left = [left] + [swap(left, "x", k) for k in (1, 3, 2)]
+    left = [left] + [swap(left, "x", k) for k in (1, 3)]
     rotated = jnp.concatenate([rotated, swap(rotated, "zh", 1)], axis=0)
     rotated, *left = barrier((rotated, *left))
+    left.append(swap(left[0], "x", 2))
     index, moves = [], []
     for number, ox in enumerate((0, 1, 3, 2)):
         for p in range(8):
@@ -111,8 +115,9 @@
             place_of = ((((n & 1) ^ core) * 4 + ((n >> 1) & 3)) * 2 + ((n >> 3) ^ zh)) * 2
             for half in range(2):
                 index.append(place_of + (block & 1))
-                moves.append((number, (), half, p, half))
+                moves.append((number, (), p, half, half))
     rotated = spread(rotated, "y").reshape(8 * rows, 2 * cols)
+    rotated, *left = barrier((rotated, *left))
     left = place(
         jnp.stack(index).astype(jnp.int32), left, (32 * cols, 2 * cols), cols, moves, 8 * 2**20
     )
@@ -129,13 +134,15 @@
 
     normed = spread(normed, "x").transpose(1, 0, 2).reshape(rows, 4 * cols)
     spectral = lax.dot_general(
-        normed, right, (((1,), (1,)), ((), ())), preferred_element_type=F32
+        normed, right_back, (((1,), (1,)), ((), ())), preferred_element_type=F32
     )
-    for offset in (1, 2, 4):
-        half = spectral.shape[1] // 2
-        sent = swap(spectral[:, half:].astype(BF16), "zl", offset)
-        spectral = spectral[:, :half] + sent.astype(F32)
-    spectral = spectral.astype(BF16)
+    spectral = spectral.astype(BF16).reshape(rows, 4, 2 * cols).transpose(1, 0, 2)
+    spectral = lax.all_to_all(
+        spectral, "zl", 0, 0, tiled=True, axis_index_groups=[[0, 1, 2, 3], [4, 5, 6, 7]]
+    )
+    spectral = jnp.sum(spectral.astype(F32), axis=0)
+    sent = swap(spectral[:, cols:].astype(BF16), "zl", 4)
+    spectral = (spectral[:, :cols] + sent.astype(F32)).astype(BF16)
 
     kept = barrier(jnp.dot(left[: 8 * rows], spectral, preferred_element_type=F32))
     sent = jnp.dot(left[8 * rows :], spectral, preferred_element_type=F32).astype(BF16)

time: 235 us -> 241 us (1.026)
  starting transfers between devices: 67.4 us -> 90.4 us
  blocking collectives: 67.4 us -> 50.9 us
  waiting for transfers between devices: 76.1 us -> 70 us
  local copies, waits for them, and re-layouts: 7.5 us -> 10.7 us
    all_to_all x4 -> x1, blocking collectives: 52.1 us -> 14.1 us  [exchange(): return lax.all_to_all(blocks, axis, 0, 0, tiled=True)]
    all_to_all x0 -> x1, blocking collectives: none -> 20.7 us  [shards(): lax.all_to_all(spectral, 'zl', 0, 0, tiled=True, axis_index_groups=[[0, 1...]
    all_to_all x2 -> x5, starting transfers between devices: 9.23 us -> 23.7 us  [exchange(): return lax.all_to_all(blocks, axis, 0, 0, tiled=True)]
    ppermute x14, waiting for transfers between devices: 75.1 us -> 66.3 us  [swap(): return lax.ppermute(value, axis, [(i, i ^ offset) for i in range(size)])]
    ppermute x14, starting transfers between devices: 58.1 us -> 66.7 us  [swap(): return lax.ppermute(value, axis, [(i, i ^ offset) for i in range(size)])]
    all_to_all x2 -> x5, waiting for transfers between devices: 0.94 us -> 3.7 us  [exchange(): return lax.all_to_all(blocks, axis, 0, 0, tiled=True)]
    unnamed x19 -> x22, local copies, waits for them, and re-layouts: 4.27 us -> 5.17 us
    all_gather x1 -> x2, blocking collectives: 15.3 us -> 16.1 us  [shards(): basis = lax.all_gather(lax.all_gather(basis, 'zh'), 'core', axis=1)]
  transfers between devices with their start and end apart: 16 -> 19, of which waited for: 10 -> 11; matrix products, arithmetic and copies ran while one was open for 2% -> 0% of each run, Pallas kernels for 0% -> 1%
where the time goes in v3:
time: 241 us; the launch traced here: 238 us
  starting transfers between devices  90.4 us (38%)
  waiting for transfers between devices  70 us (29%)
  blocking collectives  50.9 us (21%)
  local copies, waits for them, and re-layouts  10.7 us (4%)
  matrix products  6.7 us (3%)
  other arithmetic  4.32 us (2%)
    ppermute x14, starting transfers between devices, swap(): return lax.ppermute(value, axis, [(i, i ^ offset) for i in range(size)])  66.7 us
    ppermute x14, waiting for transfers between devices, swap(): return lax.ppermute(value, axis, [(i, i ^ offset) for i in range(size)])  66.3 us
    all_to_all x5, starting transfers between devices, exchange(): return lax.all_to_all(blocks, axis, 0, 0, tiled=True)  23.7 us
    all_to_all x1, blocking collectives, shards(): lax.all_to_all(spectral, 'zl', 0, 0, tiled=True, axis_index_groups=[[0, 1...  20.7 us
    all_gather x2, blocking collectives, shards(): basis = lax.all_gather(lax.all_gather(basis, 'zh'), 'core', axis=1)  16.1 us
    all_to_all x1, blocking collectives, exchange(): return lax.all_to_all(blocks, axis, 0, 0, tiled=True)  14.1 us
    unnamed x22, local copies, waits for them, and re-layouts  5.17 us
  transfers between devices with their start and end apart: 19, of which 11 were waited for; matrix products, arithmetic and copies ran while one was open for 0% of the time, Pallas kernels for 1%

profile of v3, /device:TPU:6, one launch (start us, length us, event | category | flops | bytes accessed | tf_op | source)
XLA Modules:
  0.0 237.6 jit_solution(17135909319058394688)
XLA Ops:
  3.1 9.1 %collective-permute-start = (bf16[512,128]{1,0:T(8,128)(2,1)S(1)}, bf16[512,128]{1,0:T(8,128)(2,1)S(1)}, u32[]{:S(2)}, u32[]{:S(2)}) collective-permute-start(bf16[512,128]{1,0:T(8,128)(2,1)S(1)} %pad_maximum_fusion.5), channel_id=1, source_target_pairs={{0,64},{16,80},{32,96},{48,112},{64,0},{80,16},{96,32},{112,48},{1... | collective-permute-start | bytes 393224 | tf_op jit(solution)/shard_map/ppermute | solution.py:22
  12.2 14.0 %all-gather = bf16[512,128]{1,0:T(8,128)(2,1)S(1)} all-gather(bf16[256,128]{1,0:T(8,128)(2,1)} %param.9), channel_id=2, replica_groups=mesh['x'=4,'zl'=8,'zh'=2,'y'=4,'core'=2] {'zh'}, dimensions={0}, use_global_device_ids=true | all-gather | bytes 196608 | tf_op jit(solution)/shard_map/all_gather | solution.py:71
  29.5 4.5 %all-to-all-start = ((bf16[4,2,2,256,128]{4,3,2,1,0:T(8,128)(2,1)}), bf16[4,2,2,256,128]{4,3,2,1,0:T(8,128)(2,1)S(1)}, u32[]{:S(2)}, u32[]{:S(2)}) async-start(bf16[4,2,2,256,128]{4,3,2,1,0:T(8,128)(2,1)} %broadcast_in_dim.6), calls=%async_computation | async-start | bytes 2097152 | tf_op jit(solution)/shard_map/all_to_all | solution.py:26
  34.0 12.9 %collective-permute-start.1 = (bf16[512,256]{1,0:T(8,128)(2,1)S(1)}, bf16[512,256]{1,0:T(8,128)(2,1)S(1)}, u32[]{:S(2)}, u32[]{:S(2)}) collective-permute-start(bf16[512,256]{1,0:T(8,128)(2,1)S(1)} %pad_maximum_fusion.2), channel_id=1, source_target_pairs={{0,32},{16,48},{32,0},{48,16},{64,96},{80,112},{96,64},{112,80},{1... | collective-permute-start | bytes 786440 | tf_op jit(solution)/shard_map/ppermute | solution.py:22
  48.9 8.3 %collective-permute-done.2 = bf16[128,256]{1,0:T(8,128)(2,1)S(1)} collective-permute-done((bf16[128,256]{1,0:T(8,128)(2,1)S(1)}, bf16[128,256]{1,0:T(8,128)(2,1)S(1)}, u32[]{:S(2)}, u32[]{:S(2)}) %collective-permute-start.2) | collective-permute-done | bytes 65568 | tf_op jit(solution)/shard_map/ppermute | solution.py:22
  60.4 4.8 %all-to-all-start.1 = ((bf16[4,4,256,128]{3,2,1,0:T(8,128)(2,1)}), bf16[4,4,256,128]{3,2,1,0:T(8,128)(2,1)S(1)}, u32[]{:S(2)}, u32[]{:S(2)}) async-start(bf16[4,4,256,128]{3,2,1,0:T(8,128)(2,1)} %bitcast.36), calls=%async_computation.1 | async-start | bytes 2097152 | tf_op jit(solution)/shard_map/all_to_all | solution.py:26
  67.1 4.4 %collective-permute-start.3 = (bf16[256,256]{1,0:T(8,128)(2,1)S(1)}, bf16[256,256]{1,0:T(8,128)(2,1)S(1)}, u32[]{:S(2)}, u32[]{:S(2)}) collective-permute-start(bf16[256,256]{1,0:T(8,128)(2,1)S(1)} %pad_maximum_fusion.6), channel_id=1, source_target_pairs={{0,32},{16,48},{32,0},{48,16},{64,96},{80,112},{96,64},{112,80},{1... | collective-permute-start | bytes 393224 | tf_op jit(solution)/shard_map/ppermute | solution.py:22
  71.7 9.3 %collective-permute-done.3 = bf16[256,256]{1,0:T(8,128)(2,1)S(1)} collective-permute-done((bf16[256,256]{1,0:T(8,128)(2,1)S(1)}, bf16[256,256]{1,0:T(8,128)(2,1)S(1)}, u32[]{:S(2)}, u32[]{:S(2)}) %collective-permute-start.3) | collective-permute-done | bytes 131104 | tf_op jit(solution)/shard_map/ppermute | solution.py:22
  84.8 4.8 %all-to-all-start.2 = ((bf16[4,512,128]{2,1,0:T(8,128)(2,1)}), bf16[4,512,128]{2,1,0:T(8,128)(2,1)S(1)}, u32[]{:S(2)}, u32[]{:S(2)}) async-start(bf16[4,512,128]{2,1,0:T(8,128)(2,1)} %bitcast_bitcast_fusion.1), calls=%async_computation.2 | async-start | bytes 1048576 | tf_op jit(solution)/shard_map/all_to_all | solution.py:26
  89.5 4.7 %collective-permute-start.5 = (bf16[512,256]{1,0:T(8,128)(2,1)S(1)}, bf16[512,256]{1,0:T(8,128)(2,1)S(1)}, u32[]{:S(2)}, u32[]{:S(2)}) collective-permute-start(bf16[512,256]{1,0:T(8,128)(2,1)S(1)} %pad_maximum_fusion.3), channel_id=1, source_target_pairs={{0,16},{16,0},{32,48},{48,32},{64,80},{80,64},{96,112},{112,96},{1... | collective-permute-start | bytes 786440 | tf_op jit(solution)/shard_map/ppermute | solution.py:22
  94.3 4.3 %collective-permute-done.5 = bf16[512,256]{1,0:T(8,128)(2,1)S(1)} collective-permute-done((bf16[512,256]{1,0:T(8,128)(2,1)S(1)}, bf16[512,256]{1,0:T(8,128)(2,1)S(1)}, u32[]{:S(2)}, u32[]{:S(2)}) %collective-permute-start.5) | collective-permute-done | bytes 262176 | tf_op jit(solution)/shard_map/ppermute | solution.py:22
  100.7 3.3 %collective-permute-start.7 = (bf16[1024,256]{1,0:T(8,128)(2,1)S(1)}, bf16[1024,256]{1,0:T(8,128)(2,1)S(1)}, u32[]{:S(2)}, u32[]{:S(2)}) collective-permute-start(bf16[1024,256]{1,0:T(8,128)(2,1)S(1)} %pad_maximum_fusion.1.refs_0_), channel_id=1, source_target_pairs={{0,128},{128,0},{256,384},{384,256},{1,129},{129,1},{257,385},{385... | collective-permute-start | bytes 1572872 | tf_op jit(solution)/shard_map/ppermute | solution.py:22
  104.0 9.3 %collective-permute-start.6 = (bf16[256,256]{1,0:T(8,128)(2,1)S(1)}, bf16[256,256]{1,0:T(8,128)(2,1)S(1)}, u32[]{:S(2)}, u32[]{:S(2)}) collective-permute-start(bf16[256,256]{1,0:T(8,128)(2,1)S(1)} %pad_maximum_fusion.7), channel_id=1, source_target_pairs={{0,8},{8,0},{1,9},{9,1},{2,10},{10,2},{3,11},{11,3},{4,12},{12,4},... | collective-permute-start | bytes 393224 | tf_op jit(solution)/shard_map/ppermute | solution.py:22
  113.3 10.9 %collective-permute-done.6 = bf16[256,256]{1,0:T(8,128)(2,1)S(1)} collective-permute-done((bf16[256,256]{1,0:T(8,128)(2,1)S(1)}, bf16[256,256]{1,0:T(8,128)(2,1)S(1)}, u32[]{:S(2)}, u32[]{:S(2)}) %collective-permute-start.6) | collective-permute-done | bytes 131104 | tf_op jit(solution)/shard_map/ppermute | solution.py:22
  125.5 4.2 %all-to-all-start.3 = ((bf16[4,512,256]{2,1,0:T(8,128)(2,1)}), bf16[4,512,256]{2,1,0:T(8,128)(2,1)}, u32[]{:S(2)}, u32[]{:S(2)}) async-start(bf16[4,512,256]{2,1,0:T(8,128)(2,1)} %broadcast_in_dim.7), calls=%async_computation.3 | async-start | bytes 2097152 | tf_op jit(solution)/shard_map/all_to_all | solution.py:26
  129.7 4.7 %collective-permute-start.9 = (bf16[1024,256]{1,0:T(8,128)(2,1)S(1)}, bf16[1024,256]{1,0:T(8,128)(2,1)S(1)}, u32[]{:S(2)}, u32[]{:S(2)}) collective-permute-start(bf16[1024,256]{1,0:T(8,128)(2,1)S(1)} %pad_maximum_fusion.1.refs_0_), channel_id=1, source_target_pairs={{0,256},{128,384},{256,0},{384,128},{1,257},{129,385},{257,1},{385... | collective-permute-start | bytes 1572872 | tf_op jit(solution)/shard_map/ppermute | solution.py:22
  134.5 7.8 %collective-permute-done.9.refs_3_ = bf16[1024,256]{1,0:T(8,128)(2,1)S(1)} collective-permute-done((bf16[1024,256]{1,0:T(8,128)(2,1)S(1)}, bf16[1024,256]{1,0:T(8,128)(2,1)S(1)}, u32[]{:S(2)}, u32[]{:S(2)}) %collective-permute-start.9) | collective-permute-done | bytes 524320 | tf_op jit(solution)/shard_map/ppermute | solution.py:22
  155.6 5.4 %all-to-all-start.4 = ((bf16[4,256,128]{1,2,0:T(8,128)(2,1)}), bf16[4,256,128]{1,2,0:T(8,128)(2,1)S(1)}, u32[]{:S(2)}, u32[]{:S(2)}) async-start(bf16[4,256,128]{1,2,0:T(8,128)(2,1)} %broadcast_in_dim.8), calls=%async_computation.4 | async-start | bytes 524288 | tf_op jit(solution)/shard_map/all_to_all | solution.py:26
  162.9 3.7 %all-to-all-done.4 = bf16[4,256,128]{1,2,0:T(8,128)(2,1)S(1)} async-done(((bf16[4,256,128]{1,2,0:T(8,128)(2,1)}), bf16[4,256,128]{1,2,0:T(8,128)(2,1)S(1)}, u32[]{:S(2)}, u32[]{:S(2)}) %all-to-all-start.4) | async-done | bytes 262176 | tf_op jit(solution)/shard_map/all_to_all | solution.py:26
  168.3 20.7 %all_to_all.35 = bf16[4,256,256]{2,1,0:T(8,128)(2,1)S(1)} all-to-all(bf16[4,256,256]{2,1,0:T(8,128)(2,1)S(1)} %bitcast.80), channel_id=1, replica_groups={{0,16,32,48},{64,80,96,112},{1,17,33,49},{65,81,97,113},{2,18,34,50},{6..., dimensions={0} | all-to-all | bytes 1048576 | tf_op jit(solution)/shard_map/all_to_all | solution.py:140
  191.0 10.2 %collective-permute-done.11 = bf16[256,128]{1,0:T(8,128)(2,1)S(1)} collective-permute-done((bf16[256,128]{1,0:T(8,128)(2,1)S(1)}, bf16[256,128]{1,0:T(8,128)(2,1)S(1)}, u32[]{:S(2)}, u32[]{:S(2)}) %collective-permute-start.11) | collective-permute-done | bytes 65568 | tf_op jit(solution)/shard_map/ppermute | solution.py:22
  205.6 14.1 %all_to_all.36 = bf16[4,512,128]{2,1,0:T(8,128)(2,1)S(1)} all-to-all(bf16[4,512,128]{2,1,0:T(8,128)(2,1)S(1)} %bitcast.81), channel_id=1, replica_groups=mesh['x'=4,'zl'=8,'zh'=2,'y'=4,'core'=2] {'y'}, dimensions={0} | all-to-all | bytes 1048576 | tf_op jit(solution)/shard_map/all_to_all | solution.py:26
  219.8 6.7 %collective-permute-start.13 = (bf16[256,128]{1,0:T(8,128)(2,1)S(1)}, bf16[256,128]{1,0:T(8,128)(2,1)S(1)}, u32[]{:S(2)}, u32[]{:S(2)}) collective-permute-start(bf16[256,128]{1,0:T(8,128)(2,1)S(1)} %slice.78), channel_id=1, source_target_pairs={{0,8},{8,0},{1,9},{9,1},{2,10},{10,2},{3,11},{11,3},{4,12},{12,4},... | collective-permute-start | bytes 196616 | tf_op jit(solution)/shard_map/ppermute | solution.py:22
  226.5 10.4 %collective-permute-done.13 = bf16[256,128]{1,0:T(8,128)(2,1)S(1)} collective-permute-done((bf16[256,128]{1,0:T(8,128)(2,1)S(1)}, bf16[256,128]{1,0:T(8,128)(2,1)S(1)}, u32[]{:S(2)}, u32[]{:S(2)}) %collective-permute-start.13) | collective-permute-done | bytes 65568 | tf_op jit(solution)/shard_map/ppermute | solution.py:22
  (77 shorter events, 42.7 us)
Async XLA Ops:
  3.1 25.2 %collective-permute-start = (bf16[512,128]{1,0:T(8,128)(2,1)S(1)}, bf16[512,128]{1,0:T(8,128)(2,1)S(1)}, u32[]{:S(2)}, u32[]{:S(2)}) collective-permute-start(bf16[512,128]{1,0:T(8,128)(2,1)S(1)} %pad_maximum_fusion.5), channel_id=1, source_target_pairs={{0,64},{16,80},{32,96},{48,112},{64,0},{80,16},{96,32},{112,48},{1... | collective-permute-start | bytes 393224 | tf_op jit(solution)/shard_map/ppermute | solution.py:22
  26.2 20.7 %copy-start.10 = (bf16[128,256]{1,0:T(8,128)(2,1)S(1)}, bf16[128,256]{1,0:T(8,128)(2,1)}, u32[]{:S(2)}) copy-start(bf16[128,256]{1,0:T(8,128)(2,1)} %param.8) | copy-start | bytes 196612
  29.5 29.8 %all-to-all-start = ((bf16[4,2,2,256,128]{4,3,2,1,0:T(8,128)(2,1)}), bf16[4,2,2,256,128]{4,3,2,1,0:T(8,128)(2,1)S(1)}, u32[]{:S(2)}, u32[]{:S(2)}) async-start(bf16[4,2,2,256,128]{4,3,2,1,0:T(8,128)(2,1)} %broadcast_in_dim.6), calls=%async_computation | async-start | bytes 2097152 | tf_op jit(solution)/shard_map/all_to_all | solution.py:26
  34.0 25.3 %collective-permute-start.1 = (bf16[512,256]{1,0:T(8,128)(2,1)S(1)}, bf16[512,256]{1,0:T(8,128)(2,1)S(1)}, u32[]{:S(2)}, u32[]{:S(2)}) collective-permute-start(bf16[512,256]{1,0:T(8,128)(2,1)S(1)} %pad_maximum_fusion.2), channel_id=1, source_target_pairs={{0,32},{16,48},{32,0},{48,16},{64,96},{80,112},{96,64},{112,80},{1... | collective-permute-start | bytes 786440 | tf_op jit(solution)/shard_map/ppermute | solution.py:22
  46.9 10.2 %collective-permute-start.2 = (bf16[128,256]{1,0:T(8,128)(2,1)S(1)}, bf16[128,256]{1,0:T(8,128)(2,1)S(1)}, u32[]{:S(2)}, u32[]{:S(2)}) collective-permute-start(bf16[128,256]{1,0:T(8,128)(2,1)S(1)} %copy-done.10), channel_id=1, source_target_pairs={{0,64},{16,80},{32,96},{48,112},{64,0},{80,16},{96,32},{112,48},{1... | collective-permute-start | bytes 196616 | tf_op jit(solution)/shard_map/ppermute | solution.py:22
  60.4 20.6 %all-to-all-start.1 = ((bf16[4,4,256,128]{3,2,1,0:T(8,128)(2,1)}), bf16[4,4,256,128]{3,2,1,0:T(8,128)(2,1)S(1)}, u32[]{:S(2)}, u32[]{:S(2)}) async-start(bf16[4,4,256,128]{3,2,1,0:T(8,128)(2,1)} %bitcast.36), calls=%async_computation.1 | async-start | bytes 2097152 | tf_op jit(solution)/shard_map/all_to_all | solution.py:26
  65.1 18.0 %collective-permute-start.4 = (bf16[512,512]{1,0:T(8,128)(2,1)S(1)}, bf16[512,512]{1,0:T(8,128)(2,1)S(1)}, u32[]{:S(2)}, u32[]{:S(2)}) collective-permute-start(bf16[512,512]{1,0:T(8,128)(2,1)S(1)} %pad_maximum_fusion), channel_id=1, source_target_pairs={{0,16},{16,0},{32,48},{48,32},{64,80},{80,64},{96,112},{112,96},{1... | collective-permute-start | bytes 1572872 | tf_op jit(solution)/shard_map/ppermute | solution.py:22
  67.1 13.9 %collective-permute-start.3 = (bf16[256,256]{1,0:T(8,128)(2,1)S(1)}, bf16[256,256]{1,0:T(8,128)(2,1)S(1)}, u32[]{:S(2)}, u32[]{:S(2)}) collective-permute-start(bf16[256,256]{1,0:T(8,128)(2,1)S(1)} %pad_maximum_fusion.6), channel_id=1, source_target_pairs={{0,32},{16,48},{32,0},{48,16},{64,96},{80,112},{96,64},{112,80},{1... | collective-permute-start | bytes 393224 | tf_op jit(solution)/shard_map/ppermute | solution.py:22
  84.8 13.9 %all-to-all-start.2 = ((bf16[4,512,128]{2,1,0:T(8,128)(2,1)}), bf16[4,512,128]{2,1,0:T(8,128)(2,1)S(1)}, u32[]{:S(2)}, u32[]{:S(2)}) async-start(bf16[4,512,128]{2,1,0:T(8,128)(2,1)} %bitcast_bitcast_fusion.1), calls=%async_computation.2 | async-start | bytes 1048576 | tf_op jit(solution)/shard_map/all_to_all | solution.py:26
  89.5 9.0 %collective-permute-start.5 = (bf16[512,256]{1,0:T(8,128)(2,1)S(1)}, bf16[512,256]{1,0:T(8,128)(2,1)S(1)}, u32[]{:S(2)}, u32[]{:S(2)}) collective-permute-start(bf16[512,256]{1,0:T(8,128)(2,1)S(1)} %pad_maximum_fusion.3), channel_id=1, source_target_pairs={{0,16},{16,0},{32,48},{48,32},{64,80},{80,64},{96,112},{112,96},{1... | collective-permute-start | bytes 786440 | tf_op jit(solution)/shard_map/ppermute | solution.py:22
  98.6 31.1 %copy-start.1 = (bf16[1024,256]{1,0:T(8,128)(2,1)}, bf16[1024,256]{1,0:T(8,128)(2,1)S(1)}, u32[]{:S(2)}) copy-start(bf16[1024,256]{1,0:T(8,128)(2,1)S(1)} %pad_maximum_fusion.1.refs_0_) | copy-start | bytes 1572868
  98.8 25.5 %collective-permute-start.8 = (bf16[1024,256]{1,0:T(8,128)(2,1)S(1)}, bf16[1024,256]{1,0:T(8,128)(2,1)S(1)}, u32[]{:S(2)}, u32[]{:S(2)}) collective-permute-start(bf16[1024,256]{1,0:T(8,128)(2,1)S(1)} %pad_maximum_fusion.1.refs_0_), channel_id=1, source_target_pairs={{0,384},{128,256},{256,128},{384,0},{1,385},{129,257},{257,129},{3... | collective-permute-start | bytes 1572872 | tf_op jit(solution)/shard_map/ppermute | solution.py:22
  100.7 23.6 %collective-permute-start.7 = (bf16[1024,256]{1,0:T(8,128)(2,1)S(1)}, bf16[1024,256]{1,0:T(8,128)(2,1)S(1)}, u32[]{:S(2)}, u32[]{:S(2)}) collective-permute-start(bf16[1024,256]{1,0:T(8,128)(2,1)S(1)} %pad_maximum_fusion.1.refs_0_), channel_id=1, source_target_pairs={{0,128},{128,0},{256,384},{384,256},{1,129},{129,1},{257,385},{385... | collective-permute-start | bytes 1572872 | tf_op jit(solution)/shard_map/ppermute | solution.py:22
  104.0 20.2 %collective-permute-start.6 = (bf16[256,256]{1,0:T(8,128)(2,1)S(1)}, bf16[256,256]{1,0:T(8,128)(2,1)S(1)}, u32[]{:S(2)}, u32[]{:S(2)}) collective-permute-start(bf16[256,256]{1,0:T(8,128)(2,1)S(1)} %pad_maximum_fusion.7), channel_id=1, source_target_pairs={{0,8},{8,0},{1,9},{9,1},{2,10},{10,2},{3,11},{11,3},{4,12},{12,4},... | collective-permute-start | bytes 393224 | tf_op jit(solution)/shard_map/ppermute | solution.py:22
  124.3 20.4 %copy-start.3 = (bf16[1024,256]{1,0:T(8,128)(2,1)}, bf16[1024,256]{1,0:T(8,128)(2,1)S(1)}, u32[]{:S(2)}) copy-start(bf16[1024,256]{1,0:T(8,128)(2,1)S(1)} %collective-permute-done.8.refs_2_) | copy-start | bytes 1572868
  124.3 20.4 %copy-start.5 = (bf16[1024,256]{1,0:T(8,128)(2,1)}, bf16[1024,256]{1,0:T(8,128)(2,1)S(1)}, u32[]{:S(2)}) copy-start(bf16[1024,256]{1,0:T(8,128)(2,1)S(1)} %collective-permute-done.7.refs_1_) | copy-start | bytes 1572868
  125.5 16.8 %all-to-all-start.3 = ((bf16[4,512,256]{2,1,0:T(8,128)(2,1)}), bf16[4,512,256]{2,1,0:T(8,128)(2,1)}, u32[]{:S(2)}, u32[]{:S(2)}) async-start(bf16[4,512,256]{2,1,0:T(8,128)(2,1)} %broadcast_in_dim.7), calls=%async_computation.3 | async-start | bytes 2097152 | tf_op jit(solution)/shard_map/all_to_all | solution.py:26
  129.7 12.6 %collective-permute-start.9 = (bf16[1024,256]{1,0:T(8,128)(2,1)S(1)}, bf16[1024,256]{1,0:T(8,128)(2,1)S(1)}, u32[]{:S(2)}, u32[]{:S(2)}) collective-permute-start(bf16[1024,256]{1,0:T(8,128)(2,1)S(1)} %pad_maximum_fusion.1.refs_0_), channel_id=1, source_target_pairs={{0,256},{128,384},{256,0},{384,128},{1,257},{129,385},{257,1},{385... | collective-permute-start | bytes 1572872 | tf_op jit(solution)/shard_map/ppermute | solution.py:22
  142.3 8.3 %collective-permute-start.10 = (bf16[2048,256]{1,0:T(8,128)(2,1)}, bf16[2048,256]{1,0:T(8,128)(2,1)}, u32[]{:S(2)}, u32[]{:S(2)}) collective-permute-start(bf16[2048,256]{1,0:T(8,128)(2,1)} %bitcast.46), channel_id=1, source_target_pairs={{0,1},{1,0},{2,3},{3,2},{4,5},{5,4},{6,7},{7,6},{8,9},{9,8},{10,11... | collective-permute-start | bytes 3145736 | tf_op jit(solution)/shard_map/ppermute | solution.py:22
  150.6 3.5 %copy-start.9 = (f32[256,128]{1,0:T(8,128)S(1)}, f32[256,128]{1,0:T(8,128)}, u32[]{:S(2)}) copy-start(f32[256,128]{1,0:T(8,128)} %param.7) | copy-start | bytes 393220
  155.6 11.0 %all-to-all-start.4 = ((bf16[4,256,128]{1,2,0:T(8,128)(2,1)}), bf16[4,256,128]{1,2,0:T(8,128)(2,1)S(1)}, u32[]{:S(2)}, u32[]{:S(2)}) async-start(bf16[4,256,128]{1,2,0:T(8,128)(2,1)} %broadcast_in_dim.8), calls=%async_computation.4 | async-start | bytes 524288 | tf_op jit(solution)/shard_map/all_to_all | solution.py:26
  189.1 12.2 %collective-permute-start.11 = (bf16[256,128]{1,0:T(8,128)(2,1)S(1)}, bf16[256,128]{1,0:T(8,128)(2,1)S(1)}, u32[]{:S(2)}, u32[]{:S(2)}) collective-permute-start(bf16[256,128]{1,0:T(8,128)(2,1)S(1)} %slice.79), channel_id=1, source_target_pairs={{0,64},{16,80},{32,96},{48,112},{64,0},{80,16},{96,32},{112,48},{1... | collective-permute-start | bytes 196616 | tf_op jit(solution)/shard_map/ppermute | solution.py:22
  201.7 3.8 %collective-permute-start.12 = (bf16[2048,128]{1,0:T(8,128)(2,1)S(1)}, bf16[2048,128]{1,0:T(8,128)(2,1)S(1)}, u32[]{:S(2)}, u32[]{:S(2)}) collective-permute-start(bf16[2048,128]{1,0:T(8,128)(2,1)S(1)} %convolution_convert_fusion), channel_id=1, source_target_pairs={{0,1},{1,0},{2,3},{3,2},{4,5},{5,4},{6,7},{7,6},{8,9},{9,8},{10,11... | collective-permute-start | bytes 1572872 | tf_op jit(solution)/shard_map/ppermute | solution.py:22
  219.8 17.1 %collective-permute-start.13 = (bf16[256,128]{1,0:T(8,128)(2,1)S(1)}, bf16[256,128]{1,0:T(8,128)(2,1)S(1)}, u32[]{:S(2)}, u32[]{:S(2)}) collective-permute-start(bf16[256,128]{1,0:T(8,128)(2,1)S(1)} %slice.78), channel_id=1, source_target_pairs={{0,8},{8,0},{1,9},{9,1},{2,10},{10,2},{3,11},{11,3},{4,12},{12,4},... | collective-permute-start | bytes 196616 | tf_op jit(solution)/shard_map/ppermute | solution.py:22
  (6 other events, 8.2 us)

commit v4 on v2

v4 whole, which is shorter than its diff:
```python
import jax
import jax.numpy as jnp
from jax import lax
from jax.experimental import pallas as pl
from jax.experimental.pallas import tpu as pltpu
from jax.experimental.layout import Layout, with_layout_constraint
from jax.sharding import Mesh, PartitionSpec as P

STEP = 10

beta_first = 0.95
beta_second = 0.95
epsilon = 1e-08

AXES = ("x", "z2", "z10", "zh", "y", "core")
SIZES = (4, 2, 4, 2, 4, 2)
BF16 = jnp.bfloat16
F32 = jnp.float32


def swap(value, axis, offset):
    size = dict(zip(AXES, SIZES))[axis]
    return lax.ppermute(value, axis, [(i, i ^ offset) for i in range(size)])


def exchange(blocks, axis):
    return lax.all_to_all(blocks, axis, 0, 0, tiled=True)


def spread(value, axis):
    return exchange(jnp.broadcast_to(value[None], (4,) + value.shape), axis)


def place(index, sources, shape, size, moves, vmem):
    def kernel(index_ref, *refs):
        out_ref = refs[-1]
        for n, (source, lead, row, col, out_col) in enumerate(moves):
            tile = refs[source][lead + (pl.ds(row * size, size), pl.ds(col * size, size))]
            to = pl.multiple_of(index_ref[n] * size, size)
            out_ref[pl.ds(to, size), out_col * size : (out_col + 1) * size] = tile

    in_vmem = pl.BlockSpec(memory_space=pltpu.VMEM)
    nbytes = 4 * shape[0] * shape[1]
    return pl.pallas_call(
        kernel,
        out_shape=jax.ShapeDtypeStruct(shape, BF16),
        in_specs=[pl.BlockSpec(memory_space=pltpu.SMEM)] + [in_vmem] * len(sources),
        out_specs=in_vmem,
        compiler_params=pltpu.CompilerParams(vmem_limit_bytes=vmem),
        cost_estimate=pl.CostEstimate(flops=0, bytes_accessed=nbytes, transcendentals=0),
    )(index, *sources)


OFFSETS = (0, 4, 2, 6, 1, 5, 3, 7)


def place_in_line(o):
    return ((o & 1) << 2) | (o & 2) | (o >> 2)


def shards(grad, moment, second, left_basis, right_basis):
    rows, cols = grad.shape
    x = lax.axis_index("x")
    z2 = lax.axis_index("z2")
    zl = z2 * 4 + lax.axis_index("z10")
    zh = lax.axis_index("zh")
    core = lax.axis_index("core")
    barrier = lax.optimization_barrier

    moment_new = beta_first * moment + (1.0 - beta_first) * grad.astype(F32)

    line = jnp.concatenate([grad, moment_new.astype(BF16), right_basis], axis=1)
    line = with_layout_constraint(line, Layout(major_to_minor=(0, 1)))
    line, left_basis = barrier((line, left_basis))
    left = jnp.concatenate([left_basis, swap(left_basis, "z2", 1)], axis=0)
    other = swap(line, "zh", 1)
    line = jnp.stack([jnp.where(zh == 0, line, other), jnp.where(zh == 0, other, line)])
    line, left = barrier((line, left))

    left = jnp.concatenate([left, swap(left, "z10", 2)], axis=0)
    left = jnp.concatenate([left, swap(left, "z10", 1)], axis=0)
    line = spread(line, "y")
    line, left = barrier((line, left))
    other = swap(line, "core", 1)

    basis = jnp.stack([line[..., 2 * cols :], other[..., 2 * cols :]])
    basis = basis.reshape(2, 2, 2, 2, rows, cols).transpose(3, 1, 0, 2, 4, 5)
    basis = basis.reshape(4, 4, rows, cols)
    basis = exchange(basis, "x")
    index, moves = [], []
    for block in range(4):
        for half in range(2):
            owner = (block % 2) * 4 + (core ^ (block // 2)) * 2 + half
            for ox in range(4):
                index.append(place_in_line(owner ^ zl))
                moves.append((0, (ox, block), half, 0, ox))
    index = jnp.stack(index).astype(jnp.int32)
    right = place(index, [basis], (8 * cols, 4 * cols), cols, moves, 4 * 2**20)

    lefts = [left] + [swap(left, "x", k) for k in (1, 3, 2)]
    index, moves = [], []
    for number, ox in enumerate((0, 1, 3, 2)):
        for p in range(8):
            block = (x ^ ox) * 8 + (zl ^ OFFSETS[p])
            n = block // 2
            to = ((((n & 1) ^ core) * 4 + ((n >> 1) & 3)) * 2 + (n >> 3)) * 2 + (block & 1)
            for half in range(2):
                index.append(to)
                moves.append((number, (), p, half, half))
    index = jnp.stack(index).astype(jnp.int32)
    left = place(index, lefts, (32 * cols, 2 * cols), cols, moves, 8 * 2**20)

    contract_rows = (((0,), (0,)), ((), ()))
    line = line[..., : 2 * cols].reshape(8 * rows, 2 * cols)
    other = other[..., : 2 * cols].reshape(8 * rows, 2 * cols)
    pair = lax.dot_general(
        left[: 8 * rows], line, contract_rows, preferred_element_type=F32
    ) + lax.dot_general(left[8 * rows :], other, contract_rows, preferred_element_type=F32)
    pair = pair.astype(BF16)
    pair = jnp.concatenate([pair[:, :cols], pair[:, cols:]], axis=0)

    pair = jnp.concatenate([pair, swap(pair, "z2", 1)], axis=1)
    pair = jnp.concatenate([pair, swap(pair, "z10", 2)], axis=1)
    pair = jnp.concatenate([pair, swap(pair, "z10", 1)], axis=1)
    pair = jnp.dot(pair, right, preferred_element_type=F32).astype(BF16)
    pair = pair.reshape(2 * rows, 4, cols).transpose(1, 0, 2)
    pair = jnp.sum(exchange(pair, "x").astype(F32), axis=0)
    first, other = pair[:rows], pair[rows:]
    second_new = beta_second * second + (1.0 - beta_second) * first * first
    bias_first = 1.0 - beta_first**STEP
    bias_second = 1.0 - beta_second**STEP
    normed = (other / bias_first / (jnp.sqrt(second_new / bias_second) + epsilon)).astype(BF16)

    normed = spread(normed, "x").transpose(1, 0, 2).reshape(rows, 4 * cols)
    spectral = lax.dot_general(
        normed, right, (((1,), (1,)), ((), ())), preferred_element_type=F32
    )
    for offset in (1, 2):
        half = spectral.shape[1] // 2
        sent = swap(spectral[:, half:].astype(BF16), "z10", offset)
        spectral = spectral[:, :half] + sent.astype(F32)
    spectral = spectral.astype(BF16)
    mine, others = spectral[:, :cols], spectral[:, cols:]
    spectral = jnp.concatenate(
        [jnp.where(z2 == 0, mine, others), jnp.where(z2 == 0, others, mine)], axis=1
    )

    kept = barrier(jnp.dot(left[: 8 * rows], spectral, preferred_element_type=F32))
    sent = jnp.dot(left[8 * rows :], spectral, preferred_element_type=F32).astype(BF16)
    update = (kept + swap(sent, "core", 1).astype(F32)).astype(BF16)
    update = exchange(update.reshape(4, 2 * rows, 2 * cols), "y")
    update = jnp.sum(update.astype(F32), axis=0).astype(BF16)
    update = update.reshape(2, rows, 2, cols).transpose(0, 2, 1, 3).reshape(4, rows, cols)
    update = jnp.sum(exchange(update, ("zh", "z2")).astype(F32), axis=0)
    return (moment_new, second_new, update.astype(BF16))


def solution(mesh):
    fine = Mesh(mesh.devices.reshape(SIZES), AXES)
    spec = P(("zh", "y", "core"), ("x", "z2", "z10"))
    left_spec = P(("x", "z2", "z10"), ("zh", "y", "core"))
    return jax.shard_map(
        shards,
        mesh=fine,
        in_specs=(spec, spec, spec, left_spec, spec),
        out_specs=(spec, spec, spec),
        check_vma=False,
    )
```

time: 235 us -> 253 us (1.077)
  waiting for transfers between devices: 76.1 us -> 101 us
  starting transfers between devices: 67.4 us -> 56.8 us
  blocking collectives: 67.4 us -> 62.4 us
  local copies, waits for them, and re-layouts: 7.5 us -> 11.5 us
  other arithmetic: 5.39 us -> 9.2 us
    ppermute x14, waiting for transfers between devices: 75.1 us -> 97.1 us  [swap(): return lax.ppermute(value, axis, [(i, i ^ offset) for i in range(size)])]
    all_gather x1 -> x0, blocking collectives: 15.3 us -> none  [shards(): basis = lax.all_gather(basis, 'zh')]
    ppermute x14, starting transfers between devices: 58.1 us -> 47.6 us  [swap(): return lax.ppermute(value, axis, [(i, i ^ offset) for i in range(size)])]
    all_to_all x4, blocking collectives: 52.1 us -> 62.4 us  [exchange(): return lax.all_to_all(blocks, axis, 0, 0, tiled=True)]
    slice x7 -> x8, local copies, waits for them, and re-layouts: 0.9 us -> 4.83 us  [the longest x2 2.16 us: shards(): basis = jnp.stack([line[..., 2 * cols:], other[..., 2 * cols:]])]
    all_to_all x2, waiting for transfers between devices: 0.94 us -> 4.31 us  [exchange(): return lax.all_to_all(blocks, axis, 0, 0, tiled=True)]
    concatenate x5 -> x7, other arithmetic: 0.99 us -> 4.36 us  [the longest x1 1.81 us: shards(): pair = jnp.concatenate([pair, swap(pair, 'z10', 2)], axis=1)]
  transfers between devices with their start and end apart: 16 -> 16, of which waited for: 10 -> 13; matrix products, arithmetic and copies ran while one was open for 2% -> 3% of each run, Pallas kernels for 0% -> 1%
where the time goes in v4:
time: 253 us; the launch traced here: 249 us
  waiting for transfers between devices  101 us (40%)
  blocking collectives  62.4 us (25%)
  starting transfers between devices  56.8 us (22%)
  local copies, waits for them, and re-layouts  11.5 us (5%)
  other arithmetic  9.2 us (4%)
  matrix products  4.18 us (2%)
    ppermute x14, waiting for transfers between devices, swap(): return lax.ppermute(value, axis, [(i, i ^ offset) for i in range(size)])  97.1 us
    all_to_all x4, blocking collectives, exchange(): return lax.all_to_all(blocks, axis, 0, 0, tiled=True)  62.4 us
    ppermute x14, starting transfers between devices, swap(): return lax.ppermute(value, axis, [(i, i ^ offset) for i in range(size)])  47.6 us
    all_to_all x2, starting transfers between devices, exchange(): return lax.all_to_all(blocks, axis, 0, 0, tiled=True)  9.25 us
  transfers between devices with their start and end apart: 16, of which 13 were waited for; matrix products, arithmetic and copies ran while one was open for 3% of the time, Pallas kernels for 1%

profile of v4, /device:TPU:6, one launch (start us, length us, event | category | flops | bytes accessed | tf_op | source)
XLA Modules:
  0.0 249.3 jit_solution(12275964395048226701)
XLA Ops:
  3.2 15.7 %collective-permute-start = (bf16[256,384]{1,0:T(8,128)(2,1)S(1)}, bf16[256,384]{1,0:T(8,128)(2,1)S(1)}, u32[]{:S(2)}, u32[]{:S(2)}) collective-permute-start(bf16[256,384]{1,0:T(8,128)(2,1)S(1)} %pad_maximum_fusion.6), channel_id=1, source_target_pairs={{0,8},{8,0},{1,9},{9,1},{2,10},{10,2},{3,11},{11,3},{4,12},{12,4},... | collective-permute-start | bytes 589832 | tf_op jit(solution)/shard_map/ppermute | solution.py:23
  18.9 4.3 %collective-permute-start.1 = (bf16[128,256]{1,0:T(8,128)(2,1)}, bf16[128,256]{1,0:T(8,128)(2,1)S(1)}, u32[]{:S(2)}, u32[]{:S(2)}) collective-permute-start(bf16[128,256]{1,0:T(8,128)(2,1)} %param.8), channel_id=1, source_target_pairs={{0,64},{64,0},{1,65},{65,1},{2,66},{66,2},{3,67},{67,3},{4,68},{68... | collective-permute-start | bytes 196616 | tf_op jit(solution)/shard_map/ppermute | solution.py:23
  23.2 19.4 %collective-permute-done.1 = bf16[128,256]{1,0:T(8,128)(2,1)S(1)} collective-permute-done((bf16[128,256]{1,0:T(8,128)(2,1)}, bf16[128,256]{1,0:T(8,128)(2,1)S(1)}, u32[]{:S(2)}, u32[]{:S(2)}) %collective-permute-start.1) | collective-permute-done | bytes 65568 | tf_op jit(solution)/shard_map/ppermute | solution.py:23
  44.9 4.5 %all-to-all-start = ((bf16[4,2,256,384]{3,2,1,0:T(8,128)(2,1)}), bf16[4,2,256,384]{3,2,1,0:T(8,128)(2,1)}, u32[]{:S(2)}, u32[]{:S(2)}) async-start(bf16[4,2,256,384]{3,2,1,0:T(8,128)(2,1)} %broadcast_in_dim.4), calls=%async_computation | async-start | bytes 3145728 | tf_op jit(solution)/shard_map/all_to_all | solution.py:27
  51.2 7.6 %collective-permute-done.2 = bf16[256,256]{1,0:T(8,128)(2,1)S(1)} collective-permute-done((bf16[256,256]{1,0:T(8,128)(2,1)S(1)}, bf16[256,256]{1,0:T(8,128)(2,1)S(1)}, u32[]{:S(2)}, u32[]{:S(2)}) %collective-permute-start.2) | collective-permute-done | bytes 131104 | tf_op jit(solution)/shard_map/ppermute | solution.py:23
  60.8 8.3 %collective-permute-done.3 = bf16[512,256]{1,0:T(8,128)(2,1)S(1)} collective-permute-done((bf16[512,256]{1,0:T(8,128)(2,1)S(1)}, bf16[512,256]{1,0:T(8,128)(2,1)S(1)}, u32[]{:S(2)}, u32[]{:S(2)}) %collective-permute-start.3) | collective-permute-done | bytes 262176 | tf_op jit(solution)/shard_map/ppermute | solution.py:23
  72.4 3.3 %collective-permute-start.6 = (bf16[1024,256]{1,0:T(8,128)(2,1)S(1)}, bf16[1024,256]{1,0:T(8,128)(2,1)S(1)}, u32[]{:S(2)}, u32[]{:S(2)}) collective-permute-start(bf16[1024,256]{1,0:T(8,128)(2,1)S(1)} %pad_maximum_fusion.1.refs_0_), channel_id=1, source_target_pairs={{0,256},{128,384},{256,0},{384,128},{1,257},{129,385},{257,1},{385... | collective-permute-start | bytes 1572872 | tf_op jit(solution)/shard_map/ppermute | solution.py:23
  75.7 4.0 %collective-permute-start.5 = (bf16[1024,256]{1,0:T(8,128)(2,1)S(1)}, bf16[1024,256]{1,0:T(8,128)(2,1)S(1)}, u32[]{:S(2)}, u32[]{:S(2)}) collective-permute-start(bf16[1024,256]{1,0:T(8,128)(2,1)S(1)} %pad_maximum_fusion.1.refs_0_), channel_id=1, source_target_pairs={{0,384},{128,256},{256,128},{384,0},{1,385},{129,257},{257,129},{3... | collective-permute-start | bytes 1572872 | tf_op jit(solution)/shard_map/ppermute | solution.py:23
  84.1 6.4 %collective-permute-done.6.refs_3_ = bf16[1024,256]{1,0:T(8,128)(2,1)S(1)} collective-permute-done((bf16[1024,256]{1,0:T(8,128)(2,1)S(1)}, bf16[1024,256]{1,0:T(8,128)(2,1)S(1)}, u32[]{:S(2)}, u32[]{:S(2)}) %collective-permute-start.6) | collective-permute-done | bytes 524320 | tf_op jit(solution)/shard_map/ppermute | solution.py:23
  90.5 10.8 %collective-permute-done.5.refs_2_ = bf16[1024,256]{1,0:T(8,128)(2,1)S(1)} collective-permute-done((bf16[1024,256]{1,0:T(8,128)(2,1)S(1)}, bf16[1024,256]{1,0:T(8,128)(2,1)S(1)}, u32[]{:S(2)}, u32[]{:S(2)}) %collective-permute-start.5) | collective-permute-done | bytes 524320 | tf_op jit(solution)/shard_map/ppermute | solution.py:23
  108.2 2.4 collective-permute-start.8
  112.8 12.9 %collective-permute-done.8 = bf16[512,128]{1,0:T(8,128)(2,1)S(1)} collective-permute-done((bf16[512,128]{1,0:T(8,128)(2,1)S(1)}, bf16[512,128]{1,0:T(8,128)(2,1)S(1)}, u32[]{:S(2)}, u32[]{:S(2)}) %collective-permute-start.8) | collective-permute-done | bytes 131104 | tf_op jit(solution)/shard_map/ppermute | solution.py:23
  129.5 4.8 %all-to-all-start.1 = ((bf16[4,4,256,128]{3,2,1,0:T(8,128)(2,1)}), bf16[4,4,256,128]{3,2,1,0:T(8,128)(2,1)S(1)}, u32[]{:S(2)}, u32[]{:S(2)}) async-start(bf16[4,4,256,128]{3,2,1,0:T(8,128)(2,1)} %bitcast.65), calls=%async_computation.1 | async-start | bytes 2097152 | tf_op jit(solution)/shard_map/all_to_all | solution.py:27
  134.3 6.3 %collective-permute-done.9 = bf16[512,256]{1,0:T(8,128)(2,1)} collective-permute-done((bf16[512,256]{1,0:T(8,128)(2,1)}, bf16[512,256]{1,0:T(8,128)(2,1)}, u32[]{:S(2)}, u32[]{:S(2)}) %collective-permute-start.9) | collective-permute-done | bytes 262176 | tf_op jit(solution)/shard_map/ppermute | solution.py:23
  144.5 3.0 %all-to-all-done.1.refs_0_ = bf16[4,4,256,128]{3,2,1,0:T(8,128)(2,1)S(1)} async-done(((bf16[4,4,256,128]{3,2,1,0:T(8,128)(2,1)}), bf16[4,4,256,128]{3,2,1,0:T(8,128)(2,1)S(1)}, u32[]{:S(2)}, u32[]{:S(2)}) %all-to-all-start.1) | async-done | bytes 1048608 | tf_op jit(solution)/shard_map/all_to_all | solution.py:27
  148.2 10.2 %collective-permute-done.10 = bf16[512,512]{1,0:T(8,128)(2,1)} collective-permute-done((bf16[512,512]{1,0:T(8,128)(2,1)}, bf16[512,512]{1,0:T(8,128)(2,1)}, u32[]{:S(2)}, u32[]{:S(2)}) %collective-permute-start.10) | collective-permute-done | bytes 524320 | tf_op jit(solution)/shard_map/ppermute | solution.py:23
  160.3 11.5 %all_to_all.30 = bf16[4,512,128]{1,2,0:T(8,128)(2,1)S(1)} all-to-all(bf16[4,512,128]{1,2,0:T(8,128)(2,1)S(1)} %bitcast.74), channel_id=1, replica_groups=mesh['x'=4,'z2'=2,'z10'=4,'zh'=2,'y'=4,'core'=2] {'x'}, dimensions={0} | all-to-all | bytes 1048576 | tf_op jit(solution)/shard_map/all_to_all | solution.py:27
  173.9 9.1 %all_to_all.31 = bf16[4,256,128]{1,2,0:T(8,128)(2,1)S(1)} all-to-all(bf16[4,256,128]{1,2,0:T(8,128)(2,1)S(1)} %broadcast_in_dim.5), channel_id=1, replica_groups=mesh['x'=4,'z2'=2,'z10'=4,'zh'=2,'y'=4,'core'=2] {'x'}, dimensions={0} | all-to-all | bytes 524288 | tf_op jit(solution)/shard_map/all_to_all | solution.py:27
  183.5 2.5 %collective-permute-start.11 = (bf16[256,512]{1,0:T(8,128)(2,1)S(1)}, bf16[256,512]{1,0:T(8,128)(2,1)S(1)}, u32[]{:S(2)}, u32[]{:S(2)}) collective-permute-start(bf16[256,512]{1,0:T(8,128)(2,1)S(1)} %slice.100), channel_id=1, source_target_pairs={{0,16},{16,0},{32,48},{48,32},{1,17},{17,1},{33,49},{49,33},{2,18}... | collective-permute-start | bytes 786440 | tf_op jit(solution)/shard_map/ppermute | solution.py:23
  186.0 5.7 %collective-permute-done.11 = bf16[256,512]{1,0:T(8,128)(2,1)S(1)} collective-permute-done((bf16[256,512]{1,0:T(8,128)(2,1)S(1)}, bf16[256,512]{1,0:T(8,128)(2,1)S(1)}, u32[]{:S(2)}, u32[]{:S(2)}) %collective-permute-start.11) | collective-permute-done | bytes 262176 | tf_op jit(solution)/shard_map/ppermute | solution.py:23
  193.8 7.2 %collective-permute-done.12 = bf16[256,256]{1,0:T(8,128)(2,1)S(1)} collective-permute-done((bf16[256,256]{1,0:T(8,128)(2,1)S(1)}, bf16[256,256]{1,0:T(8,128)(2,1)S(1)}, u32[]{:S(2)}, u32[]{:S(2)}) %collective-permute-start.12) | collective-permute-done | bytes 131104 | tf_op jit(solution)/shard_map/ppermute | solution.py:23
  203.9 2.2 collective-permute-done.13
  206.4 19.7 %all_to_all.32 = bf16[4,512,256]{2,1,0:T(8,128)(2,1)S(1)} all-to-all(bf16[4,512,256]{2,1,0:T(8,128)(2,1)S(1)} %bitcast.68), channel_id=1, replica_groups=mesh['x'=4,'z2'=2,'z10'=4,'zh'=2,'y'=4,'core'=2] {'y'}, dimensions={0} | all-to-all | bytes 2097152 | tf_op jit(solution)/shard_map/all_to_all | solution.py:27
  226.5 22.2 %all_to_all.33 = bf16[4,256,128]{2,1,0:T(8,128)(2,1)S(1)} all-to-all(bf16[4,256,128]{2,1,0:T(8,128)(2,1)S(1)} %bitcast.73), channel_id=1, replica_groups=mesh['x'=4,'z2'=2,'z10'=4,'zh'=2,'y'=4,'core'=2] {'zh','z2'}, dimensions={0} | all-to-all | bytes 524288 | tf_op jit(solution)/shard_map/all_to_all | solution.py:27
  (69 shorter events, 43.1 us)
Async XLA Ops:
  3.2 40.3 %collective-permute-start = (bf16[256,384]{1,0:T(8,128)(2,1)S(1)}, bf16[256,384]{1,0:T(8,128)(2,1)S(1)}, u32[]{:S(2)}, u32[]{:S(2)}) collective-permute-start(bf16[256,384]{1,0:T(8,128)(2,1)S(1)} %pad_maximum_fusion.6), channel_id=1, source_target_pairs={{0,8},{8,0},{1,9},{9,1},{2,10},{10,2},{3,11},{11,3},{4,12},{12,4},... | collective-permute-start | bytes 589832 | tf_op jit(solution)/shard_map/ppermute | solution.py:23
  18.9 23.7 %collective-permute-start.1 = (bf16[128,256]{1,0:T(8,128)(2,1)}, bf16[128,256]{1,0:T(8,128)(2,1)S(1)}, u32[]{:S(2)}, u32[]{:S(2)}) collective-permute-start(bf16[128,256]{1,0:T(8,128)(2,1)} %param.8), channel_id=1, source_target_pairs={{0,64},{64,0},{1,65},{65,1},{2,66},{66,2},{3,67},{67,3},{4,68},{68... | collective-permute-start | bytes 196616 | tf_op jit(solution)/shard_map/ppermute | solution.py:23
  44.9 25.6 %all-to-all-start = ((bf16[4,2,256,384]{3,2,1,0:T(8,128)(2,1)}), bf16[4,2,256,384]{3,2,1,0:T(8,128)(2,1)}, u32[]{:S(2)}, u32[]{:S(2)}) async-start(bf16[4,2,256,384]{3,2,1,0:T(8,128)(2,1)} %broadcast_in_dim.4), calls=%async_computation | async-start | bytes 3145728 | tf_op jit(solution)/shard_map/all_to_all | solution.py:27
  49.3 9.6 %collective-permute-start.2 = (bf16[256,256]{1,0:T(8,128)(2,1)S(1)}, bf16[256,256]{1,0:T(8,128)(2,1)S(1)}, u32[]{:S(2)}, u32[]{:S(2)}) collective-permute-start(bf16[256,256]{1,0:T(8,128)(2,1)S(1)} %pad_maximum_fusion.7), channel_id=1, source_target_pairs={{0,32},{16,48},{32,0},{48,16},{1,33},{17,49},{33,1},{49,17},{2,34}... | collective-permute-start | bytes 393224 | tf_op jit(solution)/shard_map/ppermute | solution.py:23
  58.9 10.2 %collective-permute-start.3 = (bf16[512,256]{1,0:T(8,128)(2,1)S(1)}, bf16[512,256]{1,0:T(8,128)(2,1)S(1)}, u32[]{:S(2)}, u32[]{:S(2)}) collective-permute-start(bf16[512,256]{1,0:T(8,128)(2,1)S(1)} %pad_maximum_fusion.4), channel_id=1, source_target_pairs={{0,16},{16,0},{32,48},{48,32},{1,17},{17,1},{33,49},{49,33},{2,18}... | collective-permute-start | bytes 786440 | tf_op jit(solution)/shard_map/ppermute | solution.py:23
  70.4 35.5 %collective-permute-start.7 = (bf16[4,2,256,384]{3,2,1,0:T(8,128)(2,1)}, bf16[4,2,256,384]{3,2,1,0:T(8,128)(2,1)}, u32[]{:S(2)}, u32[]{:S(2)}) collective-permute-start(bf16[4,2,256,384]{3,2,1,0:T(8,128)(2,1)} %all-to-all-done), channel_id=1, source_target_pairs={{0,1},{1,0},{2,3},{3,2},{4,5},{5,4},{6,7},{7,6},{8,9},{9,8},{10,11... | collective-permute-start | bytes 4718600 | tf_op jit(solution)/shard_map/ppermute | solution.py:23
  72.4 18.2 %collective-permute-start.6 = (bf16[1024,256]{1,0:T(8,128)(2,1)S(1)}, bf16[1024,256]{1,0:T(8,128)(2,1)S(1)}, u32[]{:S(2)}, u32[]{:S(2)}) collective-permute-start(bf16[1024,256]{1,0:T(8,128)(2,1)S(1)} %pad_maximum_fusion.1.refs_0_), channel_id=1, source_target_pairs={{0,256},{128,384},{256,0},{384,128},{1,257},{129,385},{257,1},{385... | collective-permute-start | bytes 1572872 | tf_op jit(solution)/shard_map/ppermute | solution.py:23
  75.7 25.6 %collective-permute-start.5 = (bf16[1024,256]{1,0:T(8,128)(2,1)S(1)}, bf16[1024,256]{1,0:T(8,128)(2,1)S(1)}, u32[]{:S(2)}, u32[]{:S(2)}) collective-permute-start(bf16[1024,256]{1,0:T(8,128)(2,1)S(1)} %pad_maximum_fusion.1.refs_0_), channel_id=1, source_target_pairs={{0,384},{128,256},{256,128},{384,0},{1,385},{129,257},{257,129},{3... | collective-permute-start | bytes 1572872 | tf_op jit(solution)/shard_map/ppermute | solution.py:23
  79.7 22.4 %collective-permute-start.4 = (bf16[1024,256]{1,0:T(8,128)(2,1)S(1)}, bf16[1024,256]{1,0:T(8,128)(2,1)S(1)}, u32[]{:S(2)}, u32[]{:S(2)}) collective-permute-start(bf16[1024,256]{1,0:T(8,128)(2,1)S(1)} %pad_maximum_fusion.1.refs_0_), channel_id=1, source_target_pairs={{0,128},{128,0},{256,384},{384,256},{1,129},{129,1},{257,385},{385... | collective-permute-start | bytes 1572872 | tf_op jit(solution)/shard_map/ppermute | solution.py:23
  101.3 0.8 copy-start.2
  102.1 0.8 copy-start.4
  102.9 1.0 copy-start.3
  103.9 1.0 copy-start.5
  108.2 17.5 %collective-permute-start.8 = (bf16[512,128]{1,0:T(8,128)(2,1)S(1)}, bf16[512,128]{1,0:T(8,128)(2,1)S(1)}, u32[]{:S(2)}, u32[]{:S(2)}) collective-permute-start(bf16[512,128]{1,0:T(8,128)(2,1)S(1)} %pad_maximum_fusion.8), channel_id=1, source_target_pairs={{0,64},{64,0},{1,65},{65,1},{2,66},{66,2},{3,67},{67,3},{4,68},{68... | collective-permute-start | bytes 393224 | tf_op jit(solution)/shard_map/ppermute | solution.py:23
  126.4 14.2 %collective-permute-start.9 = (bf16[512,256]{1,0:T(8,128)(2,1)}, bf16[512,256]{1,0:T(8,128)(2,1)}, u32[]{:S(2)}, u32[]{:S(2)}) collective-permute-start(bf16[512,256]{1,0:T(8,128)(2,1)} %pad_maximum_fusion.5), channel_id=1, source_target_pairs={{0,32},{16,48},{32,0},{48,16},{1,33},{17,49},{33,1},{49,17},{2,34}... | collective-permute-start | bytes 786440 | tf_op jit(solution)/shard_map/ppermute | solution.py:23
  129.5 18.0 %all-to-all-start.1 = ((bf16[4,4,256,128]{3,2,1,0:T(8,128)(2,1)}), bf16[4,4,256,128]{3,2,1,0:T(8,128)(2,1)S(1)}, u32[]{:S(2)}, u32[]{:S(2)}) async-start(bf16[4,4,256,128]{3,2,1,0:T(8,128)(2,1)} %bitcast.65), calls=%async_computation.1 | async-start | bytes 2097152 | tf_op jit(solution)/shard_map/all_to_all | solution.py:27
  142.4 16.0 %collective-permute-start.10 = (bf16[512,512]{1,0:T(8,128)(2,1)}, bf16[512,512]{1,0:T(8,128)(2,1)}, u32[]{:S(2)}, u32[]{:S(2)}) collective-permute-start(bf16[512,512]{1,0:T(8,128)(2,1)} %pad_maximum_fusion.2), channel_id=1, source_target_pairs={{0,16},{16,0},{32,48},{48,32},{1,17},{17,1},{33,49},{49,33},{2,18}... | collective-permute-start | bytes 1572872 | tf_op jit(solution)/shard_map/ppermute | solution.py:23
  148.2 12.1 %copy-start = (bf16[1024,512]{1,0:T(8,128)(2,1)}, bf16[1024,512]{1,0:T(8,128)(2,1)S(1)}, u32[]{:S(2)}) copy-start(bf16[1024,512]{1,0:T(8,128)(2,1)S(1)} %shard_map.77) | copy-start | bytes 3145732
  160.3 22.6 %copy-start.1 = (bf16[1024,512]{1,0:T(8,128)(2,1)S(1)}, bf16[1024,512]{1,0:T(8,128)(2,1)}, u32[]{:S(2)}) copy-start(bf16[1024,512]{1,0:T(8,128)(2,1)} %copy-done) | copy-start | bytes 3145732
  183.5 8.3 %collective-permute-start.11 = (bf16[256,512]{1,0:T(8,128)(2,1)S(1)}, bf16[256,512]{1,0:T(8,128)(2,1)S(1)}, u32[]{:S(2)}, u32[]{:S(2)}) collective-permute-start(bf16[256,512]{1,0:T(8,128)(2,1)S(1)} %slice.100), channel_id=1, source_target_pairs={{0,16},{16,0},{32,48},{48,32},{1,17},{17,1},{33,49},{49,33},{2,18}... | collective-permute-start | bytes 786440 | tf_op jit(solution)/shard_map/ppermute | solution.py:23
  191.9 9.2 %collective-permute-start.12 = (bf16[256,256]{1,0:T(8,128)(2,1)S(1)}, bf16[256,256]{1,0:T(8,128)(2,1)S(1)}, u32[]{:S(2)}, u32[]{:S(2)}) collective-permute-start(bf16[256,256]{1,0:T(8,128)(2,1)S(1)} %slice.101), channel_id=1, source_target_pairs={{0,32},{16,48},{32,0},{48,16},{1,33},{17,49},{33,1},{49,17},{2,34}... | collective-permute-start | bytes 393224 | tf_op jit(solution)/shard_map/ppermute | solution.py:23
  201.5 4.6 %collective-permute-start.13 = (bf16[2048,256]{1,0:T(8,128)(2,1)S(1)}, bf16[2048,256]{1,0:T(8,128)(2,1)S(1)}, u32[]{:S(2)}, u32[]{:S(2)}) collective-permute-start(bf16[2048,256]{1,0:T(8,128)(2,1)S(1)} %convolution_convert_fusion), channel_id=1, source_target_pairs={{0,1},{1,0},{2,3},{3,2},{4,5},{5,4},{6,7},{7,6},{8,9},{9,8},{10,11... | collective-permute-start | bytes 3145736 | tf_op jit(solution)/shard_map/ppermute | solution.py:23

commit v5 on v2

--- a/solution.py
+++ b/solution.py
@@ -74,7 +74,7 @@
     line, basis = barrier((line, basis))
 
     line = jnp.concatenate([line, swap(line, "zl", 2)], axis=1)
-    basis = spread(basis, "y")
+    basis = lax.all_gather(basis, "y")
     basis = basis.reshape(2, 2, 2, rows, cols).transpose(2, 0, 1, 3, 4)
     basis = basis.reshape(4, 2, rows, cols)
     line, basis = barrier((line, basis))
@@ -112,10 +112,11 @@
             for half in range(2):
                 index.append(place_of + (block & 1))
                 moves.append((number, (), half, p, half))
-    rotated = spread(rotated, "y").reshape(8 * rows, 2 * cols)
     left = place(
         jnp.stack(index).astype(jnp.int32), left, (32 * cols, 2 * cols), cols, moves, 8 * 2**20
     )
+    rotated = spread(rotated, "y").reshape(8 * rows, 2 * cols)
+    rotated, left = barrier((rotated, left))
     other = swap(rotated, "core", 1)
     contract_rows = (((0,), (0,)), ((), ()))
     rot = lax.dot_general(

time: 235 us -> 222 us (0.945)
  waiting for transfers between devices: 76.1 us -> 64.5 us
  blocking collectives: 67.4 us -> 62.7 us
  starting transfers between devices: 67.4 us -> 71.2 us
    all_to_all x4 -> x3, blocking collectives: 52.1 us -> 34.1 us  [exchange(): return lax.all_to_all(blocks, axis, 0, 0, tiled=True)]
    ppermute x14, waiting for transfers between devices: 75.1 us -> 59.6 us  [swap(): return lax.ppermute(value, axis, [(i, i ^ offset) for i in range(size)])]
    all_gather x0 -> x1, blocking collectives: none -> 13.3 us  [shards(): basis = lax.all_gather(basis, 'y')]
    all_to_all x2, waiting for transfers between devices: 0.94 us -> 4.91 us  [exchange(): return lax.all_to_all(blocks, axis, 0, 0, tiled=True)]
    ppermute x14, starting transfers between devices: 58.1 us -> 62 us  [swap(): return lax.ppermute(value, axis, [(i, i ^ offset) for i in range(size)])]
  transfers between devices with their start and end apart: 16 -> 16, of which waited for: 10 -> 11; matrix products, arithmetic and copies ran while one was open for 2% -> 2% of each run, Pallas kernels for 0% -> 0%
where the time goes in v5:
time: 222 us; the launch traced here: 220 us
  starting transfers between devices  71.2 us (32%)
  waiting for transfers between devices  64.5 us (29%)
  blocking collectives  62.7 us (28%)
  local copies, waits for them, and re-layouts  8.03 us (4%)
  other arithmetic  5.4 us (2%)
  matrix products  4.21 us (2%)
    ppermute x14, starting transfers between devices, swap(): return lax.ppermute(value, axis, [(i, i ^ offset) for i in range(size)])  62 us
    ppermute x14, waiting for transfers between devices, swap(): return lax.ppermute(value, axis, [(i, i ^ offset) for i in range(size)])  59.6 us
    all_to_all x3, blocking collectives, exchange(): return lax.all_to_all(blocks, axis, 0, 0, tiled=True)  34.1 us
    all_gather x1, blocking collectives, shards(): basis = lax.all_gather(basis, 'zh')  15.3 us
    all_gather x1, blocking collectives, shards(): basis = lax.all_gather(basis, 'y')  13.3 us
    all_to_all x2, starting transfers between devices, exchange(): return lax.all_to_all(blocks, axis, 0, 0, tiled=True)  9.22 us
    all_to_all x2, waiting for transfers between devices, exchange(): return lax.all_to_all(blocks, axis, 0, 0, tiled=True)  4.91 us
    unnamed x19, local copies, waits for them, and re-layouts  4.59 us
  transfers between devices with their start and end apart: 16, of which 11 were waited for; matrix products, arithmetic and copies ran while one was open for 2% of the time, Pallas kernels for 0%

profile of v5, /device:TPU:6, one launch (start us, length us, event | category | flops | bytes accessed | tf_op | source)
XLA Modules:
  0.0 219.7 jit_solution(890166768673699336)
XLA Ops:
  3.9 9.1 %collective-permute-start = (bf16[768,128]{1,0:T(8,128)(2,1)S(1)}, bf16[768,128]{1,0:T(8,128)(2,1)S(1)}, u32[]{:S(2)}, u32[]{:S(2)}) collective-permute-start(bf16[768,128]{1,0:T(8,128)(2,1)S(1)} %pad_maximum_fusion.3), channel_id=1, source_target_pairs={{0,64},{16,80},{32,96},{48,112},{64,0},{80,16},{96,32},{112,48},{1... | collective-permute-start | bytes 589832 | tf_op jit(solution)/shard_map/ppermute | solution.py:22
  13.0 15.3 %all-gather = bf16[512,128]{1,0:T(8,128)(2,1)S(1)} all-gather(bf16[256,128]{1,0:T(8,128)(2,1)} %param.9), channel_id=2, replica_groups=mesh['x'=4,'zl'=8,'zh'=2,'y'=4,'core'=2] {'zh'}, dimensions={0}, use_global_device_ids=true | all-gather | bytes 196608 | tf_op jit(solution)/shard_map/all_gather | solution.py:73
  28.3 7.8 %collective-permute-done = bf16[768,128]{1,0:T(8,128)(2,1)S(1)} collective-permute-done((bf16[768,128]{1,0:T(8,128)(2,1)S(1)}, bf16[768,128]{1,0:T(8,128)(2,1)S(1)}, u32[]{:S(2)}, u32[]{:S(2)}) %collective-permute-start) | collective-permute-done | bytes 196640 | tf_op jit(solution)/shard_map/ppermute | solution.py:22
  36.2 8.0 %collective-permute-start.1 = (bf16[768,256]{1,0:T(8,128)(2,1)S(1)}, bf16[768,256]{1,0:T(8,128)(2,1)S(1)}, u32[]{:S(2)}, u32[]{:S(2)}) collective-permute-start(bf16[768,256]{1,0:T(8,128)(2,1)S(1)} %pad_maximum_fusion.1), channel_id=1, source_target_pairs={{0,32},{16,48},{32,0},{48,16},{64,96},{80,112},{96,64},{112,80},{1... | collective-permute-start | bytes 1179656 | tf_op jit(solution)/shard_map/ppermute | solution.py:22
  44.2 13.3 %all-gather.1 = bf16[8,256,128]{2,1,0:T(8,128)(2,1)S(1)} all-gather(bf16[2,256,128]{2,1,0:T(8,128)(2,1)S(1)} %bitcast.66), channel_id=3, replica_groups=mesh['x'=4,'zl'=8,'zh'=2,'y'=4,'core'=2] {'y'}, dimensions={0}, use_global_device_ids=true | all-gather | bytes 655360 | tf_op jit(solution)/shard_map/all_gather | solution.py:77
  58.4 1.9 collective-permute-start.2
  60.3 12.2 %all_to_all.25.refs_0_ = bf16[4,2,256,128]{3,2,1,0:T(8,128)(2,1)S(1)} all-to-all(bf16[4,2,256,128]{3,2,1,0:T(8,128)(2,1)S(1)} %bitcast.63), channel_id=1, replica_groups=mesh['x'=4,'zl'=8,'zh'=2,'y'=4,'core'=2] {'x'}, dimensions={0} | all-to-all | bytes 1048576 | tf_op jit(solution)/shard_map/all_to_all | solution.py:26
  74.7 5.1 %collective-permute-done.2 = bf16[768,512]{1,0:T(8,128)(2,1)S(1)} collective-permute-done((bf16[768,512]{1,0:T(8,128)(2,1)S(1)}, bf16[768,512]{1,0:T(8,128)(2,1)S(1)}, u32[]{:S(2)}, u32[]{:S(2)}) %collective-permute-start.2) | collective-permute-done | bytes 786464 | tf_op jit(solution)/shard_map/ppermute | solution.py:22
  82.2 4.8 %all-to-all-start.1 = ((bf16[4,512,128]{2,1,0:T(8,128)(2,1)}), bf16[4,512,128]{2,1,0:T(8,128)(2,1)}, u32[]{:S(2)}, u32[]{:S(2)}) async-start(bf16[4,512,128]{2,1,0:T(8,128)(2,1)} %bitcast_bitcast_fusion), calls=%async_computation.1 | async-start | bytes 1048576 | tf_op jit(solution)/shard_map/all_to_all | solution.py:26
  87.0 2.8 %collective-permute-start.5 = (bf16[256,1024]{1,0:T(8,128)(2,1)S(1)}, bf16[256,1024]{1,0:T(8,128)(2,1)S(1)}, u32[]{:S(2)}, u32[]{:S(2)}) collective-permute-start(bf16[256,1024]{1,0:T(8,128)(2,1)S(1)} %slice.78.refs_0_), channel_id=1, source_target_pairs={{0,128},{128,0},{256,384},{384,256},{1,129},{129,1},{257,385},{385... | collective-permute-start | bytes 1572872 | tf_op jit(solution)/shard_map/ppermute | solution.py:22
  89.8 3.1 %collective-permute-start.6 = (bf16[256,1024]{1,0:T(8,128)(2,1)S(1)}, bf16[256,1024]{1,0:T(8,128)(2,1)S(1)}, u32[]{:S(2)}, u32[]{:S(2)}) collective-permute-start(bf16[256,1024]{1,0:T(8,128)(2,1)S(1)} %slice.78.refs_0_), channel_id=1, source_target_pairs={{0,384},{128,256},{256,128},{384,0},{1,385},{129,257},{257,129},{3... | collective-permute-start | bytes 1572872 | tf_op jit(solution)/shard_map/ppermute | solution.py:22
  92.9 4.0 %collective-permute-start.7 = (bf16[256,1024]{1,0:T(8,128)(2,1)S(1)}, bf16[256,1024]{1,0:T(8,128)(2,1)S(1)}, u32[]{:S(2)}, u32[]{:S(2)}) collective-permute-start(bf16[256,1024]{1,0:T(8,128)(2,1)S(1)} %slice.78.refs_0_), channel_id=1, source_target_pairs={{0,256},{128,384},{256,0},{384,128},{1,257},{129,385},{257,1},{385... | collective-permute-start | bytes 1572872 | tf_op jit(solution)/shard_map/ppermute | solution.py:22
  98.0 9.1 %collective-permute-start.4 = (bf16[256,256]{1,0:T(8,128)(2,1)S(1)}, bf16[256,256]{1,0:T(8,128)(2,1)S(1)}, u32[]{:S(2)}, u32[]{:S(2)}) collective-permute-start(bf16[256,256]{1,0:T(8,128)(2,1)S(1)} %pad_maximum_fusion.4), channel_id=1, source_target_pairs={{0,8},{8,0},{1,9},{9,1},{2,10},{10,2},{3,11},{11,3},{4,12},{12,4},... | collective-permute-start | bytes 393224 | tf_op jit(solution)/shard_map/ppermute | solution.py:22
  107.2 12.5 %collective-permute-done.4 = bf16[256,256]{1,0:T(8,128)(2,1)S(1)} collective-permute-done((bf16[256,256]{1,0:T(8,128)(2,1)S(1)}, bf16[256,256]{1,0:T(8,128)(2,1)S(1)}, u32[]{:S(2)}, u32[]{:S(2)}) %collective-permute-start.4) | collective-permute-done | bytes 131104 | tf_op jit(solution)/shard_map/ppermute | solution.py:22
  121.2 4.5 %all-to-all-start.2 = ((bf16[4,512,256]{2,1,0:T(8,128)(2,1)}), bf16[4,512,256]{2,1,0:T(8,128)(2,1)}, u32[]{:S(2)}, u32[]{:S(2)}) async-start(bf16[4,512,256]{2,1,0:T(8,128)(2,1)} %broadcast_in_dim.4), calls=%async_computation.2 | async-start | bytes 2097152 | tf_op jit(solution)/shard_map/all_to_all | solution.py:26
  131.7 4.9 %all-to-all-done.2 = bf16[4,512,256]{2,1,0:T(8,128)(2,1)} async-done(((bf16[4,512,256]{2,1,0:T(8,128)(2,1)}), bf16[4,512,256]{2,1,0:T(8,128)(2,1)}, u32[]{:S(2)}, u32[]{:S(2)}) %all-to-all-start.2) | async-done | bytes 1048608 | tf_op jit(solution)/shard_map/all_to_all | solution.py:26
  142.8 9.5 %all_to_all.26 = bf16[4,256,128]{1,2,0:T(8,128)(2,1)S(1)} all-to-all(bf16[4,256,128]{1,2,0:T(8,128)(2,1)S(1)} %broadcast_in_dim.5), channel_id=1, replica_groups=mesh['x'=4,'zl'=8,'zh'=2,'y'=4,'core'=2] {'x'}, dimensions={0} | all-to-all | bytes 524288 | tf_op jit(solution)/shard_map/all_to_all | solution.py:26
  152.8 7.0 %collective-permute-start.9 = (bf16[256,512]{1,0:T(8,128)(2,1)S(1)}, bf16[256,512]{1,0:T(8,128)(2,1)S(1)}, u32[]{:S(2)}, u32[]{:S(2)}) collective-permute-start(bf16[256,512]{1,0:T(8,128)(2,1)S(1)} %slice.122), channel_id=1, source_target_pairs={{0,16},{16,0},{32,48},{48,32},{64,80},{80,64},{96,112},{112,96},{1... | collective-permute-start | bytes 786440 | tf_op jit(solution)/shard_map/ppermute | solution.py:22
  159.8 5.1 %collective-permute-done.9 = bf16[256,512]{1,0:T(8,128)(2,1)S(1)} collective-permute-done((bf16[256,512]{1,0:T(8,128)(2,1)S(1)}, bf16[256,512]{1,0:T(8,128)(2,1)S(1)}, u32[]{:S(2)}, u32[]{:S(2)}) %collective-permute-start.9) | collective-permute-done | bytes 262176 | tf_op jit(solution)/shard_map/ppermute | solution.py:22
  167.0 7.2 %collective-permute-done.10 = bf16[256,256]{1,0:T(8,128)(2,1)S(1)} collective-permute-done((bf16[256,256]{1,0:T(8,128)(2,1)S(1)}, bf16[256,256]{1,0:T(8,128)(2,1)S(1)}, u32[]{:S(2)}, u32[]{:S(2)}) %collective-permute-start.10) | collective-permute-done | bytes 131104 | tf_op jit(solution)/shard_map/ppermute | solution.py:22
  176.2 9.4 %collective-permute-done.11 = bf16[256,128]{1,0:T(8,128)(2,1)S(1)} collective-permute-done((bf16[256,128]{1,0:T(8,128)(2,1)S(1)}, bf16[256,128]{1,0:T(8,128)(2,1)S(1)}, u32[]{:S(2)}, u32[]{:S(2)}) %collective-permute-start.11) | collective-permute-done | bytes 65568 | tf_op jit(solution)/shard_map/ppermute | solution.py:22
  190.0 12.5 %all_to_all.27 = bf16[4,512,128]{2,1,0:T(8,128)(2,1)S(1)} all-to-all(bf16[4,512,128]{2,1,0:T(8,128)(2,1)S(1)} %bitcast.64), channel_id=1, replica_groups=mesh['x'=4,'zl'=8,'zh'=2,'y'=4,'core'=2] {'y'}, dimensions={0} | all-to-all | bytes 1048576 | tf_op jit(solution)/shard_map/all_to_all | solution.py:26
  202.5 7.5 %collective-permute-start.13 = (bf16[256,128]{1,0:T(8,128)(2,1)S(1)}, bf16[256,128]{1,0:T(8,128)(2,1)S(1)}, u32[]{:S(2)}, u32[]{:S(2)}) collective-permute-start(bf16[256,128]{1,0:T(8,128)(2,1)S(1)} %slice.124), channel_id=1, source_target_pairs={{0,8},{8,0},{1,9},{9,1},{2,10},{10,2},{3,11},{11,3},{4,12},{12,4},... | collective-permute-start | bytes 196616 | tf_op jit(solution)/shard_map/ppermute | solution.py:22
  210.0 9.0 %collective-permute-done.13 = bf16[256,128]{1,0:T(8,128)(2,1)S(1)} collective-permute-done((bf16[256,128]{1,0:T(8,128)(2,1)S(1)}, bf16[256,128]{1,0:T(8,128)(2,1)S(1)}, u32[]{:S(2)}, u32[]{:S(2)}) %collective-permute-start.13) | collective-permute-done | bytes 65568 | tf_op jit(solution)/shard_map/ppermute | solution.py:22
  (68 shorter events, 32.2 us)
Async XLA Ops:
  3.9 32.2 %collective-permute-start = (bf16[768,128]{1,0:T(8,128)(2,1)S(1)}, bf16[768,128]{1,0:T(8,128)(2,1)S(1)}, u32[]{:S(2)}, u32[]{:S(2)}) collective-permute-start(bf16[768,128]{1,0:T(8,128)(2,1)S(1)} %pad_maximum_fusion.3), channel_id=1, source_target_pairs={{0,64},{16,80},{32,96},{48,112},{64,0},{80,16},{96,32},{112,48},{1... | collective-permute-start | bytes 589832 | tf_op jit(solution)/shard_map/ppermute | solution.py:22
  36.2 22.1 %collective-permute-start.1 = (bf16[768,256]{1,0:T(8,128)(2,1)S(1)}, bf16[768,256]{1,0:T(8,128)(2,1)S(1)}, u32[]{:S(2)}, u32[]{:S(2)}) collective-permute-start(bf16[768,256]{1,0:T(8,128)(2,1)S(1)} %pad_maximum_fusion.1), channel_id=1, source_target_pairs={{0,32},{16,48},{32,0},{48,16},{64,96},{80,112},{96,64},{112,80},{1... | collective-permute-start | bytes 1179656 | tf_op jit(solution)/shard_map/ppermute | solution.py:22
  58.4 21.4 %collective-permute-start.2 = (bf16[768,512]{1,0:T(8,128)(2,1)S(1)}, bf16[768,512]{1,0:T(8,128)(2,1)S(1)}, u32[]{:S(2)}, u32[]{:S(2)}) collective-permute-start(bf16[768,512]{1,0:T(8,128)(2,1)S(1)} %pad_maximum_fusion), channel_id=1, source_target_pairs={{0,16},{16,0},{32,48},{48,32},{64,80},{80,64},{96,112},{112,96},{1... | collective-permute-start | bytes 2359304 | tf_op jit(solution)/shard_map/ppermute | solution.py:22
  72.5 7.4 %collective-permute-start.3 = (bf16[4,2,256,128]{3,2,1,0:T(8,128)(2,1)S(1)}, bf16[4,2,256,128]{3,2,1,0:T(8,128)(2,1)S(1)}, u32[]{:S(2)}, u32[]{:S(2)}) collective-permute-start(bf16[4,2,256,128]{3,2,1,0:T(8,128)(2,1)S(1)} %all_to_all.25.refs_0_), channel_id=1, source_target_pairs={{0,1},{1,0},{2,3},{3,2},{4,5},{5,4},{6,7},{7,6},{8,9},{9,8},{10,11... | collective-permute-start | bytes 1572872 | tf_op jit(solution)/shard_map/ppermute | solution.py:22
  79.9 13.0 %copy-start = (bf16[256,1024]{1,0:T(8,128)(2,1)}, bf16[256,1024]{1,0:T(8,128)(2,1)S(1)}, u32[]{:S(2)}) copy-start(bf16[256,1024]{1,0:T(8,128)(2,1)S(1)} %slice.78.refs_0_) | copy-start | bytes 1572868
  82.2 14.6 %all-to-all-start.1 = ((bf16[4,512,128]{2,1,0:T(8,128)(2,1)}), bf16[4,512,128]{2,1,0:T(8,128)(2,1)}, u32[]{:S(2)}, u32[]{:S(2)}) async-start(bf16[4,512,128]{2,1,0:T(8,128)(2,1)} %bitcast_bitcast_fusion), calls=%async_computation.1 | async-start | bytes 1048576 | tf_op jit(solution)/shard_map/all_to_all | solution.py:26
  87.0 32.7 %collective-permute-start.5 = (bf16[256,1024]{1,0:T(8,128)(2,1)S(1)}, bf16[256,1024]{1,0:T(8,128)(2,1)S(1)}, u32[]{:S(2)}, u32[]{:S(2)}) collective-permute-start(bf16[256,1024]{1,0:T(8,128)(2,1)S(1)} %slice.78.refs_0_), channel_id=1, source_target_pairs={{0,128},{128,0},{256,384},{384,256},{1,129},{129,1},{257,385},{385... | collective-permute-start | bytes 1572872 | tf_op jit(solution)/shard_map/ppermute | solution.py:22
  89.8 29.9 %collective-permute-start.6 = (bf16[256,1024]{1,0:T(8,128)(2,1)S(1)}, bf16[256,1024]{1,0:T(8,128)(2,1)S(1)}, u32[]{:S(2)}, u32[]{:S(2)}) collective-permute-start(bf16[256,1024]{1,0:T(8,128)(2,1)S(1)} %slice.78.refs_0_), channel_id=1, source_target_pairs={{0,384},{128,256},{256,128},{384,0},{1,385},{129,257},{257,129},{3... | collective-permute-start | bytes 1572872 | tf_op jit(solution)/shard_map/ppermute | solution.py:22
  92.9 26.9 %collective-permute-start.7 = (bf16[256,1024]{1,0:T(8,128)(2,1)S(1)}, bf16[256,1024]{1,0:T(8,128)(2,1)S(1)}, u32[]{:S(2)}, u32[]{:S(2)}) collective-permute-start(bf16[256,1024]{1,0:T(8,128)(2,1)S(1)} %slice.78.refs_0_), channel_id=1, source_target_pairs={{0,256},{128,384},{256,0},{384,128},{1,257},{129,385},{257,1},{385... | collective-permute-start | bytes 1572872 | tf_op jit(solution)/shard_map/ppermute | solution.py:22
  98.0 21.6 %collective-permute-start.4 = (bf16[256,256]{1,0:T(8,128)(2,1)S(1)}, bf16[256,256]{1,0:T(8,128)(2,1)S(1)}, u32[]{:S(2)}, u32[]{:S(2)}) collective-permute-start(bf16[256,256]{1,0:T(8,128)(2,1)S(1)} %pad_maximum_fusion.4), channel_id=1, source_target_pairs={{0,8},{8,0},{1,9},{9,1},{2,10},{10,2},{3,11},{11,3},{4,12},{12,4},... | collective-permute-start | bytes 393224 | tf_op jit(solution)/shard_map/ppermute | solution.py:22
  119.7 1.2 copy-start.2
  119.7 1.3 copy-start.4
  119.7 1.5 copy-start.6
  121.2 15.5 %all-to-all-start.2 = ((bf16[4,512,256]{2,1,0:T(8,128)(2,1)}), bf16[4,512,256]{2,1,0:T(8,128)(2,1)}, u32[]{:S(2)}, u32[]{:S(2)}) async-start(bf16[4,512,256]{2,1,0:T(8,128)(2,1)} %broadcast_in_dim.4), calls=%async_computation.2 | async-start | bytes 2097152 | tf_op jit(solution)/shard_map/all_to_all | solution.py:26
  126.7 1.0 copy-start.1
  127.7 1.0 copy-start.3
  128.7 1.0 copy-start.5
  136.7 4.8 %collective-permute-start.8 = (bf16[2048,256]{1,0:T(8,128)(2,1)}, bf16[2048,256]{1,0:T(8,128)(2,1)S(1)}, u32[]{:S(2)}, u32[]{:S(2)}) collective-permute-start(bf16[2048,256]{1,0:T(8,128)(2,1)} %bitcast.13), channel_id=1, source_target_pairs={{0,1},{1,0},{2,3},{3,2},{4,5},{5,4},{6,7},{7,6},{8,9},{9,8},{10,11... | collective-permute-start | bytes 3145736 | tf_op jit(solution)/shard_map/ppermute | solution.py:22
  140.3 1.6 copy-start.8
  152.8 12.2 %collective-permute-start.9 = (bf16[256,512]{1,0:T(8,128)(2,1)S(1)}, bf16[256,512]{1,0:T(8,128)(2,1)S(1)}, u32[]{:S(2)}, u32[]{:S(2)}) collective-permute-start(bf16[256,512]{1,0:T(8,128)(2,1)S(1)} %slice.122), channel_id=1, source_target_pairs={{0,16},{16,0},{32,48},{48,32},{64,80},{80,64},{96,112},{112,96},{1... | collective-permute-start | bytes 786440 | tf_op jit(solution)/shard_map/ppermute | solution.py:22
  165.0 9.2 %collective-permute-start.10 = (bf16[256,256]{1,0:T(8,128)(2,1)S(1)}, bf16[256,256]{1,0:T(8,128)(2,1)S(1)}, u32[]{:S(2)}, u32[]{:S(2)}) collective-permute-start(bf16[256,256]{1,0:T(8,128)(2,1)S(1)} %slice.123), channel_id=1, source_target_pairs={{0,32},{16,48},{32,0},{48,16},{64,96},{80,112},{96,64},{112,80},{1... | collective-permute-start | bytes 393224 | tf_op jit(solution)/shard_map/ppermute | solution.py:22
  174.3 11.3 %collective-permute-start.11 = (bf16[256,128]{1,0:T(8,128)(2,1)S(1)}, bf16[256,128]{1,0:T(8,128)(2,1)S(1)}, u32[]{:S(2)}, u32[]{:S(2)}) collective-permute-start(bf16[256,128]{1,0:T(8,128)(2,1)S(1)} %slice.125), channel_id=1, source_target_pairs={{0,64},{16,80},{32,96},{48,112},{64,0},{80,16},{96,32},{112,48},{1... | collective-permute-start | bytes 196616 | tf_op jit(solution)/shard_map/ppermute | solution.py:22
  186.0 3.8 %collective-permute-start.12 = (bf16[2048,128]{1,0:T(8,128)(2,1)S(1)}, bf16[2048,128]{1,0:T(8,128)(2,1)S(1)}, u32[]{:S(2)}, u32[]{:S(2)}) collective-permute-start(bf16[2048,128]{1,0:T(8,128)(2,1)S(1)} %convolution_convert_fusion), channel_id=1, source_target_pairs={{0,1},{1,0},{2,3},{3,2},{4,5},{5,4},{6,7},{7,6},{8,9},{9,8},{10,11... | collective-permute-start | bytes 1572872 | tf_op jit(solution)/shard_map/ppermute | solution.py:22
  202.5 16.5 %collective-permute-start.13 = (bf16[256,128]{1,0:T(8,128)(2,1)S(1)}, bf16[256,128]{1,0:T(8,128)(2,1)S(1)}, u32[]{:S(2)}, u32[]{:S(2)}) collective-permute-start(bf16[256,128]{1,0:T(8,128)(2,1)S(1)} %slice.124), channel_id=1, source_target_pairs={{0,8},{8,0},{1,9},{9,1},{2,10},{10,2},{3,11},{11,3},{4,12},{12,4},... | collective-permute-start | bytes 196616 | tf_op jit(solution)/shard_map/ppermute | solution.py:22
  (1 other events, 1.0 us)

commit v6 on v5

--- a/solution.py
+++ b/solution.py
@@ -101,14 +101,17 @@
     rotated = jnp.concatenate([total[:rows], total[rows:]], axis=1)
 
     left = [left] + [swap(left, "x", k) for k in (1, 3, 2)]
-    rotated = jnp.concatenate([rotated, swap(rotated, "zh", 1)], axis=0)
+    other = swap(rotated, "zh", 1)
+    rotated = jnp.concatenate(
+        [jnp.where(zh == 0, rotated, other), jnp.where(zh == 0, other, rotated)], axis=0
+    )
     rotated, *left = barrier((rotated, *left))
     index, moves = [], []
     for number, ox in enumerate((0, 1, 3, 2)):
         for p in range(8):
             block = (x ^ ox) * 8 + (zl ^ reversed_bits(p))
             n = block // 2
-            place_of = ((((n & 1) ^ core) * 4 + ((n >> 1) & 3)) * 2 + ((n >> 3) ^ zh)) * 2
+            place_of = ((((n & 1) ^ core) * 4 + ((n >> 1) & 3)) * 2 + (n >> 3)) * 2
             for half in range(2):
                 index.append(place_of + (block & 1))
                 moves.append((number, (), half, p, half))
@@ -141,9 +144,8 @@
     kept = barrier(jnp.dot(left[: 8 * rows], spectral, preferred_element_type=F32))
     sent = jnp.dot(left[8 * rows :], spectral, preferred_element_type=F32).astype(BF16)
     update = (kept + swap(sent, "core", 1).astype(F32)).astype(BF16)
-    update = exchange(update.reshape(4, 2 * rows, cols), "y")
+    update = exchange(update.reshape(8, rows, cols), ("y", "zh"))
     update = jnp.sum(update.astype(F32), axis=0)
-    update = update[:rows] + swap(update[rows:].astype(BF16), "zh", 1).astype(F32)
     return (moment_new, second_new, update.astype(BF16))
 
 

time: 222 us -> 234 us (1.054)
  the two profiles are of different devices: /device:TPU:6 before, /device:TPU:33 now
where the time goes in v6:
time: 234 us; the launch traced here: 233 us
  blocking collectives  89.9 us (38%)
  starting transfers between devices  72.6 us (31%)
  waiting for transfers between devices  49.1 us (21%)
  local copies, waits for them, and re-layouts  8.02 us (3%)
  other arithmetic  5.44 us (2%)
  matrix products  4.22 us (2%)
    all_to_all x3, blocking collectives, exchange(): return lax.all_to_all(blocks, axis, 0, 0, tiled=True)  65 us
    ppermute x13, starting transfers between devices, swap(): return lax.ppermute(value, axis, [(i, i ^ offset) for i in range(size)])  64.3 us
    ppermute x13, waiting for transfers between devices, swap(): return lax.ppermute(value, axis, [(i, i ^ offset) for i in range(size)])  41 us
    all_gather x1, blocking collectives, shards(): basis = lax.all_gather(basis, 'zh')  13 us
    all_gather x1, blocking collectives, shards(): basis = lax.all_gather(basis, 'y')  11.9 us
    all_to_all x2, starting transfers between devices, exchange(): return lax.all_to_all(blocks, axis, 0, 0, tiled=True)  8.37 us
    all_to_all x2, waiting for transfers between devices, exchange(): return lax.all_to_all(blocks, axis, 0, 0, tiled=True)  8.12 us
  transfers between devices with their start and end apart: 15, of which 11 were waited for; matrix products, arithmetic and copies ran while one was open for 2% of the time, Pallas kernels for 0%

profile of v6, /device:TPU:33, one launch (start us, length us, event | category | flops | bytes accessed | tf_op | source)
XLA Modules:
  0.0 233.1 jit_solution(15295735373190632194)
XLA Ops:
  3.9 8.8 %collective-permute-start = (bf16[768,128]{1,0:T(8,128)(2,1)S(1)}, bf16[768,128]{1,0:T(8,128)(2,1)S(1)}, u32[]{:S(2)}, u32[]{:S(2)}) collective-permute-start(bf16[768,128]{1,0:T(8,128)(2,1)S(1)} %pad_maximum_fusion.3), channel_id=1, source_target_pairs={{0,64},{16,80},{32,96},{48,112},{64,0},{80,16},{96,32},{112,48},{1... | collective-permute-start | bytes 589832 | tf_op jit(solution)/shard_map/ppermute | solution.py:22
  12.7 13.0 %all-gather = bf16[512,128]{1,0:T(8,128)(2,1)S(1)} all-gather(bf16[256,128]{1,0:T(8,128)(2,1)} %param.9), channel_id=2, replica_groups=mesh['x'=4,'zl'=8,'zh'=2,'y'=4,'core'=2] {'zh'}, dimensions={0}, use_global_device_ids=true | all-gather | bytes 196608 | tf_op jit(solution)/shard_map/all_gather | solution.py:73
  26.6 12.6 %collective-permute-start.1 = (bf16[768,256]{1,0:T(8,128)(2,1)S(1)}, bf16[768,256]{1,0:T(8,128)(2,1)S(1)}, u32[]{:S(2)}, u32[]{:S(2)}) collective-permute-start(bf16[768,256]{1,0:T(8,128)(2,1)S(1)} %pad_maximum_fusion.1), channel_id=1, source_target_pairs={{0,32},{16,48},{32,0},{48,16},{64,96},{80,112},{96,64},{112,80},{1... | collective-permute-start | bytes 1179656 | tf_op jit(solution)/shard_map/ppermute | solution.py:22
  39.2 11.9 %all-gather.1 = bf16[8,256,128]{2,1,0:T(8,128)(2,1)S(1)} all-gather(bf16[2,256,128]{2,1,0:T(8,128)(2,1)S(1)} %bitcast.66), channel_id=3, replica_groups=mesh['x'=4,'zl'=8,'zh'=2,'y'=4,'core'=2] {'y'}, dimensions={0}, use_global_device_ids=true | all-gather | bytes 655360 | tf_op jit(solution)/shard_map/all_gather | solution.py:77
  51.1 4.5 %collective-permute-done.1 = bf16[768,256]{1,0:T(8,128)(2,1)S(1)} collective-permute-done((bf16[768,256]{1,0:T(8,128)(2,1)S(1)}, bf16[768,256]{1,0:T(8,128)(2,1)S(1)}, u32[]{:S(2)}, u32[]{:S(2)}) %collective-permute-start.1) | collective-permute-done | bytes 393248 | tf_op jit(solution)/shard_map/ppermute | solution.py:22
  55.6 4.7 %collective-permute-start.2 = (bf16[768,512]{1,0:T(8,128)(2,1)S(1)}, bf16[768,512]{1,0:T(8,128)(2,1)S(1)}, u32[]{:S(2)}, u32[]{:S(2)}) collective-permute-start(bf16[768,512]{1,0:T(8,128)(2,1)S(1)} %pad_maximum_fusion), channel_id=1, source_target_pairs={{0,16},{16,0},{32,48},{48,32},{64,80},{80,64},{96,112},{112,96},{1... | collective-permute-start | bytes 2359304 | tf_op jit(solution)/shard_map/ppermute | solution.py:22
  60.3 12.3 %all_to_all.25.refs_0_ = bf16[4,2,256,128]{3,2,1,0:T(8,128)(2,1)S(1)} all-to-all(bf16[4,2,256,128]{3,2,1,0:T(8,128)(2,1)S(1)} %bitcast.63), channel_id=1, replica_groups=mesh['x'=4,'zl'=8,'zh'=2,'y'=4,'core'=2] {'x'}, dimensions={0} | all-to-all | bytes 1048576 | tf_op jit(solution)/shard_map/all_to_all | solution.py:26
  72.6 3.9 %collective-permute-start.3 = (bf16[4,2,256,128]{3,2,1,0:T(8,128)(2,1)S(1)}, bf16[4,2,256,128]{3,2,1,0:T(8,128)(2,1)S(1)}, u32[]{:S(2)}, u32[]{:S(2)}) collective-permute-start(bf16[4,2,256,128]{3,2,1,0:T(8,128)(2,1)S(1)} %all_to_all.25.refs_0_), channel_id=1, source_target_pairs={{0,1},{1,0},{2,3},{3,2},{4,5},{5,4},{6,7},{7,6},{8,9},{9,8},{10,11... | collective-permute-start | bytes 1572872 | tf_op jit(solution)/shard_map/ppermute | solution.py:22
  80.3 4.1 %all-to-all-start.1 = ((bf16[4,512,128]{2,1,0:T(8,128)(2,1)}), bf16[4,512,128]{2,1,0:T(8,128)(2,1)}, u32[]{:S(2)}, u32[]{:S(2)}) async-start(bf16[4,512,128]{2,1,0:T(8,128)(2,1)} %bitcast_bitcast_fusion), calls=%async_computation.1 | async-start | bytes 1048576 | tf_op jit(solution)/shard_map/all_to_all | solution.py:26
  84.5 3.3 %collective-permute-start.5 = (bf16[256,1024]{1,0:T(8,128)(2,1)S(1)}, bf16[256,1024]{1,0:T(8,128)(2,1)S(1)}, u32[]{:S(2)}, u32[]{:S(2)}) collective-permute-start(bf16[256,1024]{1,0:T(8,128)(2,1)S(1)} %slice.69.refs_0_), channel_id=1, source_target_pairs={{0,128},{128,0},{256,384},{384,256},{1,129},{129,1},{257,385},{385... | collective-permute-start | bytes 1572872 | tf_op jit(solution)/shard_map/ppermute | solution.py:22
  87.8 3.7 %collective-permute-start.6 = (bf16[256,1024]{1,0:T(8,128)(2,1)S(1)}, bf16[256,1024]{1,0:T(8,128)(2,1)S(1)}, u32[]{:S(2)}, u32[]{:S(2)}) collective-permute-start(bf16[256,1024]{1,0:T(8,128)(2,1)S(1)} %slice.69.refs_0_), channel_id=1, source_target_pairs={{0,384},{128,256},{256,128},{384,0},{1,385},{129,257},{257,129},{3... | collective-permute-start | bytes 1572872 | tf_op jit(solution)/shard_map/ppermute | solution.py:22
  91.5 2.5 %collective-permute-start.7 = (bf16[256,1024]{1,0:T(8,128)(2,1)S(1)}, bf16[256,1024]{1,0:T(8,128)(2,1)S(1)}, u32[]{:S(2)}, u32[]{:S(2)}) collective-permute-start(bf16[256,1024]{1,0:T(8,128)(2,1)S(1)} %slice.69.refs_0_), channel_id=1, source_target_pairs={{0,256},{128,384},{256,0},{384,128},{1,257},{129,385},{257,1},{385... | collective-permute-start | bytes 1572872 | tf_op jit(solution)/shard_map/ppermute | solution.py:22
  95.2 8.8 %collective-permute-start.4 = (bf16[256,256]{1,0:T(8,128)(2,1)S(1)}, bf16[256,256]{1,0:T(8,128)(2,1)S(1)}, u32[]{:S(2)}, u32[]{:S(2)}) collective-permute-start(bf16[256,256]{1,0:T(8,128)(2,1)S(1)} %pad_maximum_fusion.4), channel_id=1, source_target_pairs={{0,8},{8,0},{1,9},{9,1},{2,10},{10,2},{3,11},{11,3},{4,12},{12,4},... | collective-permute-start | bytes 393224 | tf_op jit(solution)/shard_map/ppermute | solution.py:22
  104.1 14.6 %collective-permute-done.4 = bf16[256,256]{1,0:T(8,128)(2,1)S(1)} collective-permute-done((bf16[256,256]{1,0:T(8,128)(2,1)S(1)}, bf16[256,256]{1,0:T(8,128)(2,1)S(1)}, u32[]{:S(2)}, u32[]{:S(2)}) %collective-permute-start.4) | collective-permute-done | bytes 131104 | tf_op jit(solution)/shard_map/ppermute | solution.py:22
  120.3 4.2 %all-to-all-start.2 = ((bf16[4,512,256]{2,1,0:T(8,128)(2,1)}), bf16[4,512,256]{2,1,0:T(8,128)(2,1)}, u32[]{:S(2)}, u32[]{:S(2)}) async-start(bf16[4,512,256]{2,1,0:T(8,128)(2,1)} %broadcast_in_dim.4), calls=%async_computation.2 | async-start | bytes 2097152 | tf_op jit(solution)/shard_map/all_to_all | solution.py:26
  130.8 8.1 %all-to-all-done.2 = bf16[4,512,256]{2,1,0:T(8,128)(2,1)} async-done(((bf16[4,512,256]{2,1,0:T(8,128)(2,1)}), bf16[4,512,256]{2,1,0:T(8,128)(2,1)}, u32[]{:S(2)}, u32[]{:S(2)}) %all-to-all-start.2) | async-done | bytes 1048608 | tf_op jit(solution)/shard_map/all_to_all | solution.py:26
  138.9 3.6 %collective-permute-start.8 = (bf16[2048,256]{1,0:T(8,128)(2,1)}, bf16[2048,256]{1,0:T(8,128)(2,1)S(1)}, u32[]{:S(2)}, u32[]{:S(2)}) collective-permute-start(bf16[2048,256]{1,0:T(8,128)(2,1)} %bitcast.13), channel_id=1, source_target_pairs={{0,1},{1,0},{2,3},{3,2},{4,5},{5,4},{6,7},{7,6},{8,9},{9,8},{10,11... | collective-permute-start | bytes 3145736 | tf_op jit(solution)/shard_map/ppermute | solution.py:22
  146.4 9.5 %all_to_all.26 = bf16[4,256,128]{1,2,0:T(8,128)(2,1)S(1)} all-to-all(bf16[4,256,128]{1,2,0:T(8,128)(2,1)S(1)} %broadcast_in_dim.5), channel_id=1, replica_groups=mesh['x'=4,'zl'=8,'zh'=2,'y'=4,'core'=2] {'x'}, dimensions={0} | all-to-all | bytes 524288 | tf_op jit(solution)/shard_map/all_to_all | solution.py:26
  156.5 1.9 collective-permute-start.9
  158.4 5.9 %collective-permute-done.9 = bf16[256,512]{1,0:T(8,128)(2,1)S(1)} collective-permute-done((bf16[256,512]{1,0:T(8,128)(2,1)S(1)}, bf16[256,512]{1,0:T(8,128)(2,1)S(1)}, u32[]{:S(2)}, u32[]{:S(2)}) %collective-permute-start.9) | collective-permute-done | bytes 262176 | tf_op jit(solution)/shard_map/ppermute | solution.py:22
  166.4 4.8 %collective-permute-done.10 = bf16[256,256]{1,0:T(8,128)(2,1)S(1)} collective-permute-done((bf16[256,256]{1,0:T(8,128)(2,1)S(1)}, bf16[256,256]{1,0:T(8,128)(2,1)S(1)}, u32[]{:S(2)}, u32[]{:S(2)}) %collective-permute-start.10) | collective-permute-done | bytes 131104 | tf_op jit(solution)/shard_map/ppermute | solution.py:22
  173.1 7.4 %collective-permute-done.11 = bf16[256,128]{1,0:T(8,128)(2,1)S(1)} collective-permute-done((bf16[256,128]{1,0:T(8,128)(2,1)S(1)}, bf16[256,128]{1,0:T(8,128)(2,1)S(1)}, u32[]{:S(2)}, u32[]{:S(2)}) %collective-permute-start.11) | collective-permute-done | bytes 65568 | tf_op jit(solution)/shard_map/ppermute | solution.py:22
  181.0 6.6 %collective-permute-start.12 = (bf16[2048,128]{1,0:T(8,128)(2,1)S(1)}, bf16[2048,128]{1,0:T(8,128)(2,1)S(1)}, u32[]{:S(2)}, u32[]{:S(2)}) collective-permute-start(bf16[2048,128]{1,0:T(8,128)(2,1)S(1)} %convolution_convert_fusion), channel_id=1, source_target_pairs={{0,1},{1,0},{2,3},{3,2},{4,5},{5,4},{6,7},{7,6},{8,9},{9,8},{10,11... | collective-permute-start | bytes 1572872 | tf_op jit(solution)/shard_map/ppermute | solution.py:22
  189.2 43.2 %all_to_all.27 = bf16[8,256,128]{2,1,0:T(8,128)(2,1)S(1)} all-to-all(bf16[8,256,128]{2,1,0:T(8,128)(2,1)S(1)} %bitcast.64), channel_id=1, replica_groups=mesh['x'=4,'zl'=8,'zh'=2,'y'=4,'core'=2] {'y','zh'}, dimensions={0} | all-to-all | bytes 1048576 | tf_op jit(solution)/shard_map/all_to_all | solution.py:26
  (65 shorter events, 26.9 us)
Async XLA Ops:
  3.9 22.6 %collective-permute-start = (bf16[768,128]{1,0:T(8,128)(2,1)S(1)}, bf16[768,128]{1,0:T(8,128)(2,1)S(1)}, u32[]{:S(2)}, u32[]{:S(2)}) collective-permute-start(bf16[768,128]{1,0:T(8,128)(2,1)S(1)} %pad_maximum_fusion.3), channel_id=1, source_target_pairs={{0,64},{16,80},{32,96},{48,112},{64,0},{80,16},{96,32},{112,48},{1... | collective-permute-start | bytes 589832 | tf_op jit(solution)/shard_map/ppermute | solution.py:22
  26.6 29.0 %collective-permute-start.1 = (bf16[768,256]{1,0:T(8,128)(2,1)S(1)}, bf16[768,256]{1,0:T(8,128)(2,1)S(1)}, u32[]{:S(2)}, u32[]{:S(2)}) collective-permute-start(bf16[768,256]{1,0:T(8,128)(2,1)S(1)} %pad_maximum_fusion.1), channel_id=1, source_target_pairs={{0,32},{16,48},{32,0},{48,16},{64,96},{80,112},{96,64},{112,80},{1... | collective-permute-start | bytes 1179656 | tf_op jit(solution)/shard_map/ppermute | solution.py:22
  55.6 22.1 %collective-permute-start.2 = (bf16[768,512]{1,0:T(8,128)(2,1)S(1)}, bf16[768,512]{1,0:T(8,128)(2,1)S(1)}, u32[]{:S(2)}, u32[]{:S(2)}) collective-permute-start(bf16[768,512]{1,0:T(8,128)(2,1)S(1)} %pad_maximum_fusion), channel_id=1, source_target_pairs={{0,16},{16,0},{32,48},{48,32},{64,80},{80,64},{96,112},{112,96},{1... | collective-permute-start | bytes 2359304 | tf_op jit(solution)/shard_map/ppermute | solution.py:22
  72.6 5.4 %collective-permute-start.3 = (bf16[4,2,256,128]{3,2,1,0:T(8,128)(2,1)S(1)}, bf16[4,2,256,128]{3,2,1,0:T(8,128)(2,1)S(1)}, u32[]{:S(2)}, u32[]{:S(2)}) collective-permute-start(bf16[4,2,256,128]{3,2,1,0:T(8,128)(2,1)S(1)} %all_to_all.25.refs_0_), channel_id=1, source_target_pairs={{0,1},{1,0},{2,3},{3,2},{4,5},{5,4},{6,7},{7,6},{8,9},{9,8},{10,11... | collective-permute-start | bytes 1572872 | tf_op jit(solution)/shard_map/ppermute | solution.py:22
  77.9 13.6 %copy-start = (bf16[256,1024]{1,0:T(8,128)(2,1)}, bf16[256,1024]{1,0:T(8,128)(2,1)S(1)}, u32[]{:S(2)}) copy-start(bf16[256,1024]{1,0:T(8,128)(2,1)S(1)} %slice.69.refs_0_) | copy-start | bytes 1572868
  80.3 13.7 %all-to-all-start.1 = ((bf16[4,512,128]{2,1,0:T(8,128)(2,1)}), bf16[4,512,128]{2,1,0:T(8,128)(2,1)}, u32[]{:S(2)}, u32[]{:S(2)}) async-start(bf16[4,512,128]{2,1,0:T(8,128)(2,1)} %bitcast_bitcast_fusion), calls=%async_computation.1 | async-start | bytes 1048576 | tf_op jit(solution)/shard_map/all_to_all | solution.py:26
  84.5 34.3 %collective-permute-start.5 = (bf16[256,1024]{1,0:T(8,128)(2,1)S(1)}, bf16[256,1024]{1,0:T(8,128)(2,1)S(1)}, u32[]{:S(2)}, u32[]{:S(2)}) collective-permute-start(bf16[256,1024]{1,0:T(8,128)(2,1)S(1)} %slice.69.refs_0_), channel_id=1, source_target_pairs={{0,128},{128,0},{256,384},{384,256},{1,129},{129,1},{257,385},{385... | collective-permute-start | bytes 1572872 | tf_op jit(solution)/shard_map/ppermute | solution.py:22
  87.8 31.0 %collective-permute-start.6 = (bf16[256,1024]{1,0:T(8,128)(2,1)S(1)}, bf16[256,1024]{1,0:T(8,128)(2,1)S(1)}, u32[]{:S(2)}, u32[]{:S(2)}) collective-permute-start(bf16[256,1024]{1,0:T(8,128)(2,1)S(1)} %slice.69.refs_0_), channel_id=1, source_target_pairs={{0,384},{128,256},{256,128},{384,0},{1,385},{129,257},{257,129},{3... | collective-permute-start | bytes 1572872 | tf_op jit(solution)/shard_map/ppermute | solution.py:22
  91.5 27.3 %collective-permute-start.7 = (bf16[256,1024]{1,0:T(8,128)(2,1)S(1)}, bf16[256,1024]{1,0:T(8,128)(2,1)S(1)}, u32[]{:S(2)}, u32[]{:S(2)}) collective-permute-start(bf16[256,1024]{1,0:T(8,128)(2,1)S(1)} %slice.69.refs_0_), channel_id=1, source_target_pairs={{0,256},{128,384},{256,0},{384,128},{1,257},{129,385},{257,1},{385... | collective-permute-start | bytes 1572872 | tf_op jit(solution)/shard_map/ppermute | solution.py:22
  95.2 23.5 %collective-permute-start.4 = (bf16[256,256]{1,0:T(8,128)(2,1)S(1)}, bf16[256,256]{1,0:T(8,128)(2,1)S(1)}, u32[]{:S(2)}, u32[]{:S(2)}) collective-permute-start(bf16[256,256]{1,0:T(8,128)(2,1)S(1)} %pad_maximum_fusion.4), channel_id=1, source_target_pairs={{0,8},{8,0},{1,9},{9,1},{2,10},{10,2},{3,11},{11,3},{4,12},{12,4},... | collective-permute-start | bytes 393224 | tf_op jit(solution)/shard_map/ppermute | solution.py:22
  118.8 1.2 copy-start.2
  118.8 1.3 copy-start.4
  118.8 1.5 copy-start.6
  120.3 18.6 %all-to-all-start.2 = ((bf16[4,512,256]{2,1,0:T(8,128)(2,1)}), bf16[4,512,256]{2,1,0:T(8,128)(2,1)}, u32[]{:S(2)}, u32[]{:S(2)}) async-start(bf16[4,512,256]{2,1,0:T(8,128)(2,1)} %broadcast_in_dim.4), calls=%async_computation.2 | async-start | bytes 2097152 | tf_op jit(solution)/shard_map/all_to_all | solution.py:26
  125.7 1.0 copy-start.1
  126.8 1.0 copy-start.3
  127.8 1.0 copy-start.5
  128.9 1.0 copy-start.7
  138.9 6.1 %collective-permute-start.8 = (bf16[2048,256]{1,0:T(8,128)(2,1)}, bf16[2048,256]{1,0:T(8,128)(2,1)S(1)}, u32[]{:S(2)}, u32[]{:S(2)}) collective-permute-start(bf16[2048,256]{1,0:T(8,128)(2,1)} %bitcast.13), channel_id=1, source_target_pairs={{0,1},{1,0},{2,3},{3,2},{4,5},{5,4},{6,7},{7,6},{8,9},{9,8},{10,11... | collective-permute-start | bytes 3145736 | tf_op jit(solution)/shard_map/ppermute | solution.py:22
  144.3 1.3 copy-start.8
  156.5 7.9 %collective-permute-start.9 = (bf16[256,512]{1,0:T(8,128)(2,1)S(1)}, bf16[256,512]{1,0:T(8,128)(2,1)S(1)}, u32[]{:S(2)}, u32[]{:S(2)}) collective-permute-start(bf16[256,512]{1,0:T(8,128)(2,1)S(1)} %slice.107), channel_id=1, source_target_pairs={{0,16},{16,0},{32,48},{48,32},{64,80},{80,64},{96,112},{112,96},{1... | collective-permute-start | bytes 786440 | tf_op jit(solution)/shard_map/ppermute | solution.py:22
  164.4 6.7 %collective-permute-start.10 = (bf16[256,256]{1,0:T(8,128)(2,1)S(1)}, bf16[256,256]{1,0:T(8,128)(2,1)S(1)}, u32[]{:S(2)}, u32[]{:S(2)}) collective-permute-start(bf16[256,256]{1,0:T(8,128)(2,1)S(1)} %slice.108), channel_id=1, source_target_pairs={{0,32},{16,48},{32,0},{48,16},{64,96},{80,112},{96,64},{112,80},{1... | collective-permute-start | bytes 393224 | tf_op jit(solution)/shard_map/ppermute | solution.py:22
  171.2 9.4 %collective-permute-start.11 = (bf16[256,128]{1,0:T(8,128)(2,1)S(1)}, bf16[256,128]{1,0:T(8,128)(2,1)S(1)}, u32[]{:S(2)}, u32[]{:S(2)}) collective-permute-start(bf16[256,128]{1,0:T(8,128)(2,1)S(1)} %slice.109), channel_id=1, source_target_pairs={{0,64},{16,80},{32,96},{48,112},{64,0},{80,16},{96,32},{112,48},{1... | collective-permute-start | bytes 196616 | tf_op jit(solution)/shard_map/ppermute | solution.py:22
  181.0 8.1 %collective-permute-start.12 = (bf16[2048,128]{1,0:T(8,128)(2,1)S(1)}, bf16[2048,128]{1,0:T(8,128)(2,1)S(1)}, u32[]{:S(2)}, u32[]{:S(2)}) collective-permute-start(bf16[2048,128]{1,0:T(8,128)(2,1)S(1)} %convolution_convert_fusion), channel_id=1, source_target_pairs={{0,1},{1,0},{2,3},{3,2},{4,5},{5,4},{6,7},{7,6},{8,9},{9,8},{10,11... | collective-permute-start | bytes 1572872 | tf_op jit(solution)/shard_map/ppermute | solution.py:22

commit v7 on v5

--- a/solution.py
+++ b/solution.py
@@ -50,6 +50,48 @@
     )(index, *sources)
 
 
+def begin(grad, moment, left_basis):
+    rows, cols = grad.shape
+    half = rows // 2
+
+    def kernel(grad_ref, moment_ref, left_ref, moment_new_ref, line_ref, old_ref, sems):
+        moves = [
+            (grad_ref, line_ref.at[pl.ds(0, rows)]),
+            (moment_ref, old_ref),
+            (left_ref.at[:, pl.ds(0, cols)], line_ref.at[pl.ds(2 * rows, half)]),
+            (left_ref.at[:, pl.ds(cols, cols)], line_ref.at[pl.ds(2 * rows + half, half)]),
+        ]
+        copies = [
+            pltpu.make_async_copy(source, target, sems.at[n])
+            for n, (source, target) in enumerate(moves)
+        ]
+        for copy in copies:
+            copy.start()
+        copies[0].wait()
+        copies[1].wait()
+        new = beta_first * old_ref[...] + (1.0 - beta_first) * line_ref[:rows].astype(F32)
+        moment_new_ref[...] = new
+        line_ref[rows : 2 * rows] = new.astype(BF16)
+        copies[2].wait()
+        copies[3].wait()
+
+    in_hbm = pl.BlockSpec(memory_space=pltpu.HBM)
+    in_vmem = pl.BlockSpec(memory_space=pltpu.VMEM)
+    return pl.pallas_call(
+        kernel,
+        out_shape=(
+            jax.ShapeDtypeStruct(moment.shape, F32),
+            jax.ShapeDtypeStruct((3 * rows, cols), BF16),
+        ),
+        in_specs=[in_hbm] * 3,
+        out_specs=(in_vmem, in_vmem),
+        scratch_shapes=[pltpu.VMEM(moment.shape, F32), pltpu.SemaphoreType.DMA((4,))],
+        cost_estimate=pl.CostEstimate(
+            flops=3 * rows * cols, bytes_accessed=18 * rows * cols, transcendentals=0
+        ),
+    )(grad, moment, left_basis)
+
+
 def reversed_bits(o):
     return ((o & 1) << 2) | (o & 2) | (o >> 2)
 
@@ -63,10 +105,7 @@
     core = lax.axis_index("core")
     barrier = lax.optimization_barrier
 
-    moment_new = beta_first * moment + (1.0 - beta_first) * grad.astype(F32)
-    line = jnp.concatenate(
-        [grad, moment_new.astype(BF16), left_basis[:, :cols], left_basis[:, cols:]], axis=0
-    )
+    moment_new, line = begin(grad, moment, left_basis)
     line, basis = barrier((line, right_basis))
 
     line = jnp.concatenate([line, swap(line, "zl", 4)], axis=1)

time: 222 us -> 223 us (level)
  no operation moved by 1% of the time
where the time goes in v7:
time: 223 us; the launch traced here: 220 us
  starting transfers between devices  71.6 us (32%)
  waiting for transfers between devices  64.5 us (29%)
  blocking collectives  62.9 us (28%)
  local copies, waits for them, and re-layouts  7.24 us (3%)
  matrix products  4.2 us (2%)
  other arithmetic  3.85 us (2%)
  Pallas kernels  3.38 us (2%)
    ppermute x14, starting transfers between devices, swap(): return lax.ppermute(value, axis, [(i, i ^ offset) for i in range(size)])  62.4 us
    ppermute x14, waiting for transfers between devices, swap(): return lax.ppermute(value, axis, [(i, i ^ offset) for i in range(size)])  59.6 us
    all_to_all x3, blocking collectives, exchange(): return lax.all_to_all(blocks, axis, 0, 0, tiled=True)  34.1 us
    all_gather x1, blocking collectives, shards(): basis = lax.all_gather(basis, 'zh')  15.5 us
    all_gather x1, blocking collectives, shards(): basis = lax.all_gather(basis, 'y')  13.3 us
    all_to_all x2, starting transfers between devices, exchange(): return lax.all_to_all(blocks, axis, 0, 0, tiled=True)  9.24 us
    all_to_all x2, waiting for transfers between devices, exchange(): return lax.all_to_all(blocks, axis, 0, 0, tiled=True)  4.91 us
    unnamed x19, local copies, waits for them, and re-layouts  4.58 us
  transfers between devices with their start and end apart: 16, of which 11 were waited for; matrix products, arithmetic and copies ran while one was open for 2% of the time, Pallas kernels for 0%

profile of v7, /device:TPU:6, one launch (start us, length us, event | category | flops | bytes accessed | tf_op | source)
XLA Modules:
  0.0 219.7 jit_solution(6325561840715318647)
XLA Ops:
  2.4 9.1 %collective-permute-start = (bf16[768,128]{1,0:T(8,128)(2,1)}, bf16[768,128]{1,0:T(8,128)(2,1)S(1)}, u32[]{:S(2)}, u32[]{:S(2)}) collective-permute-start(bf16[768,128]{1,0:T(8,128)(2,1)} %get-tuple-element.22), channel_id=1, source_target_pairs={{0,64},{16,80},{32,96},{48,112},{64,0},{80,16},{96,32},{112,48},{1... | collective-permute-start | bytes 589832 | tf_op jit(solution)/shard_map/ppermute | solution.py:22
  11.5 15.5 %all-gather = bf16[512,128]{1,0:T(8,128)(2,1)S(1)} all-gather(bf16[256,128]{1,0:T(8,128)(2,1)} %param.9), channel_id=2, replica_groups=mesh['x'=4,'zl'=8,'zh'=2,'y'=4,'core'=2] {'zh'}, dimensions={0}, use_global_device_ids=true | all-gather | bytes 196608 | tf_op jit(solution)/shard_map/all_gather | solution.py:112
  27.0 7.8 %collective-permute-done = bf16[768,128]{1,0:T(8,128)(2,1)S(1)} collective-permute-done((bf16[768,128]{1,0:T(8,128)(2,1)}, bf16[768,128]{1,0:T(8,128)(2,1)S(1)}, u32[]{:S(2)}, u32[]{:S(2)}) %collective-permute-start) | collective-permute-done | bytes 196640 | tf_op jit(solution)/shard_map/ppermute | solution.py:22
  35.8 8.0 %collective-permute-start.1 = (bf16[768,256]{1,0:T(8,128)(2,1)S(1)}, bf16[768,256]{1,0:T(8,128)(2,1)S(1)}, u32[]{:S(2)}, u32[]{:S(2)}) collective-permute-start(bf16[768,256]{1,0:T(8,128)(2,1)S(1)} %pad_maximum_fusion.1), channel_id=1, source_target_pairs={{0,32},{16,48},{32,0},{48,16},{64,96},{80,112},{96,64},{112,80},{1... | collective-permute-start | bytes 1179656 | tf_op jit(solution)/shard_map/ppermute | solution.py:22
  43.8 13.3 %all-gather.1 = bf16[8,256,128]{2,1,0:T(8,128)(2,1)S(1)} all-gather(bf16[2,256,128]{2,1,0:T(8,128)(2,1)S(1)} %bitcast.66), channel_id=3, replica_groups=mesh['x'=4,'zl'=8,'zh'=2,'y'=4,'core'=2] {'y'}, dimensions={0}, use_global_device_ids=true | all-gather | bytes 655360 | tf_op jit(solution)/shard_map/all_gather | solution.py:116
  60.0 12.2 %all_to_all.25.refs_0_ = bf16[4,2,256,128]{3,2,1,0:T(8,128)(2,1)S(1)} all-to-all(bf16[4,2,256,128]{3,2,1,0:T(8,128)(2,1)S(1)} %bitcast.63), channel_id=1, replica_groups=mesh['x'=4,'zl'=8,'zh'=2,'y'=4,'core'=2] {'x'}, dimensions={0} | all-to-all | bytes 1048576 | tf_op jit(solution)/shard_map/all_to_all | solution.py:26
  74.4 5.1 %collective-permute-done.2 = bf16[768,512]{1,0:T(8,128)(2,1)S(1)} collective-permute-done((bf16[768,512]{1,0:T(8,128)(2,1)S(1)}, bf16[768,512]{1,0:T(8,128)(2,1)S(1)}, u32[]{:S(2)}, u32[]{:S(2)}) %collective-permute-start.2) | collective-permute-done | bytes 786464 | tf_op jit(solution)/shard_map/ppermute | solution.py:22
  82.0 4.8 %all-to-all-start.1 = ((bf16[4,512,128]{2,1,0:T(8,128)(2,1)}), bf16[4,512,128]{2,1,0:T(8,128)(2,1)}, u32[]{:S(2)}, u32[]{:S(2)}) async-start(bf16[4,512,128]{2,1,0:T(8,128)(2,1)} %bitcast_bitcast_fusion), calls=%async_computation.1 | async-start | bytes 1048576 | tf_op jit(solution)/shard_map/all_to_all | solution.py:26
  86.8 2.8 %collective-permute-start.5 = (bf16[256,1024]{1,0:T(8,128)(2,1)S(1)}, bf16[256,1024]{1,0:T(8,128)(2,1)S(1)}, u32[]{:S(2)}, u32[]{:S(2)}) collective-permute-start(bf16[256,1024]{1,0:T(8,128)(2,1)S(1)} %slice.70.refs_0_), channel_id=1, source_target_pairs={{0,128},{128,0},{256,384},{384,256},{1,129},{129,1},{257,385},{385... | collective-permute-start | bytes 1572872 | tf_op jit(solution)/shard_map/ppermute | solution.py:22
  89.5 3.1 %collective-permute-start.6 = (bf16[256,1024]{1,0:T(8,128)(2,1)S(1)}, bf16[256,1024]{1,0:T(8,128)(2,1)S(1)}, u32[]{:S(2)}, u32[]{:S(2)}) collective-permute-start(bf16[256,1024]{1,0:T(8,128)(2,1)S(1)} %slice.70.refs_0_), channel_id=1, source_target_pairs={{0,384},{128,256},{256,128},{384,0},{1,385},{129,257},{257,129},{3... | collective-permute-start | bytes 1572872 | tf_op jit(solution)/shard_map/ppermute | solution.py:22
  92.6 4.0 %collective-permute-start.7 = (bf16[256,1024]{1,0:T(8,128)(2,1)S(1)}, bf16[256,1024]{1,0:T(8,128)(2,1)S(1)}, u32[]{:S(2)}, u32[]{:S(2)}) collective-permute-start(bf16[256,1024]{1,0:T(8,128)(2,1)S(1)} %slice.70.refs_0_), channel_id=1, source_target_pairs={{0,256},{128,384},{256,0},{384,128},{1,257},{129,385},{257,1},{385... | collective-permute-start | bytes 1572872 | tf_op jit(solution)/shard_map/ppermute | solution.py:22
  97.8 9.1 %collective-permute-start.4 = (bf16[256,256]{1,0:T(8,128)(2,1)S(1)}, bf16[256,256]{1,0:T(8,128)(2,1)S(1)}, u32[]{:S(2)}, u32[]{:S(2)}) collective-permute-start(bf16[256,256]{1,0:T(8,128)(2,1)S(1)} %pad_maximum_fusion.3), channel_id=1, source_target_pairs={{0,8},{8,0},{1,9},{9,1},{2,10},{10,2},{3,11},{11,3},{4,12},{12,4},... | collective-permute-start | bytes 393224 | tf_op jit(solution)/shard_map/ppermute | solution.py:22
  106.9 12.4 %collective-permute-done.4 = bf16[256,256]{1,0:T(8,128)(2,1)S(1)} collective-permute-done((bf16[256,256]{1,0:T(8,128)(2,1)S(1)}, bf16[256,256]{1,0:T(8,128)(2,1)S(1)}, u32[]{:S(2)}, u32[]{:S(2)}) %collective-permute-start.4) | collective-permute-done | bytes 131104 | tf_op jit(solution)/shard_map/ppermute | solution.py:22
  120.9 4.5 %all-to-all-start.2 = ((bf16[4,512,256]{2,1,0:T(8,128)(2,1)}), bf16[4,512,256]{2,1,0:T(8,128)(2,1)}, u32[]{:S(2)}, u32[]{:S(2)}) async-start(bf16[4,512,256]{2,1,0:T(8,128)(2,1)} %broadcast_in_dim.4), calls=%async_computation.2 | async-start | bytes 2097152 | tf_op jit(solution)/shard_map/all_to_all | solution.py:26
  131.4 4.9 %all-to-all-done.2 = bf16[4,512,256]{2,1,0:T(8,128)(2,1)} async-done(((bf16[4,512,256]{2,1,0:T(8,128)(2,1)}), bf16[4,512,256]{2,1,0:T(8,128)(2,1)}, u32[]{:S(2)}, u32[]{:S(2)}) %all-to-all-start.2) | async-done | bytes 1048608 | tf_op jit(solution)/shard_map/all_to_all | solution.py:26
  142.4 9.5 %all_to_all.26 = bf16[4,256,128]{1,2,0:T(8,128)(2,1)S(1)} all-to-all(bf16[4,256,128]{1,2,0:T(8,128)(2,1)S(1)} %broadcast_in_dim.5), channel_id=1, replica_groups=mesh['x'=4,'zl'=8,'zh'=2,'y'=4,'core'=2] {'x'}, dimensions={0} | all-to-all | bytes 524288 | tf_op jit(solution)/shard_map/all_to_all | solution.py:26
  152.5 7.2 %collective-permute-start.9 = (bf16[256,512]{1,0:T(8,128)(2,1)S(1)}, bf16[256,512]{1,0:T(8,128)(2,1)S(1)}, u32[]{:S(2)}, u32[]{:S(2)}) collective-permute-start(bf16[256,512]{1,0:T(8,128)(2,1)S(1)} %slice.114), channel_id=1, source_target_pairs={{0,16},{16,0},{32,48},{48,32},{64,80},{80,64},{96,112},{112,96},{1... | collective-permute-start | bytes 786440 | tf_op jit(solution)/shard_map/ppermute | solution.py:22
  159.7 5.2 %collective-permute-done.9 = bf16[256,512]{1,0:T(8,128)(2,1)S(1)} collective-permute-done((bf16[256,512]{1,0:T(8,128)(2,1)S(1)}, bf16[256,512]{1,0:T(8,128)(2,1)S(1)}, u32[]{:S(2)}, u32[]{:S(2)}) %collective-permute-start.9) | collective-permute-done | bytes 262176 | tf_op jit(solution)/shard_map/ppermute | solution.py:22
  166.9 7.2 %collective-permute-done.10 = bf16[256,256]{1,0:T(8,128)(2,1)S(1)} collective-permute-done((bf16[256,256]{1,0:T(8,128)(2,1)S(1)}, bf16[256,256]{1,0:T(8,128)(2,1)S(1)}, u32[]{:S(2)}, u32[]{:S(2)}) %collective-permute-start.10) | collective-permute-done | bytes 131104 | tf_op jit(solution)/shard_map/ppermute | solution.py:22
  174.1 1.9 collective-permute-start.11
  176.1 9.4 %collective-permute-done.11 = bf16[256,128]{1,0:T(8,128)(2,1)S(1)} collective-permute-done((bf16[256,128]{1,0:T(8,128)(2,1)S(1)}, bf16[256,128]{1,0:T(8,128)(2,1)S(1)}, u32[]{:S(2)}, u32[]{:S(2)}) %collective-permute-start.11) | collective-permute-done | bytes 65568 | tf_op jit(solution)/shard_map/ppermute | solution.py:22
  189.8 12.5 %all_to_all.27 = bf16[4,512,128]{2,1,0:T(8,128)(2,1)S(1)} all-to-all(bf16[4,512,128]{2,1,0:T(8,128)(2,1)S(1)} %bitcast.64), channel_id=1, replica_groups=mesh['x'=4,'zl'=8,'zh'=2,'y'=4,'core'=2] {'y'}, dimensions={0} | all-to-all | bytes 1048576 | tf_op jit(solution)/shard_map/all_to_all | solution.py:26
  202.4 7.7 %collective-permute-start.13 = (bf16[256,128]{1,0:T(8,128)(2,1)S(1)}, bf16[256,128]{1,0:T(8,128)(2,1)S(1)}, u32[]{:S(2)}, u32[]{:S(2)}) collective-permute-start(bf16[256,128]{1,0:T(8,128)(2,1)S(1)} %slice.116), channel_id=1, source_target_pairs={{0,8},{8,0},{1,9},{9,1},{2,10},{10,2},{3,11},{11,3},{4,12},{12,4},... | collective-permute-start | bytes 196616 | tf_op jit(solution)/shard_map/ppermute | solution.py:22
  210.1 9.0 %collective-permute-done.13 = bf16[256,128]{1,0:T(8,128)(2,1)S(1)} collective-permute-done((bf16[256,128]{1,0:T(8,128)(2,1)S(1)}, bf16[256,128]{1,0:T(8,128)(2,1)S(1)}, u32[]{:S(2)}, u32[]{:S(2)}) %collective-permute-start.13) | collective-permute-done | bytes 65568 | tf_op jit(solution)/shard_map/ppermute | solution.py:22
  (66 shorter events, 31.7 us)
Async XLA Ops:
  2.4 32.5 %collective-permute-start = (bf16[768,128]{1,0:T(8,128)(2,1)}, bf16[768,128]{1,0:T(8,128)(2,1)S(1)}, u32[]{:S(2)}, u32[]{:S(2)}) collective-permute-start(bf16[768,128]{1,0:T(8,128)(2,1)} %get-tuple-element.22), channel_id=1, source_target_pairs={{0,64},{16,80},{32,96},{48,112},{64,0},{80,16},{96,32},{112,48},{1... | collective-permute-start | bytes 589832 | tf_op jit(solution)/shard_map/ppermute | solution.py:22
  35.8 22.2 %collective-permute-start.1 = (bf16[768,256]{1,0:T(8,128)(2,1)S(1)}, bf16[768,256]{1,0:T(8,128)(2,1)S(1)}, u32[]{:S(2)}, u32[]{:S(2)}) collective-permute-start(bf16[768,256]{1,0:T(8,128)(2,1)S(1)} %pad_maximum_fusion.1), channel_id=1, source_target_pairs={{0,32},{16,48},{32,0},{48,16},{64,96},{80,112},{96,64},{112,80},{1... | collective-permute-start | bytes 1179656 | tf_op jit(solution)/shard_map/ppermute | solution.py:22
  58.1 21.4 %collective-permute-start.2 = (bf16[768,512]{1,0:T(8,128)(2,1)S(1)}, bf16[768,512]{1,0:T(8,128)(2,1)S(1)}, u32[]{:S(2)}, u32[]{:S(2)}) collective-permute-start(bf16[768,512]{1,0:T(8,128)(2,1)S(1)} %pad_maximum_fusion), channel_id=1, source_target_pairs={{0,16},{16,0},{32,48},{48,32},{64,80},{80,64},{96,112},{112,96},{1... | collective-permute-start | bytes 2359304 | tf_op jit(solution)/shard_map/ppermute | solution.py:22
  72.2 7.4 %collective-permute-start.3 = (bf16[4,2,256,128]{3,2,1,0:T(8,128)(2,1)S(1)}, bf16[4,2,256,128]{3,2,1,0:T(8,128)(2,1)S(1)}, u32[]{:S(2)}, u32[]{:S(2)}) collective-permute-start(bf16[4,2,256,128]{3,2,1,0:T(8,128)(2,1)S(1)} %all_to_all.25.refs_0_), channel_id=1, source_target_pairs={{0,1},{1,0},{2,3},{3,2},{4,5},{5,4},{6,7},{7,6},{8,9},{9,8},{10,11... | collective-permute-start | bytes 1572872 | tf_op jit(solution)/shard_map/ppermute | solution.py:22
  79.6 13.0 %copy-start = (bf16[256,1024]{1,0:T(8,128)(2,1)}, bf16[256,1024]{1,0:T(8,128)(2,1)S(1)}, u32[]{:S(2)}) copy-start(bf16[256,1024]{1,0:T(8,128)(2,1)S(1)} %slice.70.refs_0_) | copy-start | bytes 1572868
  82.0 14.6 %all-to-all-start.1 = ((bf16[4,512,128]{2,1,0:T(8,128)(2,1)}), bf16[4,512,128]{2,1,0:T(8,128)(2,1)}, u32[]{:S(2)}, u32[]{:S(2)}) async-start(bf16[4,512,128]{2,1,0:T(8,128)(2,1)} %bitcast_bitcast_fusion), calls=%async_computation.1 | async-start | bytes 1048576 | tf_op jit(solution)/shard_map/all_to_all | solution.py:26
  86.8 32.6 %collective-permute-start.5 = (bf16[256,1024]{1,0:T(8,128)(2,1)S(1)}, bf16[256,1024]{1,0:T(8,128)(2,1)S(1)}, u32[]{:S(2)}, u32[]{:S(2)}) collective-permute-start(bf16[256,1024]{1,0:T(8,128)(2,1)S(1)} %slice.70.refs_0_), channel_id=1, source_target_pairs={{0,128},{128,0},{256,384},{384,256},{1,129},{129,1},{257,385},{385... | collective-permute-start | bytes 1572872 | tf_op jit(solution)/shard_map/ppermute | solution.py:22
  89.5 29.9 %collective-permute-start.6 = (bf16[256,1024]{1,0:T(8,128)(2,1)S(1)}, bf16[256,1024]{1,0:T(8,128)(2,1)S(1)}, u32[]{:S(2)}, u32[]{:S(2)}) collective-permute-start(bf16[256,1024]{1,0:T(8,128)(2,1)S(1)} %slice.70.refs_0_), channel_id=1, source_target_pairs={{0,384},{128,256},{256,128},{384,0},{1,385},{129,257},{257,129},{3... | collective-permute-start | bytes 1572872 | tf_op jit(solution)/shard_map/ppermute | solution.py:22
  92.6 26.8 %collective-permute-start.7 = (bf16[256,1024]{1,0:T(8,128)(2,1)S(1)}, bf16[256,1024]{1,0:T(8,128)(2,1)S(1)}, u32[]{:S(2)}, u32[]{:S(2)}) collective-permute-start(bf16[256,1024]{1,0:T(8,128)(2,1)S(1)} %slice.70.refs_0_), channel_id=1, source_target_pairs={{0,256},{128,384},{256,0},{384,128},{1,257},{129,385},{257,1},{385... | collective-permute-start | bytes 1572872 | tf_op jit(solution)/shard_map/ppermute | solution.py:22
  97.8 21.6 %collective-permute-start.4 = (bf16[256,256]{1,0:T(8,128)(2,1)S(1)}, bf16[256,256]{1,0:T(8,128)(2,1)S(1)}, u32[]{:S(2)}, u32[]{:S(2)}) collective-permute-start(bf16[256,256]{1,0:T(8,128)(2,1)S(1)} %pad_maximum_fusion.3), channel_id=1, source_target_pairs={{0,8},{8,0},{1,9},{9,1},{2,10},{10,2},{3,11},{11,3},{4,12},{12,4},... | collective-permute-start | bytes 393224 | tf_op jit(solution)/shard_map/ppermute | solution.py:22
  119.4 1.2 copy-start.2
  119.4 1.3 copy-start.4
  119.4 1.5 copy-start.6
  120.9 15.5 %all-to-all-start.2 = ((bf16[4,512,256]{2,1,0:T(8,128)(2,1)}), bf16[4,512,256]{2,1,0:T(8,128)(2,1)}, u32[]{:S(2)}, u32[]{:S(2)}) async-start(bf16[4,512,256]{2,1,0:T(8,128)(2,1)} %broadcast_in_dim.4), calls=%async_computation.2 | async-start | bytes 2097152 | tf_op jit(solution)/shard_map/all_to_all | solution.py:26
  126.3 1.0 copy-start.1
  127.4 1.0 copy-start.3
  128.4 1.0 copy-start.5
  136.3 4.8 %collective-permute-start.8 = (bf16[2048,256]{1,0:T(8,128)(2,1)}, bf16[2048,256]{1,0:T(8,128)(2,1)S(1)}, u32[]{:S(2)}, u32[]{:S(2)}) collective-permute-start(bf16[2048,256]{1,0:T(8,128)(2,1)} %bitcast.13), channel_id=1, source_target_pairs={{0,1},{1,0},{2,3},{3,2},{4,5},{5,4},{6,7},{7,6},{8,9},{9,8},{10,11... | collective-permute-start | bytes 3145736 | tf_op jit(solution)/shard_map/ppermute | solution.py:22
  139.9 1.6 copy-start.8
  152.5 12.3 %collective-permute-start.9 = (bf16[256,512]{1,0:T(8,128)(2,1)S(1)}, bf16[256,512]{1,0:T(8,128)(2,1)S(1)}, u32[]{:S(2)}, u32[]{:S(2)}) collective-permute-start(bf16[256,512]{1,0:T(8,128)(2,1)S(1)} %slice.114), channel_id=1, source_target_pairs={{0,16},{16,0},{32,48},{48,32},{64,80},{80,64},{96,112},{112,96},{1... | collective-permute-start | bytes 786440 | tf_op jit(solution)/shard_map/ppermute | solution.py:22
  164.9 9.2 %collective-permute-start.10 = (bf16[256,256]{1,0:T(8,128)(2,1)S(1)}, bf16[256,256]{1,0:T(8,128)(2,1)S(1)}, u32[]{:S(2)}, u32[]{:S(2)}) collective-permute-start(bf16[256,256]{1,0:T(8,128)(2,1)S(1)} %slice.115), channel_id=1, source_target_pairs={{0,32},{16,48},{32,0},{48,16},{64,96},{80,112},{96,64},{112,80},{1... | collective-permute-start | bytes 393224 | tf_op jit(solution)/shard_map/ppermute | solution.py:22
  174.1 11.3 %collective-permute-start.11 = (bf16[256,128]{1,0:T(8,128)(2,1)S(1)}, bf16[256,128]{1,0:T(8,128)(2,1)S(1)}, u32[]{:S(2)}, u32[]{:S(2)}) collective-permute-start(bf16[256,128]{1,0:T(8,128)(2,1)S(1)} %slice.117), channel_id=1, source_target_pairs={{0,64},{16,80},{32,96},{48,112},{64,0},{80,16},{96,32},{112,48},{1... | collective-permute-start | bytes 196616 | tf_op jit(solution)/shard_map/ppermute | solution.py:22
  185.9 3.8 %collective-permute-start.12 = (bf16[2048,128]{1,0:T(8,128)(2,1)S(1)}, bf16[2048,128]{1,0:T(8,128)(2,1)S(1)}, u32[]{:S(2)}, u32[]{:S(2)}) collective-permute-start(bf16[2048,128]{1,0:T(8,128)(2,1)S(1)} %convolution_convert_fusion), channel_id=1, source_target_pairs={{0,1},{1,0},{2,3},{3,2},{4,5},{5,4},{6,7},{7,6},{8,9},{9,8},{10,11... | collective-permute-start | bytes 1572872 | tf_op jit(solution)/shard_map/ppermute | solution.py:22
  202.4 16.7 %collective-permute-start.13 = (bf16[256,128]{1,0:T(8,128)(2,1)S(1)}, bf16[256,128]{1,0:T(8,128)(2,1)S(1)}, u32[]{:S(2)}, u32[]{:S(2)}) collective-permute-start(bf16[256,128]{1,0:T(8,128)(2,1)S(1)} %slice.116), channel_id=1, source_target_pairs={{0,8},{8,0},{1,9},{9,1},{2,10},{10,2},{3,11},{11,3},{4,12},{12,4},... | collective-permute-start | bytes 196616 | tf_op jit(solution)/shard_map/ppermute | solution.py:22
  (1 other events, 1.0 us)

commit v8 on v5

--- a/solution.py
+++ b/solution.py
@@ -70,8 +70,8 @@
     line, basis = barrier((line, right_basis))
 
     line = jnp.concatenate([line, swap(line, "zl", 4)], axis=1)
-    basis = lax.all_gather(basis, "zh")
-    line, basis = barrier((line, basis))
+    other = swap(basis, "zh", 1)
+    basis = jnp.stack([jnp.where(zh == 0, basis, other), jnp.where(zh == 0, other, basis)])
 
     line = jnp.concatenate([line, swap(line, "zl", 2)], axis=1)
     basis = lax.all_gather(basis, "y")

time: 222 us -> 215 us (0.968)
  starting transfers between devices: 71.2 us -> 90.3 us
  blocking collectives: 62.7 us -> 46.6 us
  waiting for transfers between devices: 64.5 us -> 54.9 us
    ppermute x14 -> x15, starting transfers between devices: 62 us -> 81 us  [swap(): return lax.ppermute(value, axis, [(i, i ^ offset) for i in range(size)])]
    all_gather x1 -> x0, blocking collectives: 15.3 us -> none  [shards(): basis = lax.all_gather(basis, 'zh')]
    ppermute x14 -> x15, waiting for transfers between devices: 59.6 us -> 49.9 us  [swap(): return lax.ppermute(value, axis, [(i, i ^ offset) for i in range(size)])]
    unnamed x19 -> x21, local copies, waits for them, and re-layouts: 4.59 us -> 4.49 us
  transfers between devices with their start and end apart: 16 -> 17, of which waited for: 11 -> 12; matrix products, arithmetic and copies ran while one was open for 2% -> 2% of each run, Pallas kernels for 0% -> 0%
where the time goes in v8:
time: 215 us; the launch traced here: 213 us
  starting transfers between devices  90.3 us (42%)
  waiting for transfers between devices  54.9 us (26%)
  blocking collectives  46.6 us (22%)
  local copies, waits for them, and re-layouts  7.92 us (4%)
  other arithmetic  5.44 us (3%)
  matrix products  4.2 us (2%)
    ppermute x15, starting transfers between devices, swap(): return lax.ppermute(value, axis, [(i, i ^ offset) for i in range(size)])  81 us
    ppermute x15, waiting for transfers between devices, swap(): return lax.ppermute(value, axis, [(i, i ^ offset) for i in range(size)])  49.9 us
    all_to_all x3, blocking collectives, exchange(): return lax.all_to_all(blocks, axis, 0, 0, tiled=True)  33.3 us
    all_gather x1, blocking collectives, shards(): basis = lax.all_gather(basis, 'y')  13.3 us
    all_to_all x2, starting transfers between devices, exchange(): return lax.all_to_all(blocks, axis, 0, 0, tiled=True)  9.33 us
    all_to_all x2, waiting for transfers between devices, exchange(): return lax.all_to_all(blocks, axis, 0, 0, tiled=True)  5.01 us
    unnamed x21, local copies, waits for them, and re-layouts  4.49 us
  transfers between devices with their start and end apart: 17, of which 12 were waited for; matrix products, arithmetic and copies ran while one was open for 2% of the time, Pallas kernels for 0%

profile of v8, /device:TPU:6, one launch (start us, length us, event | category | flops | bytes accessed | tf_op | source)
XLA Modules:
  0.0 212.9 jit_solution(13533609745247586693)
XLA Ops:
  3.9 9.1 %collective-permute-start = (bf16[768,128]{1,0:T(8,128)(2,1)S(1)}, bf16[768,128]{1,0:T(8,128)(2,1)S(1)}, u32[]{:S(2)}, u32[]{:S(2)}) collective-permute-start(bf16[768,128]{1,0:T(8,128)(2,1)S(1)} %pad_maximum_fusion.3), channel_id=1, source_target_pairs={{0,64},{16,80},{32,96},{48,112},{64,0},{80,16},{96,32},{112,48},{1... | collective-permute-start | bytes 589832 | tf_op jit(solution)/shard_map/ppermute | solution.py:22
  13.0 10.9 %collective-permute-start.2 = (bf16[256,128]{1,0:T(8,128)(2,1)}, bf16[256,128]{1,0:T(8,128)(2,1)S(1)}, u32[]{:S(2)}, u32[]{:S(2)}) collective-permute-start(bf16[256,128]{1,0:T(8,128)(2,1)} %param.9), channel_id=1, source_target_pairs={{0,8},{8,0},{1,9},{9,1},{2,10},{10,2},{3,11},{11,3},{4,12},{12,4},... | collective-permute-start | bytes 196616 | tf_op jit(solution)/shard_map/ppermute | solution.py:22
  24.0 12.1 %collective-permute-done = bf16[768,128]{1,0:T(8,128)(2,1)S(1)} collective-permute-done((bf16[768,128]{1,0:T(8,128)(2,1)S(1)}, bf16[768,128]{1,0:T(8,128)(2,1)S(1)}, u32[]{:S(2)}, u32[]{:S(2)}) %collective-permute-start) | collective-permute-done | bytes 196640 | tf_op jit(solution)/shard_map/ppermute | solution.py:22
  38.1 13.3 %all-gather = bf16[8,256,128]{2,1,0:T(8,128)(2,1)S(1)} all-gather(bf16[2,256,128]{2,1,0:T(8,128)(2,1)S(1)} %pad_maximum_fusion.4), channel_id=2, replica_groups=mesh['x'=4,'zl'=8,'zh'=2,'y'=4,'core'=2] {'y'}, dimensions={0}, use_global_device_ids=true | all-gather | bytes 655360 | tf_op jit(solution)/shard_map/all_gather | solution.py:77
  51.4 6.2 %collective-permute-done.1 = bf16[768,256]{1,0:T(8,128)(2,1)S(1)} collective-permute-done((bf16[768,256]{1,0:T(8,128)(2,1)S(1)}, bf16[768,256]{1,0:T(8,128)(2,1)S(1)}, u32[]{:S(2)}, u32[]{:S(2)}) %collective-permute-start.1) | collective-permute-done | bytes 393248 | tf_op jit(solution)/shard_map/ppermute | solution.py:22
  59.6 11.3 %all_to_all.25.refs_0_ = bf16[4,2,256,128]{3,2,1,0:T(8,128)(2,1)S(1)} all-to-all(bf16[4,2,256,128]{3,2,1,0:T(8,128)(2,1)S(1)} %bitcast.66), channel_id=1, replica_groups=mesh['x'=4,'zl'=8,'zh'=2,'y'=4,'core'=2] {'x'}, dimensions={0} | all-to-all | bytes 1048576 | tf_op jit(solution)/shard_map/all_to_all | solution.py:26
  73.1 5.1 %collective-permute-done.3 = bf16[768,512]{1,0:T(8,128)(2,1)S(1)} collective-permute-done((bf16[768,512]{1,0:T(8,128)(2,1)S(1)}, bf16[768,512]{1,0:T(8,128)(2,1)S(1)}, u32[]{:S(2)}, u32[]{:S(2)}) %collective-permute-start.3) | collective-permute-done | bytes 786464 | tf_op jit(solution)/shard_map/ppermute | solution.py:22
  80.7 4.8 %all-to-all-start.1 = ((bf16[4,512,128]{2,1,0:T(8,128)(2,1)}), bf16[4,512,128]{2,1,0:T(8,128)(2,1)}, u32[]{:S(2)}, u32[]{:S(2)}) async-start(bf16[4,512,128]{2,1,0:T(8,128)(2,1)} %bitcast_bitcast_fusion), calls=%async_computation.1 | async-start | bytes 1048576 | tf_op jit(solution)/shard_map/all_to_all | solution.py:26
  88.2 3.1 %collective-permute-start.7 = (bf16[256,1024]{1,0:T(8,128)(2,1)S(1)}, bf16[256,1024]{1,0:T(8,128)(2,1)S(1)}, u32[]{:S(2)}, u32[]{:S(2)}) collective-permute-start(bf16[256,1024]{1,0:T(8,128)(2,1)S(1)} %slice.78.refs_0_), channel_id=1, source_target_pairs={{0,384},{128,256},{256,128},{384,0},{1,385},{129,257},{257,129},{3... | collective-permute-start | bytes 1572872 | tf_op jit(solution)/shard_map/ppermute | solution.py:22
  91.3 4.0 %collective-permute-start.8 = (bf16[256,1024]{1,0:T(8,128)(2,1)S(1)}, bf16[256,1024]{1,0:T(8,128)(2,1)S(1)}, u32[]{:S(2)}, u32[]{:S(2)}) collective-permute-start(bf16[256,1024]{1,0:T(8,128)(2,1)S(1)} %slice.78.refs_0_), channel_id=1, source_target_pairs={{0,256},{128,384},{256,0},{384,128},{1,257},{129,385},{257,1},{385... | collective-permute-start | bytes 1572872 | tf_op jit(solution)/shard_map/ppermute | solution.py:22
  96.5 10.5 %collective-permute-start.5 = (bf16[256,256]{1,0:T(8,128)(2,1)S(1)}, bf16[256,256]{1,0:T(8,128)(2,1)S(1)}, u32[]{:S(2)}, u32[]{:S(2)}) collective-permute-start(bf16[256,256]{1,0:T(8,128)(2,1)S(1)} %pad_maximum_fusion.5), channel_id=1, source_target_pairs={{0,8},{8,0},{1,9},{9,1},{2,10},{10,2},{3,11},{11,3},{4,12},{12,4},... | collective-permute-start | bytes 393224 | tf_op jit(solution)/shard_map/ppermute | solution.py:22
  107.0 5.3 %collective-permute-done.5 = bf16[256,256]{1,0:T(8,128)(2,1)S(1)} collective-permute-done((bf16[256,256]{1,0:T(8,128)(2,1)S(1)}, bf16[256,256]{1,0:T(8,128)(2,1)S(1)}, u32[]{:S(2)}, u32[]{:S(2)}) %collective-permute-start.5) | collective-permute-done | bytes 131104 | tf_op jit(solution)/shard_map/ppermute | solution.py:22
  116.5 4.6 %all-to-all-start.2 = ((bf16[4,512,256]{2,1,0:T(8,128)(2,1)}), bf16[4,512,256]{2,1,0:T(8,128)(2,1)}, u32[]{:S(2)}, u32[]{:S(2)}) async-start(bf16[4,512,256]{2,1,0:T(8,128)(2,1)} %broadcast_in_dim.4), calls=%async_computation.2 | async-start | bytes 2097152 | tf_op jit(solution)/shard_map/all_to_all | solution.py:26
  127.0 5.0 %all-to-all-done.2 = bf16[4,512,256]{2,1,0:T(8,128)(2,1)} async-done(((bf16[4,512,256]{2,1,0:T(8,128)(2,1)}), bf16[4,512,256]{2,1,0:T(8,128)(2,1)}, u32[]{:S(2)}, u32[]{:S(2)}) %all-to-all-start.2) | async-done | bytes 1048608 | tf_op jit(solution)/shard_map/all_to_all | solution.py:26
  138.1 9.5 %all_to_all.26 = bf16[4,256,128]{1,2,0:T(8,128)(2,1)S(1)} all-to-all(bf16[4,256,128]{1,2,0:T(8,128)(2,1)S(1)} %broadcast_in_dim.5), channel_id=1, replica_groups=mesh['x'=4,'zl'=8,'zh'=2,'y'=4,'core'=2] {'x'}, dimensions={0} | all-to-all | bytes 524288 | tf_op jit(solution)/shard_map/all_to_all | solution.py:26
  148.2 5.4 %collective-permute-start.10 = (bf16[256,512]{1,0:T(8,128)(2,1)S(1)}, bf16[256,512]{1,0:T(8,128)(2,1)S(1)}, u32[]{:S(2)}, u32[]{:S(2)}) collective-permute-start(bf16[256,512]{1,0:T(8,128)(2,1)S(1)} %slice.122), channel_id=1, source_target_pairs={{0,16},{16,0},{32,48},{48,32},{64,80},{80,64},{96,112},{112,96},{1... | collective-permute-start | bytes 786440 | tf_op jit(solution)/shard_map/ppermute | solution.py:22
  153.6 5.1 %collective-permute-done.10 = bf16[256,512]{1,0:T(8,128)(2,1)S(1)} collective-permute-done((bf16[256,512]{1,0:T(8,128)(2,1)S(1)}, bf16[256,512]{1,0:T(8,128)(2,1)S(1)}, u32[]{:S(2)}, u32[]{:S(2)}) %collective-permute-start.10) | collective-permute-done | bytes 262176 | tf_op jit(solution)/shard_map/ppermute | solution.py:22
  158.8 5.6 %collective-permute-start.11 = (bf16[256,256]{1,0:T(8,128)(2,1)S(1)}, bf16[256,256]{1,0:T(8,128)(2,1)S(1)}, u32[]{:S(2)}, u32[]{:S(2)}) collective-permute-start(bf16[256,256]{1,0:T(8,128)(2,1)S(1)} %slice.123), channel_id=1, source_target_pairs={{0,32},{16,48},{32,0},{48,16},{64,96},{80,112},{96,64},{112,80},{1... | collective-permute-start | bytes 393224 | tf_op jit(solution)/shard_map/ppermute | solution.py:22
  164.5 4.3 %collective-permute-done.11 = bf16[256,256]{1,0:T(8,128)(2,1)S(1)} collective-permute-done((bf16[256,256]{1,0:T(8,128)(2,1)S(1)}, bf16[256,256]{1,0:T(8,128)(2,1)S(1)}, u32[]{:S(2)}, u32[]{:S(2)}) %collective-permute-start.11) | collective-permute-done | bytes 131104 | tf_op jit(solution)/shard_map/ppermute | solution.py:22
  168.9 6.8 %collective-permute-start.12 = (bf16[256,128]{1,0:T(8,128)(2,1)S(1)}, bf16[256,128]{1,0:T(8,128)(2,1)S(1)}, u32[]{:S(2)}, u32[]{:S(2)}) collective-permute-start(bf16[256,128]{1,0:T(8,128)(2,1)S(1)} %slice.125), channel_id=1, source_target_pairs={{0,64},{16,80},{32,96},{48,112},{64,0},{80,16},{96,32},{112,48},{1... | collective-permute-start | bytes 196616 | tf_op jit(solution)/shard_map/ppermute | solution.py:22
  175.7 3.4 %collective-permute-done.12 = bf16[256,128]{1,0:T(8,128)(2,1)S(1)} collective-permute-done((bf16[256,128]{1,0:T(8,128)(2,1)S(1)}, bf16[256,128]{1,0:T(8,128)(2,1)S(1)}, u32[]{:S(2)}, u32[]{:S(2)}) %collective-permute-start.12) | collective-permute-done | bytes 65568 | tf_op jit(solution)/shard_map/ppermute | solution.py:22
  183.4 12.5 %all_to_all.27 = bf16[4,512,128]{2,1,0:T(8,128)(2,1)S(1)} all-to-all(bf16[4,512,128]{2,1,0:T(8,128)(2,1)S(1)} %bitcast.67), channel_id=1, replica_groups=mesh['x'=4,'zl'=8,'zh'=2,'y'=4,'core'=2] {'y'}, dimensions={0} | all-to-all | bytes 1048576 | tf_op jit(solution)/shard_map/all_to_all | solution.py:26
  196.0 13.2 %collective-permute-start.14 = (bf16[256,128]{1,0:T(8,128)(2,1)S(1)}, bf16[256,128]{1,0:T(8,128)(2,1)S(1)}, u32[]{:S(2)}, u32[]{:S(2)}) collective-permute-start(bf16[256,128]{1,0:T(8,128)(2,1)S(1)} %slice.124), channel_id=1, source_target_pairs={{0,8},{8,0},{1,9},{9,1},{2,10},{10,2},{3,11},{11,3},{4,12},{12,4},... | collective-permute-start | bytes 196616 | tf_op jit(solution)/shard_map/ppermute | solution.py:22
  209.2 3.0 %collective-permute-done.14 = bf16[256,128]{1,0:T(8,128)(2,1)S(1)} collective-permute-done((bf16[256,128]{1,0:T(8,128)(2,1)S(1)}, bf16[256,128]{1,0:T(8,128)(2,1)S(1)}, u32[]{:S(2)}, u32[]{:S(2)}) %collective-permute-start.14) | collective-permute-done | bytes 65568 | tf_op jit(solution)/shard_map/ppermute | solution.py:22
  (73 shorter events, 36.9 us)
Async XLA Ops:
  0.6 37.4 %copy-start.9 = (bf16[256,128]{1,0:T(8,128)(2,1)S(1)}, bf16[256,128]{1,0:T(8,128)(2,1)}, u32[]{:S(2)}) copy-start(bf16[256,128]{1,0:T(8,128)(2,1)} %param.9) | copy-start | bytes 196612
  3.9 32.1 %collective-permute-start = (bf16[768,128]{1,0:T(8,128)(2,1)S(1)}, bf16[768,128]{1,0:T(8,128)(2,1)S(1)}, u32[]{:S(2)}, u32[]{:S(2)}) collective-permute-start(bf16[768,128]{1,0:T(8,128)(2,1)S(1)} %pad_maximum_fusion.3), channel_id=1, source_target_pairs={{0,64},{16,80},{32,96},{48,112},{64,0},{80,16},{96,32},{112,48},{1... | collective-permute-start | bytes 589832 | tf_op jit(solution)/shard_map/ppermute | solution.py:22
  13.0 25.0 %collective-permute-start.2 = (bf16[256,128]{1,0:T(8,128)(2,1)}, bf16[256,128]{1,0:T(8,128)(2,1)S(1)}, u32[]{:S(2)}, u32[]{:S(2)}) collective-permute-start(bf16[256,128]{1,0:T(8,128)(2,1)} %param.9), channel_id=1, source_target_pairs={{0,8},{8,0},{1,9},{9,1},{2,10},{10,2},{3,11},{11,3},{4,12},{12,4},... | collective-permute-start | bytes 196616 | tf_op jit(solution)/shard_map/ppermute | solution.py:22
  36.1 21.5 %collective-permute-start.1 = (bf16[768,256]{1,0:T(8,128)(2,1)S(1)}, bf16[768,256]{1,0:T(8,128)(2,1)S(1)}, u32[]{:S(2)}, u32[]{:S(2)}) collective-permute-start(bf16[768,256]{1,0:T(8,128)(2,1)S(1)} %pad_maximum_fusion.1), channel_id=1, source_target_pairs={{0,32},{16,48},{32,0},{48,16},{64,96},{80,112},{96,64},{112,80},{1... | collective-permute-start | bytes 1179656 | tf_op jit(solution)/shard_map/ppermute | solution.py:22
  57.7 20.5 %collective-permute-start.3 = (bf16[768,512]{1,0:T(8,128)(2,1)S(1)}, bf16[768,512]{1,0:T(8,128)(2,1)S(1)}, u32[]{:S(2)}, u32[]{:S(2)}) collective-permute-start(bf16[768,512]{1,0:T(8,128)(2,1)S(1)} %pad_maximum_fusion), channel_id=1, source_target_pairs={{0,16},{16,0},{32,48},{48,32},{64,80},{80,64},{96,112},{112,96},{1... | collective-permute-start | bytes 2359304 | tf_op jit(solution)/shard_map/ppermute | solution.py:22
  70.9 7.4 %collective-permute-start.4 = (bf16[4,2,256,128]{3,2,1,0:T(8,128)(2,1)S(1)}, bf16[4,2,256,128]{3,2,1,0:T(8,128)(2,1)S(1)}, u32[]{:S(2)}, u32[]{:S(2)}) collective-permute-start(bf16[4,2,256,128]{3,2,1,0:T(8,128)(2,1)S(1)} %all_to_all.25.refs_0_), channel_id=1, source_target_pairs={{0,1},{1,0},{2,3},{3,2},{4,5},{5,4},{6,7},{7,6},{8,9},{9,8},{10,11... | collective-permute-start | bytes 1572872 | tf_op jit(solution)/shard_map/ppermute | solution.py:22
  78.3 13.0 %copy-start = (bf16[256,1024]{1,0:T(8,128)(2,1)}, bf16[256,1024]{1,0:T(8,128)(2,1)S(1)}, u32[]{:S(2)}) copy-start(bf16[256,1024]{1,0:T(8,128)(2,1)S(1)} %slice.78.refs_0_) | copy-start | bytes 1572868
  80.7 14.6 %all-to-all-start.1 = ((bf16[4,512,128]{2,1,0:T(8,128)(2,1)}), bf16[4,512,128]{2,1,0:T(8,128)(2,1)}, u32[]{:S(2)}, u32[]{:S(2)}) async-start(bf16[4,512,128]{2,1,0:T(8,128)(2,1)} %bitcast_bitcast_fusion), calls=%async_computation.1 | async-start | bytes 1048576 | tf_op jit(solution)/shard_map/all_to_all | solution.py:26
  85.4 26.9 %collective-permute-start.6 = (bf16[256,1024]{1,0:T(8,128)(2,1)S(1)}, bf16[256,1024]{1,0:T(8,128)(2,1)S(1)}, u32[]{:S(2)}, u32[]{:S(2)}) collective-permute-start(bf16[256,1024]{1,0:T(8,128)(2,1)S(1)} %slice.78.refs_0_), channel_id=1, source_target_pairs={{0,128},{128,0},{256,384},{384,256},{1,129},{129,1},{257,385},{385... | collective-permute-start | bytes 1572872 | tf_op jit(solution)/shard_map/ppermute | solution.py:22
  88.2 27.0 %collective-permute-start.7 = (bf16[256,1024]{1,0:T(8,128)(2,1)S(1)}, bf16[256,1024]{1,0:T(8,128)(2,1)S(1)}, u32[]{:S(2)}, u32[]{:S(2)}) collective-permute-start(bf16[256,1024]{1,0:T(8,128)(2,1)S(1)} %slice.78.refs_0_), channel_id=1, source_target_pairs={{0,384},{128,256},{256,128},{384,0},{1,385},{129,257},{257,129},{3... | collective-permute-start | bytes 1572872 | tf_op jit(solution)/shard_map/ppermute | solution.py:22
  91.3 23.9 %collective-permute-start.8 = (bf16[256,1024]{1,0:T(8,128)(2,1)S(1)}, bf16[256,1024]{1,0:T(8,128)(2,1)S(1)}, u32[]{:S(2)}, u32[]{:S(2)}) collective-permute-start(bf16[256,1024]{1,0:T(8,128)(2,1)S(1)} %slice.78.refs_0_), channel_id=1, source_target_pairs={{0,256},{128,384},{256,0},{384,128},{1,257},{129,385},{257,1},{385... | collective-permute-start | bytes 1572872 | tf_op jit(solution)/shard_map/ppermute | solution.py:22
  96.5 15.9 %collective-permute-start.5 = (bf16[256,256]{1,0:T(8,128)(2,1)S(1)}, bf16[256,256]{1,0:T(8,128)(2,1)S(1)}, u32[]{:S(2)}, u32[]{:S(2)}) collective-permute-start(bf16[256,256]{1,0:T(8,128)(2,1)S(1)} %pad_maximum_fusion.5), channel_id=1, source_target_pairs={{0,8},{8,0},{1,9},{9,1},{2,10},{10,2},{3,11},{11,3},{4,12},{12,4},... | collective-permute-start | bytes 393224 | tf_op jit(solution)/shard_map/ppermute | solution.py:22
  112.4 3.9 %copy-start.2 = (bf16[256,1024]{1,0:T(8,128)(2,1)}, bf16[256,1024]{1,0:T(8,128)(2,1)S(1)}, u32[]{:S(2)}) copy-start(bf16[256,1024]{1,0:T(8,128)(2,1)S(1)} %collective-permute-done.6.refs_1_) | copy-start | bytes 1572868
  115.2 1.2 copy-start.4
  115.2 1.3 copy-start.6
  116.5 15.6 %all-to-all-start.2 = ((bf16[4,512,256]{2,1,0:T(8,128)(2,1)}), bf16[4,512,256]{2,1,0:T(8,128)(2,1)}, u32[]{:S(2)}, u32[]{:S(2)}) async-start(bf16[4,512,256]{2,1,0:T(8,128)(2,1)} %broadcast_in_dim.4), calls=%async_computation.2 | async-start | bytes 2097152 | tf_op jit(solution)/shard_map/all_to_all | solution.py:26
  121.9 1.0 copy-start.1
  132.0 4.8 %collective-permute-start.9 = (bf16[2048,256]{1,0:T(8,128)(2,1)}, bf16[2048,256]{1,0:T(8,128)(2,1)S(1)}, u32[]{:S(2)}, u32[]{:S(2)}) collective-permute-start(bf16[2048,256]{1,0:T(8,128)(2,1)} %bitcast.14), channel_id=1, source_target_pairs={{0,1},{1,0},{2,3},{3,2},{4,5},{5,4},{6,7},{7,6},{8,9},{9,8},{10,11... | collective-permute-start | bytes 3145736 | tf_op jit(solution)/shard_map/ppermute | solution.py:22
  135.7 1.6 copy-start.8
  148.2 10.5 %collective-permute-start.10 = (bf16[256,512]{1,0:T(8,128)(2,1)S(1)}, bf16[256,512]{1,0:T(8,128)(2,1)S(1)}, u32[]{:S(2)}, u32[]{:S(2)}) collective-permute-start(bf16[256,512]{1,0:T(8,128)(2,1)S(1)} %slice.122), channel_id=1, source_target_pairs={{0,16},{16,0},{32,48},{48,32},{64,80},{80,64},{96,112},{112,96},{1... | collective-permute-start | bytes 786440 | tf_op jit(solution)/shard_map/ppermute | solution.py:22
  158.8 10.0 %collective-permute-start.11 = (bf16[256,256]{1,0:T(8,128)(2,1)S(1)}, bf16[256,256]{1,0:T(8,128)(2,1)S(1)}, u32[]{:S(2)}, u32[]{:S(2)}) collective-permute-start(bf16[256,256]{1,0:T(8,128)(2,1)S(1)} %slice.123), channel_id=1, source_target_pairs={{0,32},{16,48},{32,0},{48,16},{64,96},{80,112},{96,64},{112,80},{1... | collective-permute-start | bytes 393224 | tf_op jit(solution)/shard_map/ppermute | solution.py:22
  168.9 10.2 %collective-permute-start.12 = (bf16[256,128]{1,0:T(8,128)(2,1)S(1)}, bf16[256,128]{1,0:T(8,128)(2,1)S(1)}, u32[]{:S(2)}, u32[]{:S(2)}) collective-permute-start(bf16[256,128]{1,0:T(8,128)(2,1)S(1)} %slice.125), channel_id=1, source_target_pairs={{0,64},{16,80},{32,96},{48,112},{64,0},{80,16},{96,32},{112,48},{1... | collective-permute-start | bytes 196616 | tf_op jit(solution)/shard_map/ppermute | solution.py:22
  179.5 3.8 %collective-permute-start.13 = (bf16[2048,128]{1,0:T(8,128)(2,1)S(1)}, bf16[2048,128]{1,0:T(8,128)(2,1)S(1)}, u32[]{:S(2)}, u32[]{:S(2)}) collective-permute-start(bf16[2048,128]{1,0:T(8,128)(2,1)S(1)} %convolution_convert_fusion), channel_id=1, source_target_pairs={{0,1},{1,0},{2,3},{3,2},{4,5},{5,4},{6,7},{7,6},{8,9},{9,8},{10,11... | collective-permute-start | bytes 1572872 | tf_op jit(solution)/shard_map/ppermute | solution.py:22
  196.0 16.3 %collective-permute-start.14 = (bf16[256,128]{1,0:T(8,128)(2,1)S(1)}, bf16[256,128]{1,0:T(8,128)(2,1)S(1)}, u32[]{:S(2)}, u32[]{:S(2)}) collective-permute-start(bf16[256,128]{1,0:T(8,128)(2,1)S(1)} %slice.124), channel_id=1, source_target_pairs={{0,8},{8,0},{1,9},{9,1},{2,10},{10,2},{3,11},{11,3},{4,12},{12,4},... | collective-permute-start | bytes 196616 | tf_op jit(solution)/shard_map/ppermute | solution.py:22
  (3 other events, 3.1 us)

commit v9 on v7

--- a/solution.py
+++ b/solution.py
@@ -109,8 +109,8 @@
     line, basis = barrier((line, right_basis))
 
     line = jnp.concatenate([line, swap(line, "zl", 4)], axis=1)
-    basis = lax.all_gather(basis, "zh")
-    line, basis = barrier((line, basis))
+    other = swap(basis, "zh", 1)
+    basis = jnp.stack([jnp.where(zh == 0, basis, other), jnp.where(zh == 0, other, basis)])
 
     line = jnp.concatenate([line, swap(line, "zl", 2)], axis=1)
     basis = lax.all_gather(basis, "y")

time: 223 us -> 216 us (0.969)
  starting transfers between devices: 71.6 us -> 88.4 us
  blocking collectives: 62.9 us -> 46.6 us
  waiting for transfers between devices: 64.5 us -> 56.8 us
    ppermute x14 -> x15, starting transfers between devices: 62.4 us -> 79.1 us  [swap(): return lax.ppermute(value, axis, [(i, i ^ offset) for i in range(size)])]
    all_gather x1 -> x0, blocking collectives: 15.5 us -> none  [shards(): basis = lax.all_gather(basis, 'zh')]
    ppermute x14 -> x15, waiting for transfers between devices: 59.6 us -> 51.8 us  [swap(): return lax.ppermute(value, axis, [(i, i ^ offset) for i in range(size)])]
    unnamed x19 -> x21, local copies, waits for them, and re-layouts: 4.58 us -> 4.48 us
  transfers between devices with their start and end apart: 16 -> 17, of which waited for: 11 -> 12; matrix products, arithmetic and copies ran while one was open for 2% -> 3% of each run, Pallas kernels for 0% -> 0%
where the time goes in v9:
time: 216 us; the launch traced here: 213 us
  starting transfers between devices  88.4 us (41%)
  waiting for transfers between devices  56.8 us (26%)
  blocking collectives  46.6 us (22%)
  local copies, waits for them, and re-layouts  7.1 us (3%)
  other arithmetic  4.73 us (2%)
  matrix products  4.2 us (2%)
  Pallas kernels  3.37 us (2%)
    ppermute x15, starting transfers between devices, swap(): return lax.ppermute(value, axis, [(i, i ^ offset) for i in range(size)])  79.1 us
    ppermute x15, waiting for transfers between devices, swap(): return lax.ppermute(value, axis, [(i, i ^ offset) for i in range(size)])  51.8 us
    all_to_all x3, blocking collectives, exchange(): return lax.all_to_all(blocks, axis, 0, 0, tiled=True)  33.3 us
    all_gather x1, blocking collectives, shards(): basis = lax.all_gather(basis, 'y')  13.3 us
    all_to_all x2, starting transfers between devices, exchange(): return lax.all_to_all(blocks, axis, 0, 0, tiled=True)  9.32 us
    all_to_all x2, waiting for transfers between devices, exchange(): return lax.all_to_all(blocks, axis, 0, 0, tiled=True)  5.01 us
    unnamed x21, local copies, waits for them, and re-layouts  4.48 us
  transfers between devices with their start and end apart: 17, of which 12 were waited for; matrix products, arithmetic and copies ran while one was open for 3% of the time, Pallas kernels for 0%

profile of v9, /device:TPU:6, one launch (start us, length us, event | category | flops | bytes accessed | tf_op | source)
XLA Modules:
  0.0 213.0 jit_solution(15903780290328893025)
XLA Ops:
  2.4 9.2 %collective-permute-start = (bf16[768,128]{1,0:T(8,128)(2,1)}, bf16[768,128]{1,0:T(8,128)(2,1)S(1)}, u32[]{:S(2)}, u32[]{:S(2)}) collective-permute-start(bf16[768,128]{1,0:T(8,128)(2,1)} %get-tuple-element.20), channel_id=1, source_target_pairs={{0,64},{16,80},{32,96},{48,112},{64,0},{80,16},{96,32},{112,48},{1... | collective-permute-start | bytes 589832 | tf_op jit(solution)/shard_map/ppermute | solution.py:22
  11.6 10.9 %collective-permute-start.2 = (bf16[256,128]{1,0:T(8,128)(2,1)}, bf16[256,128]{1,0:T(8,128)(2,1)S(1)}, u32[]{:S(2)}, u32[]{:S(2)}) collective-permute-start(bf16[256,128]{1,0:T(8,128)(2,1)} %param.9), channel_id=1, source_target_pairs={{0,8},{8,0},{1,9},{9,1},{2,10},{10,2},{3,11},{11,3},{4,12},{12,4},... | collective-permute-start | bytes 196616 | tf_op jit(solution)/shard_map/ppermute | solution.py:22
  22.5 12.4 %collective-permute-done = bf16[768,128]{1,0:T(8,128)(2,1)S(1)} collective-permute-done((bf16[768,128]{1,0:T(8,128)(2,1)}, bf16[768,128]{1,0:T(8,128)(2,1)S(1)}, u32[]{:S(2)}, u32[]{:S(2)}) %collective-permute-start) | collective-permute-done | bytes 196640 | tf_op jit(solution)/shard_map/ppermute | solution.py:22
  38.8 13.3 %all-gather = bf16[8,256,128]{2,1,0:T(8,128)(2,1)S(1)} all-gather(bf16[2,256,128]{2,1,0:T(8,128)(2,1)S(1)} %pad_maximum_fusion.3), channel_id=2, replica_groups=mesh['x'=4,'zl'=8,'zh'=2,'y'=4,'core'=2] {'y'}, dimensions={0}, use_global_device_ids=true | all-gather | bytes 655360 | tf_op jit(solution)/shard_map/all_gather | solution.py:116
  52.1 5.3 %collective-permute-done.1 = bf16[768,256]{1,0:T(8,128)(2,1)S(1)} collective-permute-done((bf16[768,256]{1,0:T(8,128)(2,1)S(1)}, bf16[768,256]{1,0:T(8,128)(2,1)S(1)}, u32[]{:S(2)}, u32[]{:S(2)}) %collective-permute-start.1) | collective-permute-done | bytes 393248 | tf_op jit(solution)/shard_map/ppermute | solution.py:22
  59.4 11.3 %all_to_all.25.refs_0_ = bf16[4,2,256,128]{3,2,1,0:T(8,128)(2,1)S(1)} all-to-all(bf16[4,2,256,128]{3,2,1,0:T(8,128)(2,1)S(1)} %bitcast.66), channel_id=1, replica_groups=mesh['x'=4,'zl'=8,'zh'=2,'y'=4,'core'=2] {'x'}, dimensions={0} | all-to-all | bytes 1048576 | tf_op jit(solution)/shard_map/all_to_all | solution.py:26
  72.9 5.1 %collective-permute-done.3 = bf16[768,512]{1,0:T(8,128)(2,1)S(1)} collective-permute-done((bf16[768,512]{1,0:T(8,128)(2,1)S(1)}, bf16[768,512]{1,0:T(8,128)(2,1)S(1)}, u32[]{:S(2)}, u32[]{:S(2)}) %collective-permute-start.3) | collective-permute-done | bytes 786464 | tf_op jit(solution)/shard_map/ppermute | solution.py:22
  80.5 4.8 %all-to-all-start.1 = ((bf16[4,512,128]{2,1,0:T(8,128)(2,1)}), bf16[4,512,128]{2,1,0:T(8,128)(2,1)}, u32[]{:S(2)}, u32[]{:S(2)}) async-start(bf16[4,512,128]{2,1,0:T(8,128)(2,1)} %bitcast_bitcast_fusion), calls=%async_computation.1 | async-start | bytes 1048576 | tf_op jit(solution)/shard_map/all_to_all | solution.py:26
  88.0 3.1 %collective-permute-start.7 = (bf16[256,1024]{1,0:T(8,128)(2,1)S(1)}, bf16[256,1024]{1,0:T(8,128)(2,1)S(1)}, u32[]{:S(2)}, u32[]{:S(2)}) collective-permute-start(bf16[256,1024]{1,0:T(8,128)(2,1)S(1)} %slice.70.refs_0_), channel_id=1, source_target_pairs={{0,384},{128,256},{256,128},{384,0},{1,385},{129,257},{257,129},{3... | collective-permute-start | bytes 1572872 | tf_op jit(solution)/shard_map/ppermute | solution.py:22
  91.1 4.0 %collective-permute-start.8 = (bf16[256,1024]{1,0:T(8,128)(2,1)S(1)}, bf16[256,1024]{1,0:T(8,128)(2,1)S(1)}, u32[]{:S(2)}, u32[]{:S(2)}) collective-permute-start(bf16[256,1024]{1,0:T(8,128)(2,1)S(1)} %slice.70.refs_0_), channel_id=1, source_target_pairs={{0,256},{128,384},{256,0},{384,128},{1,257},{129,385},{257,1},{385... | collective-permute-start | bytes 1572872 | tf_op jit(solution)/shard_map/ppermute | solution.py:22
  96.3 10.6 %collective-permute-start.5 = (bf16[256,256]{1,0:T(8,128)(2,1)S(1)}, bf16[256,256]{1,0:T(8,128)(2,1)S(1)}, u32[]{:S(2)}, u32[]{:S(2)}) collective-permute-start(bf16[256,256]{1,0:T(8,128)(2,1)S(1)} %pad_maximum_fusion.4), channel_id=1, source_target_pairs={{0,8},{8,0},{1,9},{9,1},{2,10},{10,2},{3,11},{11,3},{4,12},{12,4},... | collective-permute-start | bytes 393224 | tf_op jit(solution)/shard_map/ppermute | solution.py:22
  106.8 5.2 %collective-permute-done.5 = bf16[256,256]{1,0:T(8,128)(2,1)S(1)} collective-permute-done((bf16[256,256]{1,0:T(8,128)(2,1)S(1)}, bf16[256,256]{1,0:T(8,128)(2,1)S(1)}, u32[]{:S(2)}, u32[]{:S(2)}) %collective-permute-start.5) | collective-permute-done | bytes 131104 | tf_op jit(solution)/shard_map/ppermute | solution.py:22
  116.3 4.5 %all-to-all-start.2 = ((bf16[4,512,256]{2,1,0:T(8,128)(2,1)}), bf16[4,512,256]{2,1,0:T(8,128)(2,1)}, u32[]{:S(2)}, u32[]{:S(2)}) async-start(bf16[4,512,256]{2,1,0:T(8,128)(2,1)} %broadcast_in_dim.4), calls=%async_computation.2 | async-start | bytes 2097152 | tf_op jit(solution)/shard_map/all_to_all | solution.py:26
  126.8 5.0 %all-to-all-done.2 = bf16[4,512,256]{2,1,0:T(8,128)(2,1)} async-done(((bf16[4,512,256]{2,1,0:T(8,128)(2,1)}), bf16[4,512,256]{2,1,0:T(8,128)(2,1)}, u32[]{:S(2)}, u32[]{:S(2)}) %all-to-all-start.2) | async-done | bytes 1048608 | tf_op jit(solution)/shard_map/all_to_all | solution.py:26
  137.9 9.5 %all_to_all.26 = bf16[4,256,128]{1,2,0:T(8,128)(2,1)S(1)} all-to-all(bf16[4,256,128]{1,2,0:T(8,128)(2,1)S(1)} %broadcast_in_dim.5), channel_id=1, replica_groups=mesh['x'=4,'zl'=8,'zh'=2,'y'=4,'core'=2] {'x'}, dimensions={0} | all-to-all | bytes 524288 | tf_op jit(solution)/shard_map/all_to_all | solution.py:26
  148.0 6.0 %collective-permute-start.10 = (bf16[256,512]{1,0:T(8,128)(2,1)S(1)}, bf16[256,512]{1,0:T(8,128)(2,1)S(1)}, u32[]{:S(2)}, u32[]{:S(2)}) collective-permute-start(bf16[256,512]{1,0:T(8,128)(2,1)S(1)} %slice.114), channel_id=1, source_target_pairs={{0,16},{16,0},{32,48},{48,32},{64,80},{80,64},{96,112},{112,96},{1... | collective-permute-start | bytes 786440 | tf_op jit(solution)/shard_map/ppermute | solution.py:22
  153.9 5.2 %collective-permute-done.10 = bf16[256,512]{1,0:T(8,128)(2,1)S(1)} collective-permute-done((bf16[256,512]{1,0:T(8,128)(2,1)S(1)}, bf16[256,512]{1,0:T(8,128)(2,1)S(1)}, u32[]{:S(2)}, u32[]{:S(2)}) %collective-permute-start.10) | collective-permute-done | bytes 262176 | tf_op jit(solution)/shard_map/ppermute | solution.py:22
  159.2 5.4 %collective-permute-start.11 = (bf16[256,256]{1,0:T(8,128)(2,1)S(1)}, bf16[256,256]{1,0:T(8,128)(2,1)S(1)}, u32[]{:S(2)}, u32[]{:S(2)}) collective-permute-start(bf16[256,256]{1,0:T(8,128)(2,1)S(1)} %slice.115), channel_id=1, source_target_pairs={{0,32},{16,48},{32,0},{48,16},{64,96},{80,112},{96,64},{112,80},{1... | collective-permute-start | bytes 393224 | tf_op jit(solution)/shard_map/ppermute | solution.py:22
  164.6 4.5 %collective-permute-done.11 = bf16[256,256]{1,0:T(8,128)(2,1)S(1)} collective-permute-done((bf16[256,256]{1,0:T(8,128)(2,1)S(1)}, bf16[256,256]{1,0:T(8,128)(2,1)S(1)}, u32[]{:S(2)}, u32[]{:S(2)}) %collective-permute-start.11) | collective-permute-done | bytes 131104 | tf_op jit(solution)/shard_map/ppermute | solution.py:22
  169.1 7.2 %collective-permute-start.12 = (bf16[256,128]{1,0:T(8,128)(2,1)S(1)}, bf16[256,128]{1,0:T(8,128)(2,1)S(1)}, u32[]{:S(2)}, u32[]{:S(2)}) collective-permute-start(bf16[256,128]{1,0:T(8,128)(2,1)S(1)} %slice.117), channel_id=1, source_target_pairs={{0,64},{16,80},{32,96},{48,112},{64,0},{80,16},{96,32},{112,48},{1... | collective-permute-start | bytes 196616 | tf_op jit(solution)/shard_map/ppermute | solution.py:22
  176.3 4.3 %collective-permute-done.12 = bf16[256,128]{1,0:T(8,128)(2,1)S(1)} collective-permute-done((bf16[256,128]{1,0:T(8,128)(2,1)S(1)}, bf16[256,128]{1,0:T(8,128)(2,1)S(1)}, u32[]{:S(2)}, u32[]{:S(2)}) %collective-permute-start.12) | collective-permute-done | bytes 65568 | tf_op jit(solution)/shard_map/ppermute | solution.py:22
  185.0 12.5 %all_to_all.27 = bf16[4,512,128]{2,1,0:T(8,128)(2,1)S(1)} all-to-all(bf16[4,512,128]{2,1,0:T(8,128)(2,1)S(1)} %bitcast.67), channel_id=1, replica_groups=mesh['x'=4,'zl'=8,'zh'=2,'y'=4,'core'=2] {'y'}, dimensions={0} | all-to-all | bytes 1048576 | tf_op jit(solution)/shard_map/all_to_all | solution.py:26
  197.5 10.5 %collective-permute-start.14 = (bf16[256,128]{1,0:T(8,128)(2,1)S(1)}, bf16[256,128]{1,0:T(8,128)(2,1)S(1)}, u32[]{:S(2)}, u32[]{:S(2)}) collective-permute-start(bf16[256,128]{1,0:T(8,128)(2,1)S(1)} %slice.116), channel_id=1, source_target_pairs={{0,8},{8,0},{1,9},{9,1},{2,10},{10,2},{3,11},{11,3},{4,12},{12,4},... | collective-permute-start | bytes 196616 | tf_op jit(solution)/shard_map/ppermute | solution.py:22
  208.0 4.3 %collective-permute-done.14 = bf16[256,128]{1,0:T(8,128)(2,1)S(1)} collective-permute-done((bf16[256,128]{1,0:T(8,128)(2,1)S(1)}, bf16[256,128]{1,0:T(8,128)(2,1)S(1)}, u32[]{:S(2)}, u32[]{:S(2)}) %collective-permute-start.14) | collective-permute-done | bytes 65568 | tf_op jit(solution)/shard_map/ppermute | solution.py:22
  (71 shorter events, 37.2 us)
Async XLA Ops:
  2.4 55.1 %copy-start.8 = (bf16[768,128]{1,0:T(8,128)(2,1)S(1)}, bf16[768,128]{1,0:T(8,128)(2,1)}, u32[]{:S(2)}) copy-start(bf16[768,128]{1,0:T(8,128)(2,1)} %get-tuple-element.20) | copy-start | bytes 589828
  2.4 32.6 %collective-permute-start = (bf16[768,128]{1,0:T(8,128)(2,1)}, bf16[768,128]{1,0:T(8,128)(2,1)S(1)}, u32[]{:S(2)}, u32[]{:S(2)}) collective-permute-start(bf16[768,128]{1,0:T(8,128)(2,1)} %get-tuple-element.20), channel_id=1, source_target_pairs={{0,64},{16,80},{32,96},{48,112},{64,0},{80,16},{96,32},{112,48},{1... | collective-permute-start | bytes 589832 | tf_op jit(solution)/shard_map/ppermute | solution.py:22
  11.6 26.3 %collective-permute-start.2 = (bf16[256,128]{1,0:T(8,128)(2,1)}, bf16[256,128]{1,0:T(8,128)(2,1)S(1)}, u32[]{:S(2)}, u32[]{:S(2)}) collective-permute-start(bf16[256,128]{1,0:T(8,128)(2,1)} %param.9), channel_id=1, source_target_pairs={{0,8},{8,0},{1,9},{9,1},{2,10},{10,2},{3,11},{11,3},{4,12},{12,4},... | collective-permute-start | bytes 196616 | tf_op jit(solution)/shard_map/ppermute | solution.py:22
  35.9 21.5 %collective-permute-start.1 = (bf16[768,256]{1,0:T(8,128)(2,1)S(1)}, bf16[768,256]{1,0:T(8,128)(2,1)S(1)}, u32[]{:S(2)}, u32[]{:S(2)}) collective-permute-start(bf16[768,256]{1,0:T(8,128)(2,1)S(1)} %pad_maximum_fusion.1), channel_id=1, source_target_pairs={{0,32},{16,48},{32,0},{48,16},{64,96},{80,112},{96,64},{112,80},{1... | collective-permute-start | bytes 1179656 | tf_op jit(solution)/shard_map/ppermute | solution.py:22
  57.5 20.5 %collective-permute-start.3 = (bf16[768,512]{1,0:T(8,128)(2,1)S(1)}, bf16[768,512]{1,0:T(8,128)(2,1)S(1)}, u32[]{:S(2)}, u32[]{:S(2)}) collective-permute-start(bf16[768,512]{1,0:T(8,128)(2,1)S(1)} %pad_maximum_fusion), channel_id=1, source_target_pairs={{0,16},{16,0},{32,48},{48,32},{64,80},{80,64},{96,112},{112,96},{1... | collective-permute-start | bytes 2359304 | tf_op jit(solution)/shard_map/ppermute | solution.py:22
  70.7 7.4 %collective-permute-start.4 = (bf16[4,2,256,128]{3,2,1,0:T(8,128)(2,1)S(1)}, bf16[4,2,256,128]{3,2,1,0:T(8,128)(2,1)S(1)}, u32[]{:S(2)}, u32[]{:S(2)}) collective-permute-start(bf16[4,2,256,128]{3,2,1,0:T(8,128)(2,1)S(1)} %all_to_all.25.refs_0_), channel_id=1, source_target_pairs={{0,1},{1,0},{2,3},{3,2},{4,5},{5,4},{6,7},{7,6},{8,9},{9,8},{10,11... | collective-permute-start | bytes 1572872 | tf_op jit(solution)/shard_map/ppermute | solution.py:22
  78.1 13.0 %copy-start = (bf16[256,1024]{1,0:T(8,128)(2,1)}, bf16[256,1024]{1,0:T(8,128)(2,1)S(1)}, u32[]{:S(2)}) copy-start(bf16[256,1024]{1,0:T(8,128)(2,1)S(1)} %slice.70.refs_0_) | copy-start | bytes 1572868
  80.5 14.6 %all-to-all-start.1 = ((bf16[4,512,128]{2,1,0:T(8,128)(2,1)}), bf16[4,512,128]{2,1,0:T(8,128)(2,1)}, u32[]{:S(2)}, u32[]{:S(2)}) async-start(bf16[4,512,128]{2,1,0:T(8,128)(2,1)} %bitcast_bitcast_fusion), calls=%async_computation.1 | async-start | bytes 1048576 | tf_op jit(solution)/shard_map/all_to_all | solution.py:26
  85.2 26.8 %collective-permute-start.6 = (bf16[256,1024]{1,0:T(8,128)(2,1)S(1)}, bf16[256,1024]{1,0:T(8,128)(2,1)S(1)}, u32[]{:S(2)}, u32[]{:S(2)}) collective-permute-start(bf16[256,1024]{1,0:T(8,128)(2,1)S(1)} %slice.70.refs_0_), channel_id=1, source_target_pairs={{0,128},{128,0},{256,384},{384,256},{1,129},{129,1},{257,385},{385... | collective-permute-start | bytes 1572872 | tf_op jit(solution)/shard_map/ppermute | solution.py:22
  88.0 26.9 %collective-permute-start.7 = (bf16[256,1024]{1,0:T(8,128)(2,1)S(1)}, bf16[256,1024]{1,0:T(8,128)(2,1)S(1)}, u32[]{:S(2)}, u32[]{:S(2)}) collective-permute-start(bf16[256,1024]{1,0:T(8,128)(2,1)S(1)} %slice.70.refs_0_), channel_id=1, source_target_pairs={{0,384},{128,256},{256,128},{384,0},{1,385},{129,257},{257,129},{3... | collective-permute-start | bytes 1572872 | tf_op jit(solution)/shard_map/ppermute | solution.py:22
  91.1 23.8 %collective-permute-start.8 = (bf16[256,1024]{1,0:T(8,128)(2,1)S(1)}, bf16[256,1024]{1,0:T(8,128)(2,1)S(1)}, u32[]{:S(2)}, u32[]{:S(2)}) collective-permute-start(bf16[256,1024]{1,0:T(8,128)(2,1)S(1)} %slice.70.refs_0_), channel_id=1, source_target_pairs={{0,256},{128,384},{256,0},{384,128},{1,257},{129,385},{257,1},{385... | collective-permute-start | bytes 1572872 | tf_op jit(solution)/shard_map/ppermute | solution.py:22
  96.3 15.7 %collective-permute-start.5 = (bf16[256,256]{1,0:T(8,128)(2,1)S(1)}, bf16[256,256]{1,0:T(8,128)(2,1)S(1)}, u32[]{:S(2)}, u32[]{:S(2)}) collective-permute-start(bf16[256,256]{1,0:T(8,128)(2,1)S(1)} %pad_maximum_fusion.4), channel_id=1, source_target_pairs={{0,8},{8,0},{1,9},{9,1},{2,10},{10,2},{3,11},{11,3},{4,12},{12,4},... | collective-permute-start | bytes 393224 | tf_op jit(solution)/shard_map/ppermute | solution.py:22
  112.0 4.0 %copy-start.2 = (bf16[256,1024]{1,0:T(8,128)(2,1)}, bf16[256,1024]{1,0:T(8,128)(2,1)S(1)}, u32[]{:S(2)}) copy-start(bf16[256,1024]{1,0:T(8,128)(2,1)S(1)} %collective-permute-done.6.refs_1_) | copy-start | bytes 1572868
  114.9 1.1 copy-start.4
  115.0 1.3 copy-start.6
  116.3 15.5 %all-to-all-start.2 = ((bf16[4,512,256]{2,1,0:T(8,128)(2,1)}), bf16[4,512,256]{2,1,0:T(8,128)(2,1)}, u32[]{:S(2)}, u32[]{:S(2)}) async-start(bf16[4,512,256]{2,1,0:T(8,128)(2,1)} %broadcast_in_dim.4), calls=%async_computation.2 | async-start | bytes 2097152 | tf_op jit(solution)/shard_map/all_to_all | solution.py:26
  121.7 1.0 copy-start.1
  131.8 4.8 %collective-permute-start.9 = (bf16[2048,256]{1,0:T(8,128)(2,1)}, bf16[2048,256]{1,0:T(8,128)(2,1)S(1)}, u32[]{:S(2)}, u32[]{:S(2)}) collective-permute-start(bf16[2048,256]{1,0:T(8,128)(2,1)} %bitcast.14), channel_id=1, source_target_pairs={{0,1},{1,0},{2,3},{3,2},{4,5},{5,4},{6,7},{7,6},{8,9},{9,8},{10,11... | collective-permute-start | bytes 3145736 | tf_op jit(solution)/shard_map/ppermute | solution.py:22
  135.4 1.6 copy-start.9
  148.0 11.1 %collective-permute-start.10 = (bf16[256,512]{1,0:T(8,128)(2,1)S(1)}, bf16[256,512]{1,0:T(8,128)(2,1)S(1)}, u32[]{:S(2)}, u32[]{:S(2)}) collective-permute-start(bf16[256,512]{1,0:T(8,128)(2,1)S(1)} %slice.114), channel_id=1, source_target_pairs={{0,16},{16,0},{32,48},{48,32},{64,80},{80,64},{96,112},{112,96},{1... | collective-permute-start | bytes 786440 | tf_op jit(solution)/shard_map/ppermute | solution.py:22
  159.2 9.9 %collective-permute-start.11 = (bf16[256,256]{1,0:T(8,128)(2,1)S(1)}, bf16[256,256]{1,0:T(8,128)(2,1)S(1)}, u32[]{:S(2)}, u32[]{:S(2)}) collective-permute-start(bf16[256,256]{1,0:T(8,128)(2,1)S(1)} %slice.115), channel_id=1, source_target_pairs={{0,32},{16,48},{32,0},{48,16},{64,96},{80,112},{96,64},{112,80},{1... | collective-permute-start | bytes 393224 | tf_op jit(solution)/shard_map/ppermute | solution.py:22
  169.1 11.5 %collective-permute-start.12 = (bf16[256,128]{1,0:T(8,128)(2,1)S(1)}, bf16[256,128]{1,0:T(8,128)(2,1)S(1)}, u32[]{:S(2)}, u32[]{:S(2)}) collective-permute-start(bf16[256,128]{1,0:T(8,128)(2,1)S(1)} %slice.117), channel_id=1, source_target_pairs={{0,64},{16,80},{32,96},{48,112},{64,0},{80,16},{96,32},{112,48},{1... | collective-permute-start | bytes 196616 | tf_op jit(solution)/shard_map/ppermute | solution.py:22
  181.0 3.8 %collective-permute-start.13 = (bf16[2048,128]{1,0:T(8,128)(2,1)S(1)}, bf16[2048,128]{1,0:T(8,128)(2,1)S(1)}, u32[]{:S(2)}, u32[]{:S(2)}) collective-permute-start(bf16[2048,128]{1,0:T(8,128)(2,1)S(1)} %convolution_convert_fusion), channel_id=1, source_target_pairs={{0,1},{1,0},{2,3},{3,2},{4,5},{5,4},{6,7},{7,6},{8,9},{9,8},{10,11... | collective-permute-start | bytes 1572872 | tf_op jit(solution)/shard_map/ppermute | solution.py:22
  197.5 14.9 %collective-permute-start.14 = (bf16[256,128]{1,0:T(8,128)(2,1)S(1)}, bf16[256,128]{1,0:T(8,128)(2,1)S(1)}, u32[]{:S(2)}, u32[]{:S(2)}) collective-permute-start(bf16[256,128]{1,0:T(8,128)(2,1)S(1)} %slice.116), channel_id=1, source_target_pairs={{0,8},{8,0},{1,9},{9,1},{2,10},{10,2},{3,11},{11,3},{4,12},{12,4},... | collective-permute-start | bytes 196616 | tf_op jit(solution)/shard_map/ppermute | solution.py:22
  (3 other events, 3.1 us)

commit v10 on v8

--- a/solution.py
+++ b/solution.py
@@ -102,7 +102,7 @@
 
     left = [left] + [swap(left, "x", k) for k in (1, 3, 2)]
     rotated = jnp.concatenate([rotated, swap(rotated, "zh", 1)], axis=0)
-    rotated, *left = barrier((rotated, *left))
+    rotated, left[1], left[3] = barrier((rotated, left[1], left[3]))
     index, moves = [], []
     for number, ox in enumerate((0, 1, 3, 2)):
         for p in range(8):

time: 215 us -> 225 us (1.047)
  waiting for transfers between devices: 54.9 us -> 70 us
  starting transfers between devices: 90.3 us -> 83.7 us
    ppermute x15, waiting for transfers between devices: 49.9 us -> 66.4 us  [swap(): return lax.ppermute(value, axis, [(i, i ^ offset) for i in range(size)])]
    ppermute x15, starting transfers between devices: 81 us -> 74.5 us  [swap(): return lax.ppermute(value, axis, [(i, i ^ offset) for i in range(size)])]
  transfers between devices with their start and end apart: 17 -> 17, of which waited for: 12 -> 13; matrix products, arithmetic and copies ran while one was open for 2% -> 1% of each run, Pallas kernels for 0% -> 0%
where the time goes in v10:
time: 225 us; the launch traced here: 223 us
  starting transfers between devices  83.7 us (37%)
  waiting for transfers between devices  70 us (31%)
  blocking collectives  48.3 us (21%)
  local copies, waits for them, and re-layouts  8.54 us (4%)
  other arithmetic  4.4 us (2%)
  matrix products  4.25 us (2%)
    ppermute x15, starting transfers between devices, swap(): return lax.ppermute(value, axis, [(i, i ^ offset) for i in range(size)])  74.5 us
    ppermute x15, waiting for transfers between devices, swap(): return lax.ppermute(value, axis, [(i, i ^ offset) for i in range(size)])  66.4 us
    all_to_all x3, blocking collectives, exchange(): return lax.all_to_all(blocks, axis, 0, 0, tiled=True)  35 us
    all_gather x1, blocking collectives, shards(): basis = lax.all_gather(basis, 'y')  13.3 us
    all_to_all x2, starting transfers between devices, exchange(): return lax.all_to_all(blocks, axis, 0, 0, tiled=True)  9.24 us
    unnamed x21, local copies, waits for them, and re-layouts  5.11 us
  transfers between devices with their start and end apart: 17, of which 13 were waited for; matrix products, arithmetic and copies ran while one was open for 1% of the time, Pallas kernels for 0%

profile of v10, /device:TPU:6, one launch (start us, length us, event | category | flops | bytes accessed | tf_op | source)
XLA Modules:
  0.0 222.9 jit_solution(2985238639687271387)
XLA Ops:
  3.9 9.1 %collective-permute-start = (bf16[768,128]{1,0:T(8,128)(2,1)S(1)}, bf16[768,128]{1,0:T(8,128)(2,1)S(1)}, u32[]{:S(2)}, u32[]{:S(2)}) collective-permute-start(bf16[768,128]{1,0:T(8,128)(2,1)S(1)} %pad_maximum_fusion.3), channel_id=1, source_target_pairs={{0,64},{16,80},{32,96},{48,112},{64,0},{80,16},{96,32},{112,48},{1... | collective-permute-start | bytes 589832 | tf_op jit(solution)/shard_map/ppermute | solution.py:22
  13.0 10.9 %collective-permute-start.2 = (bf16[256,128]{1,0:T(8,128)(2,1)}, bf16[256,128]{1,0:T(8,128)(2,1)S(1)}, u32[]{:S(2)}, u32[]{:S(2)}) collective-permute-start(bf16[256,128]{1,0:T(8,128)(2,1)} %param.9), channel_id=1, source_target_pairs={{0,8},{8,0},{1,9},{9,1},{2,10},{10,2},{3,11},{11,3},{4,12},{12,4},... | collective-permute-start | bytes 196616 | tf_op jit(solution)/shard_map/ppermute | solution.py:22
  24.0 12.1 %collective-permute-done = bf16[768,128]{1,0:T(8,128)(2,1)S(1)} collective-permute-done((bf16[768,128]{1,0:T(8,128)(2,1)S(1)}, bf16[768,128]{1,0:T(8,128)(2,1)S(1)}, u32[]{:S(2)}, u32[]{:S(2)}) %collective-permute-start) | collective-permute-done | bytes 196640 | tf_op jit(solution)/shard_map/ppermute | solution.py:22
  38.1 13.3 %all-gather = bf16[8,256,128]{2,1,0:T(8,128)(2,1)S(1)} all-gather(bf16[2,256,128]{2,1,0:T(8,128)(2,1)S(1)} %pad_maximum_fusion.4), channel_id=2, replica_groups=mesh['x'=4,'zl'=8,'zh'=2,'y'=4,'core'=2] {'y'}, dimensions={0}, use_global_device_ids=true | all-gather | bytes 655360 | tf_op jit(solution)/shard_map/all_gather | solution.py:77
  51.4 6.2 %collective-permute-done.1 = bf16[768,256]{1,0:T(8,128)(2,1)S(1)} collective-permute-done((bf16[768,256]{1,0:T(8,128)(2,1)S(1)}, bf16[768,256]{1,0:T(8,128)(2,1)S(1)}, u32[]{:S(2)}, u32[]{:S(2)}) %collective-permute-start.1) | collective-permute-done | bytes 393248 | tf_op jit(solution)/shard_map/ppermute | solution.py:22
  59.6 11.3 %all_to_all.25.refs_0_ = bf16[4,2,256,128]{3,2,1,0:T(8,128)(2,1)S(1)} all-to-all(bf16[4,2,256,128]{3,2,1,0:T(8,128)(2,1)S(1)} %bitcast.66), channel_id=1, replica_groups=mesh['x'=4,'zl'=8,'zh'=2,'y'=4,'core'=2] {'x'}, dimensions={0} | all-to-all | bytes 1048576 | tf_op jit(solution)/shard_map/all_to_all | solution.py:26
  73.1 5.1 %collective-permute-done.3 = bf16[768,512]{1,0:T(8,128)(2,1)S(1)} collective-permute-done((bf16[768,512]{1,0:T(8,128)(2,1)S(1)}, bf16[768,512]{1,0:T(8,128)(2,1)S(1)}, u32[]{:S(2)}, u32[]{:S(2)}) %collective-permute-start.3) | collective-permute-done | bytes 786464 | tf_op jit(solution)/shard_map/ppermute | solution.py:22
  80.7 4.8 %all-to-all-start.1 = ((bf16[4,512,128]{2,1,0:T(8,128)(2,1)}), bf16[4,512,128]{2,1,0:T(8,128)(2,1)S(1)}, u32[]{:S(2)}, u32[]{:S(2)}) async-start(bf16[4,512,128]{2,1,0:T(8,128)(2,1)} %bitcast_bitcast_fusion), calls=%async_computation.1 | async-start | bytes 1048576 | tf_op jit(solution)/shard_map/all_to_all | solution.py:26
  90.7 3.6 %all-to-all-done.1 = bf16[4,512,128]{2,1,0:T(8,128)(2,1)S(1)} async-done(((bf16[4,512,128]{2,1,0:T(8,128)(2,1)}), bf16[4,512,128]{2,1,0:T(8,128)(2,1)S(1)}, u32[]{:S(2)}, u32[]{:S(2)}) %all-to-all-start.1) | async-done | bytes 524320 | tf_op jit(solution)/shard_map/all_to_all | solution.py:26
  94.5 10.5 %collective-permute-start.5 = (bf16[256,256]{1,0:T(8,128)(2,1)S(1)}, bf16[256,256]{1,0:T(8,128)(2,1)S(1)}, u32[]{:S(2)}, u32[]{:S(2)}) collective-permute-start(bf16[256,256]{1,0:T(8,128)(2,1)S(1)} %pad_maximum_fusion.5), channel_id=1, source_target_pairs={{0,8},{8,0},{1,9},{9,1},{2,10},{10,2},{3,11},{11,3},{4,12},{12,4},... | collective-permute-start | bytes 393224 | tf_op jit(solution)/shard_map/ppermute | solution.py:22
  105.0 7.0 %collective-permute-done.5 = bf16[256,256]{1,0:T(8,128)(2,1)S(1)} collective-permute-done((bf16[256,256]{1,0:T(8,128)(2,1)S(1)}, bf16[256,256]{1,0:T(8,128)(2,1)S(1)}, u32[]{:S(2)}, u32[]{:S(2)}) %collective-permute-start.5) | collective-permute-done | bytes 131104 | tf_op jit(solution)/shard_map/ppermute | solution.py:22
  114.9 4.5 %all-to-all-start.2 = ((bf16[4,512,256]{2,1,0:T(8,128)(2,1)}), bf16[4,512,256]{2,1,0:T(8,128)(2,1)}, u32[]{:S(2)}, u32[]{:S(2)}) async-start(bf16[4,512,256]{2,1,0:T(8,128)(2,1)} %broadcast_in_dim.4), calls=%async_computation.2 | async-start | bytes 2097152 | tf_op jit(solution)/shard_map/all_to_all | solution.py:26
  119.3 4.0 %collective-permute-start.8 = (bf16[256,1024]{1,0:T(8,128)(2,1)S(1)}, bf16[256,1024]{1,0:T(8,128)(2,1)S(1)}, u32[]{:S(2)}, u32[]{:S(2)}) collective-permute-start(bf16[256,1024]{1,0:T(8,128)(2,1)S(1)} %slice.78.refs_0_), channel_id=1, source_target_pairs={{0,384},{128,256},{256,128},{384,0},{1,385},{129,257},{257,129},{3... | collective-permute-start | bytes 1572872 | tf_op jit(solution)/shard_map/ppermute | solution.py:22
  124.5 8.6 %collective-permute-done.8.refs_2_ = bf16[256,1024]{1,0:T(8,128)(2,1)S(1)} collective-permute-done((bf16[256,1024]{1,0:T(8,128)(2,1)S(1)}, bf16[256,1024]{1,0:T(8,128)(2,1)S(1)}, u32[]{:S(2)}, u32[]{:S(2)}) %collective-permute-start.8) | collective-permute-done | bytes 524320 | tf_op jit(solution)/shard_map/ppermute | solution.py:22
  146.8 9.6 %all_to_all.26 = bf16[4,256,128]{1,2,0:T(8,128)(2,1)S(1)} all-to-all(bf16[4,256,128]{1,2,0:T(8,128)(2,1)S(1)} %broadcast_in_dim.5), channel_id=1, replica_groups=mesh['x'=4,'zl'=8,'zh'=2,'y'=4,'core'=2] {'x'}, dimensions={0} | all-to-all | bytes 524288 | tf_op jit(solution)/shard_map/all_to_all | solution.py:26
  157.0 3.7 %collective-permute-start.10 = (bf16[256,512]{1,0:T(8,128)(2,1)S(1)}, bf16[256,512]{1,0:T(8,128)(2,1)S(1)}, u32[]{:S(2)}, u32[]{:S(2)}) collective-permute-start(bf16[256,512]{1,0:T(8,128)(2,1)S(1)} %slice.122), channel_id=1, source_target_pairs={{0,16},{16,0},{32,48},{48,32},{64,80},{80,64},{96,112},{112,96},{1... | collective-permute-start | bytes 786440 | tf_op jit(solution)/shard_map/ppermute | solution.py:22
  160.7 5.8 %collective-permute-done.10 = bf16[256,512]{1,0:T(8,128)(2,1)S(1)} collective-permute-done((bf16[256,512]{1,0:T(8,128)(2,1)S(1)}, bf16[256,512]{1,0:T(8,128)(2,1)S(1)}, u32[]{:S(2)}, u32[]{:S(2)}) %collective-permute-start.10) | collective-permute-done | bytes 262176 | tf_op jit(solution)/shard_map/ppermute | solution.py:22
  166.6 6.2 %collective-permute-start.11 = (bf16[256,256]{1,0:T(8,128)(2,1)S(1)}, bf16[256,256]{1,0:T(8,128)(2,1)S(1)}, u32[]{:S(2)}, u32[]{:S(2)}) collective-permute-start(bf16[256,256]{1,0:T(8,128)(2,1)S(1)} %slice.123), channel_id=1, source_target_pairs={{0,32},{16,48},{32,0},{48,16},{64,96},{80,112},{96,64},{112,80},{1... | collective-permute-start | bytes 393224 | tf_op jit(solution)/shard_map/ppermute | solution.py:22
  172.8 4.8 %collective-permute-done.11 = bf16[256,256]{1,0:T(8,128)(2,1)S(1)} collective-permute-done((bf16[256,256]{1,0:T(8,128)(2,1)S(1)}, bf16[256,256]{1,0:T(8,128)(2,1)S(1)}, u32[]{:S(2)}, u32[]{:S(2)}) %collective-permute-start.11) | collective-permute-done | bytes 131104 | tf_op jit(solution)/shard_map/ppermute | solution.py:22
  177.7 4.6 %collective-permute-start.12 = (bf16[256,128]{1,0:T(8,128)(2,1)S(1)}, bf16[256,128]{1,0:T(8,128)(2,1)S(1)}, u32[]{:S(2)}, u32[]{:S(2)}) collective-permute-start(bf16[256,128]{1,0:T(8,128)(2,1)S(1)} %slice.125), channel_id=1, source_target_pairs={{0,64},{16,80},{32,96},{48,112},{64,0},{80,16},{96,32},{112,48},{1... | collective-permute-start | bytes 196616 | tf_op jit(solution)/shard_map/ppermute | solution.py:22
  182.3 6.7 %collective-permute-done.12 = bf16[256,128]{1,0:T(8,128)(2,1)S(1)} collective-permute-done((bf16[256,128]{1,0:T(8,128)(2,1)S(1)}, bf16[256,128]{1,0:T(8,128)(2,1)S(1)}, u32[]{:S(2)}, u32[]{:S(2)}) %collective-permute-start.12) | collective-permute-done | bytes 65568 | tf_op jit(solution)/shard_map/ppermute | solution.py:22
  193.3 14.0 %all_to_all.27 = bf16[4,512,128]{2,1,0:T(8,128)(2,1)S(1)} all-to-all(bf16[4,512,128]{2,1,0:T(8,128)(2,1)S(1)} %bitcast.67), channel_id=1, replica_groups=mesh['x'=4,'zl'=8,'zh'=2,'y'=4,'core'=2] {'y'}, dimensions={0} | all-to-all | bytes 1048576 | tf_op jit(solution)/shard_map/all_to_all | solution.py:26
  207.4 10.6 %collective-permute-start.14 = (bf16[256,128]{1,0:T(8,128)(2,1)S(1)}, bf16[256,128]{1,0:T(8,128)(2,1)S(1)}, u32[]{:S(2)}, u32[]{:S(2)}) collective-permute-start(bf16[256,128]{1,0:T(8,128)(2,1)S(1)} %slice.124), channel_id=1, source_target_pairs={{0,8},{8,0},{1,9},{9,1},{2,10},{10,2},{3,11},{11,3},{4,12},{12,4},... | collective-permute-start | bytes 196616 | tf_op jit(solution)/shard_map/ppermute | solution.py:22
  218.0 4.3 %collective-permute-done.14 = bf16[256,128]{1,0:T(8,128)(2,1)S(1)} collective-permute-done((bf16[256,128]{1,0:T(8,128)(2,1)S(1)}, bf16[256,128]{1,0:T(8,128)(2,1)S(1)}, u32[]{:S(2)}, u32[]{:S(2)}) %collective-permute-start.14) | collective-permute-done | bytes 65568 | tf_op jit(solution)/shard_map/ppermute | solution.py:22
  (73 shorter events, 39.7 us)
Async XLA Ops:
  0.6 37.4 %copy-start.9 = (bf16[256,128]{1,0:T(8,128)(2,1)S(1)}, bf16[256,128]{1,0:T(8,128)(2,1)}, u32[]{:S(2)}) copy-start(bf16[256,128]{1,0:T(8,128)(2,1)} %param.9) | copy-start | bytes 196612
  3.9 32.1 %collective-permute-start = (bf16[768,128]{1,0:T(8,128)(2,1)S(1)}, bf16[768,128]{1,0:T(8,128)(2,1)S(1)}, u32[]{:S(2)}, u32[]{:S(2)}) collective-permute-start(bf16[768,128]{1,0:T(8,128)(2,1)S(1)} %pad_maximum_fusion.3), channel_id=1, source_target_pairs={{0,64},{16,80},{32,96},{48,112},{64,0},{80,16},{96,32},{112,48},{1... | collective-permute-start | bytes 589832 | tf_op jit(solution)/shard_map/ppermute | solution.py:22
  13.0 25.0 %collective-permute-start.2 = (bf16[256,128]{1,0:T(8,128)(2,1)}, bf16[256,128]{1,0:T(8,128)(2,1)S(1)}, u32[]{:S(2)}, u32[]{:S(2)}) collective-permute-start(bf16[256,128]{1,0:T(8,128)(2,1)} %param.9), channel_id=1, source_target_pairs={{0,8},{8,0},{1,9},{9,1},{2,10},{10,2},{3,11},{11,3},{4,12},{12,4},... | collective-permute-start | bytes 196616 | tf_op jit(solution)/shard_map/ppermute | solution.py:22
  36.1 21.5 %collective-permute-start.1 = (bf16[768,256]{1,0:T(8,128)(2,1)S(1)}, bf16[768,256]{1,0:T(8,128)(2,1)S(1)}, u32[]{:S(2)}, u32[]{:S(2)}) collective-permute-start(bf16[768,256]{1,0:T(8,128)(2,1)S(1)} %pad_maximum_fusion.1), channel_id=1, source_target_pairs={{0,32},{16,48},{32,0},{48,16},{64,96},{80,112},{96,64},{112,80},{1... | collective-permute-start | bytes 1179656 | tf_op jit(solution)/shard_map/ppermute | solution.py:22
  57.7 20.5 %collective-permute-start.3 = (bf16[768,512]{1,0:T(8,128)(2,1)S(1)}, bf16[768,512]{1,0:T(8,128)(2,1)S(1)}, u32[]{:S(2)}, u32[]{:S(2)}) collective-permute-start(bf16[768,512]{1,0:T(8,128)(2,1)S(1)} %pad_maximum_fusion), channel_id=1, source_target_pairs={{0,16},{16,0},{32,48},{48,32},{64,80},{80,64},{96,112},{112,96},{1... | collective-permute-start | bytes 2359304 | tf_op jit(solution)/shard_map/ppermute | solution.py:22
  70.9 7.4 %collective-permute-start.4 = (bf16[4,2,256,128]{3,2,1,0:T(8,128)(2,1)S(1)}, bf16[4,2,256,128]{3,2,1,0:T(8,128)(2,1)S(1)}, u32[]{:S(2)}, u32[]{:S(2)}) collective-permute-start(bf16[4,2,256,128]{3,2,1,0:T(8,128)(2,1)S(1)} %all_to_all.25.refs_0_), channel_id=1, source_target_pairs={{0,1},{1,0},{2,3},{3,2},{4,5},{5,4},{6,7},{7,6},{8,9},{9,8},{10,11... | collective-permute-start | bytes 1572872 | tf_op jit(solution)/shard_map/ppermute | solution.py:22
  78.3 41.0 %copy-start = (bf16[256,1024]{1,0:T(8,128)(2,1)}, bf16[256,1024]{1,0:T(8,128)(2,1)S(1)}, u32[]{:S(2)}) copy-start(bf16[256,1024]{1,0:T(8,128)(2,1)S(1)} %slice.78.refs_0_) | copy-start | bytes 1572868
  80.7 13.7 %all-to-all-start.1 = ((bf16[4,512,128]{2,1,0:T(8,128)(2,1)}), bf16[4,512,128]{2,1,0:T(8,128)(2,1)S(1)}, u32[]{:S(2)}, u32[]{:S(2)}) async-start(bf16[4,512,128]{2,1,0:T(8,128)(2,1)} %bitcast_bitcast_fusion), calls=%async_computation.1 | async-start | bytes 1048576 | tf_op jit(solution)/shard_map/all_to_all | solution.py:26
  85.4 26.6 %collective-permute-start.6 = (bf16[256,1024]{1,0:T(8,128)(2,1)S(1)}, bf16[256,1024]{1,0:T(8,128)(2,1)S(1)}, u32[]{:S(2)}, u32[]{:S(2)}) collective-permute-start(bf16[256,1024]{1,0:T(8,128)(2,1)S(1)} %slice.78.refs_0_), channel_id=1, source_target_pairs={{0,128},{128,0},{256,384},{384,256},{1,129},{129,1},{257,385},{385... | collective-permute-start | bytes 1572872 | tf_op jit(solution)/shard_map/ppermute | solution.py:22
  88.2 25.5 %collective-permute-start.7 = (bf16[256,1024]{1,0:T(8,128)(2,1)S(1)}, bf16[256,1024]{1,0:T(8,128)(2,1)S(1)}, u32[]{:S(2)}, u32[]{:S(2)}) collective-permute-start(bf16[256,1024]{1,0:T(8,128)(2,1)S(1)} %slice.78.refs_0_), channel_id=1, source_target_pairs={{0,256},{128,384},{256,0},{384,128},{1,257},{129,385},{257,1},{385... | collective-permute-start | bytes 1572872 | tf_op jit(solution)/shard_map/ppermute | solution.py:22
  94.5 17.5 %collective-permute-start.5 = (bf16[256,256]{1,0:T(8,128)(2,1)S(1)}, bf16[256,256]{1,0:T(8,128)(2,1)S(1)}, u32[]{:S(2)}, u32[]{:S(2)}) collective-permute-start(bf16[256,256]{1,0:T(8,128)(2,1)S(1)} %pad_maximum_fusion.5), channel_id=1, source_target_pairs={{0,8},{8,0},{1,9},{9,1},{2,10},{10,2},{3,11},{11,3},{4,12},{12,4},... | collective-permute-start | bytes 393224 | tf_op jit(solution)/shard_map/ppermute | solution.py:22
  112.0 2.8 %copy-start.2 = (bf16[256,1024]{1,0:T(8,128)(2,1)}, bf16[256,1024]{1,0:T(8,128)(2,1)S(1)}, u32[]{:S(2)}) copy-start(bf16[256,1024]{1,0:T(8,128)(2,1)S(1)} %collective-permute-done.6.refs_1_) | copy-start | bytes 1572868
  113.7 1.2 copy-start.4
  114.9 24.1 %all-to-all-start.2 = ((bf16[4,512,256]{2,1,0:T(8,128)(2,1)}), bf16[4,512,256]{2,1,0:T(8,128)(2,1)}, u32[]{:S(2)}, u32[]{:S(2)}) async-start(bf16[4,512,256]{2,1,0:T(8,128)(2,1)} %broadcast_in_dim.4), calls=%async_computation.2 | async-start | bytes 2097152 | tf_op jit(solution)/shard_map/all_to_all | solution.py:26
  119.3 13.8 %collective-permute-start.8 = (bf16[256,1024]{1,0:T(8,128)(2,1)S(1)}, bf16[256,1024]{1,0:T(8,128)(2,1)S(1)}, u32[]{:S(2)}, u32[]{:S(2)}) collective-permute-start(bf16[256,1024]{1,0:T(8,128)(2,1)S(1)} %slice.78.refs_0_), channel_id=1, source_target_pairs={{0,384},{128,256},{256,128},{384,0},{1,385},{129,257},{257,129},{3... | collective-permute-start | bytes 1572872 | tf_op jit(solution)/shard_map/ppermute | solution.py:22
  133.9 1.0 copy-start.1
  134.9 1.0 copy-start.3
  139.0 4.8 %collective-permute-start.9 = (bf16[2048,256]{1,0:T(8,128)(2,1)}, bf16[2048,256]{1,0:T(8,128)(2,1)S(1)}, u32[]{:S(2)}, u32[]{:S(2)}) collective-permute-start(bf16[2048,256]{1,0:T(8,128)(2,1)} %bitcast.14), channel_id=1, source_target_pairs={{0,1},{1,0},{2,3},{3,2},{4,5},{5,4},{6,7},{7,6},{8,9},{9,8},{10,11... | collective-permute-start | bytes 3145736 | tf_op jit(solution)/shard_map/ppermute | solution.py:22
  144.2 1.8 copy-start.8
  157.0 9.5 %collective-permute-start.10 = (bf16[256,512]{1,0:T(8,128)(2,1)S(1)}, bf16[256,512]{1,0:T(8,128)(2,1)S(1)}, u32[]{:S(2)}, u32[]{:S(2)}) collective-permute-start(bf16[256,512]{1,0:T(8,128)(2,1)S(1)} %slice.122), channel_id=1, source_target_pairs={{0,16},{16,0},{32,48},{48,32},{64,80},{80,64},{96,112},{112,96},{1... | collective-permute-start | bytes 786440 | tf_op jit(solution)/shard_map/ppermute | solution.py:22
  166.6 11.0 %collective-permute-start.11 = (bf16[256,256]{1,0:T(8,128)(2,1)S(1)}, bf16[256,256]{1,0:T(8,128)(2,1)S(1)}, u32[]{:S(2)}, u32[]{:S(2)}) collective-permute-start(bf16[256,256]{1,0:T(8,128)(2,1)S(1)} %slice.123), channel_id=1, source_target_pairs={{0,32},{16,48},{32,0},{48,16},{64,96},{80,112},{96,64},{112,80},{1... | collective-permute-start | bytes 393224 | tf_op jit(solution)/shard_map/ppermute | solution.py:22
  177.7 11.3 %collective-permute-start.12 = (bf16[256,128]{1,0:T(8,128)(2,1)S(1)}, bf16[256,128]{1,0:T(8,128)(2,1)S(1)}, u32[]{:S(2)}, u32[]{:S(2)}) collective-permute-start(bf16[256,128]{1,0:T(8,128)(2,1)S(1)} %slice.125), channel_id=1, source_target_pairs={{0,64},{16,80},{32,96},{48,112},{64,0},{80,16},{96,32},{112,48},{1... | collective-permute-start | bytes 196616 | tf_op jit(solution)/shard_map/ppermute | solution.py:22
  189.4 3.8 %collective-permute-start.13 = (bf16[2048,128]{1,0:T(8,128)(2,1)S(1)}, bf16[2048,128]{1,0:T(8,128)(2,1)S(1)}, u32[]{:S(2)}, u32[]{:S(2)}) collective-permute-start(bf16[2048,128]{1,0:T(8,128)(2,1)S(1)} %convolution_convert_fusion), channel_id=1, source_target_pairs={{0,1},{1,0},{2,3},{3,2},{4,5},{5,4},{6,7},{7,6},{8,9},{9,8},{10,11... | collective-permute-start | bytes 1572872 | tf_op jit(solution)/shard_map/ppermute | solution.py:22
  207.4 14.9 %collective-permute-start.14 = (bf16[256,128]{1,0:T(8,128)(2,1)S(1)}, bf16[256,128]{1,0:T(8,128)(2,1)S(1)}, u32[]{:S(2)}, u32[]{:S(2)}) collective-permute-start(bf16[256,128]{1,0:T(8,128)(2,1)S(1)} %slice.124), channel_id=1, source_target_pairs={{0,8},{8,0},{1,9},{9,1},{2,10},{10,2},{3,11},{11,3},{4,12},{12,4},... | collective-permute-start | bytes 196616 | tf_op jit(solution)/shard_map/ppermute | solution.py:22
  (3 other events, 2.9 us)
